TPU v7x, 32 devices: a whole 2x2x4 slice. The times are simulated.
32 devices in a mesh: fy: 8 (over y, x, core), fx: 4 (over z).
Axes of the slice: x: 2, y: 2, z: 4, core: 2. Of those that a mesh axis runs over, the one named last changes fastest.
Arguments:
- start_image: float32 [16, 256, 512], P(None, 'fy', 'fx'), may hold values from 0.2 to 2
- dirty: float32 [16, 256, 512], P(None, 'fy', 'fx'), may hold values from -50 to 50
- sampling: float32 [16, 256, 512], P(None, 'fy', 'fx'), may hold values from 0.25 to 1
- basis_seed: float32 [16, 4], replicated, may hold values from -0.75 to 2.75
- margin: int32 [8, 4, 2, 2], P('fy', 'fx'), may hold values from 8 to 30, as said below
Outputs:
- image: float32 [16, 256, 512], P(None, 'fy', 'fx')
- data_dual: float32 [16, 256, 512], P(None, 'fy', 'fx')
Inputs may be any that keep to these rules, and one draw needn't show every extreme that they name: margin[a, b, l, 0] and margin[a, b, l, 1] are the widths kept above and to the left at dilation 2^l, at most 15 * 2^l; the value 30 occurs at the widest dilation in every draw.
All inputs are finite; a program needn't handle non-finite values.
Results may differ from a plain program's by a relative error of at most 0.0003.
Values sent between devices are 32-bit elements; how exact they have to be, the bound alone decides.
No kernel may reach another device: no remote copies, remote signals or barrier semaphores. Data moves between devices by JAX's collectives and lax.ppermute only.
A program may use at most 64 MiB of HBM per device.

v0:
```python
import math

import jax
import jax.numpy as jnp
from jax import lax
from jax.sharding import PartitionSpec as P

LEVELS = 2
REACH = 30


DAUBECHIES = [
    -0.00011747678400228192,
    0.0006754494059985568,
    -0.0003917403729959771,
    -0.00487035299301066,
    0.008746094047015655,
    0.013981027917015516,
    -0.04408825393106472,
    -0.01736930100202211,
    0.128747426620186,
    0.00047248457399797254,
    -0.2840155429624281,
    -0.015829105256023893,
    0.5853546836548691,
    0.6756307362980128,
    0.3128715909144659,
    0.05441584224308161,
]
DUAL_STEP = 0.5
PRIMAL_STEP = 0.5
CLIP_LEVEL = 0.08
BALL_SCALE = 0.8
NORM_EPS = 1e-06


def passed_along(value, axis, steps):
    count = lax.axis_size(axis)
    first, last = (max(0, -steps), min(count, count - steps))
    return lax.ppermute(value, axis, [(source, source + steps) for source in range(first, last)])


def band_matrix(filter_taps, extent, border, dilation):
    rows_idx = jnp.arange(extent + border)[:, None]
    cols_idx = jnp.arange(extent)[None, :]
    offset = cols_idx + border - rows_idx
    matrix = jnp.zeros((extent + border, extent), jnp.float32)
    for tap_idx in range(len(filter_taps)):
        matrix = matrix + filter_taps[tap_idx] * (offset == tap_idx * dilation).astype(jnp.float32)
    return matrix


def level_tables(row_count, col_count, border, dilation):
    low_taps = [tap_value / math.sqrt(2.0) for tap_value in DAUBECHIES]
    high_taps = [
        (-1.0) ** tap_idx * low_taps[len(low_taps) - 1 - tap_idx]
        for tap_idx in range(len(low_taps))
    ]
    return (
        band_matrix(low_taps, row_count, border, dilation),
        band_matrix(high_taps, row_count, border, dilation),
        band_matrix(low_taps, col_count, border, dilation),
        band_matrix(high_taps, col_count, border, dilation),
    )


def facet_mask(widths_pair, row_count, col_count, border):
    row_keep = (jnp.arange(row_count + border) >= border - widths_pair[0]).astype(jnp.float32)
    col_keep = (jnp.arange(col_count + border) >= border - widths_pair[1]).astype(jnp.float32)
    return row_keep[:, None] * col_keep[None, :]


def analyse(extended, tables):
    low_rows, high_rows, low_cols, high_cols = tables
    highest = lax.Precision.HIGHEST
    col_low = jnp.einsum("cjv,vw->cjw", extended, low_cols, precision=highest)
    col_high = jnp.einsum("cjv,vw->cjw", extended, high_cols, precision=highest)
    band_lh = jnp.einsum("ji,cjw->ciw", low_rows, col_high, precision=highest)
    band_hl = jnp.einsum("ji,cjw->ciw", high_rows, col_low, precision=highest)
    band_hh = jnp.einsum("ji,cjw->ciw", high_rows, col_high, precision=highest)
    return jnp.stack([band_lh, band_hl, band_hh])


def synthesise(bands, tables):
    low_rows, high_rows, low_cols, high_cols = tables
    highest = lax.Precision.HIGHEST
    rows_high = jnp.einsum("ji,ciw->cjw", low_rows, bands[0], precision=highest) + jnp.einsum(
        "ji,ciw->cjw", high_rows, bands[2], precision=highest
    )
    rows_low = jnp.einsum("ji,ciw->cjw", high_rows, bands[1], precision=highest)
    return jnp.einsum("cjw,vw->cjv", rows_high, high_cols, precision=highest) + jnp.einsum(
        "cjw,vw->cjv", rows_low, low_cols, precision=highest
    )


def orthonormal(basis_seed):
    columns = []
    for column_idx in range(basis_seed.shape[1]):
        vector = basis_seed[:, column_idx]
        for previous in columns:
            vector = vector - jnp.sum(previous * vector) * previous
        vector = vector / jnp.sqrt(jnp.sum(vector * vector))
        columns.append(vector)
    return jnp.stack(columns, axis=1)


def project(spectral, stepped):
    highest = lax.Precision.HIGHEST
    weights = jnp.einsum("cr,cij->rij", spectral, stepped, precision=highest)
    return jnp.einsum("cr,rij->cij", spectral, weights, precision=highest)


def extend_local(tile, border):
    from_above = passed_along(tile[:, -border:, :], "fy", 1)
    taller = jnp.concatenate([from_above, tile], axis=1)
    from_left = passed_along(taller[:, :, -border:], "fx", 1)
    return jnp.concatenate([from_left, taller], axis=2)


def retract_local(grown, border):
    arrived = passed_along(grown[:, :, :border], "fx", -1)
    interior = grown[:, :, border:]
    interior = jnp.concatenate(
        [interior[:, :, :-border], interior[:, :, -border:] + arrived], axis=2
    )
    arrived = passed_along(interior[:, :border, :], "fy", -1)
    interior = interior[:, border:, :]
    return jnp.concatenate([interior[:, :-border, :], interior[:, -border:, :] + arrived], axis=1)


def per_device(start_image, dirty, sampling, basis_seed, margin):
    channels, row_count, col_count = start_image.shape
    widths = margin[0, 0]
    spectral = orthonormal(basis_seed)
    radius = BALL_SCALE * math.sqrt(
        channels * row_count * col_count * lax.axis_size("fy") * lax.axis_size("fx")
    )
    weight = 1.0 / math.sqrt(LEVELS)
    band_duals = [
        jnp.zeros((3, channels, row_count, col_count), jnp.float32) for level_idx in range(LEVELS)
    ]
    shifted = DUAL_STEP * sampling * start_image - DUAL_STEP * dirty
    energy = lax.psum(jnp.sum(shifted * shifted), ("fy", "fx"))
    factor = jnp.maximum(0.0, 1.0 - DUAL_STEP * radius / jnp.sqrt(energy + NORM_EPS))
    data_dual = factor * shifted
    extended = extend_local(start_image, REACH)
    returned = jnp.zeros_like(extended)
    for level_idx in range(LEVELS):
        tables = level_tables(row_count, col_count, REACH, 2**level_idx)
        keep_mask = facet_mask(widths[level_idx], row_count, col_count, REACH)
        coefficients = analyse(extended * keep_mask, tables)
        band_duals[level_idx] = jnp.clip(DUAL_STEP * weight * coefficients, -CLIP_LEVEL, CLIP_LEVEL)
        returned = returned + synthesise(band_duals[level_idx], tables) * keep_mask
    prior_term = retract_local(returned, REACH)
    stepped = start_image - PRIMAL_STEP * (sampling * data_dual + weight * prior_term)
    updated = jnp.maximum(project(spectral, stepped), 0.0)
    return (updated, data_dual)


def solution(mesh):
    return jax.shard_map(
        per_device,
        mesh=mesh,
        in_specs=(
            P(None, "fy", "fx"),
            P(None, "fy", "fx"),
            P(None, "fy", "fx"),
            P(),
            P("fy", "fx", None, None),
        ),
        out_specs=(P(None, "fy", "fx"), P(None, "fy", "fx")),
        check_vma=False,
    )
```

profile of v0, /device:TPU:1, one launch (start us, length us, event | category | flops | bytes accessed | tf_op | source)
XLA Modules:
  0.0 119.4 jit_solution(15713892850354551526)
XLA Ops:
  0.6 1.0 slice.88
  1.7 4.5 %collective-permute-start = (f32[16,30,128]{2,1,0:T(8,128)S(1)}, f32[16,30,128]{2,1,0:T(8,128)S(1)}, u32[]{:S(2)}, u32[]{:S(2)}) collective-permute-start(f32[16,30,128]{2,1,0:T(8,128)S(1)} %slice.88), channel_id=1, source_target_pairs={{0,4},{4,8},{8,12},{12,16},{16,20},{20,24},{24,28},{1,5},{5,9},{9,... | collective-permute-start | bytes 737288 | tf_op jit(solution)/shard_map/ppermute | solution.py:40
  7.5 0.7 fusion.449
  8.2 1.3 %fusion.447 = (f32[]{:T(128)}, f32[]{:T(128)}, f32[]{:T(128)}) fusion(f32[16,1]{0,1:T(1,128)S(1)} %get-tuple-element.19, f32[16,4]{0,1:T(4,128)S(1)} %copy-done.3, f32[]{:T(128)} %get-tuple-element.18), kind=kLoop, calls=%fused_computation.482 | loop fusion | flops 125 | bytes 272 | tf_op jit(solution)/shard_map/reduce_sum | solution.py:101
  10.2 2.0 %multiply_reduce_fusion.5 = (f32[]{:T(128)}, f32[16]{0:T(128)S(1)}, f32[16]{0:T(128)S(1)}) fusion(f32[16,1]{0,1:T(1,128)S(1)} %get-tuple-element.19, f32[]{:T(128)} %get-tuple-element.6, f32[16,4]{0,1:T(4,128)S(1)} %copy-done.3, f32[]{:T(128)S(6)} %sqrt.16, f32[]{:T(128)} %get-tuple-element.18), kind=kLoop, calls=%fused_computation.502 | loop fusion | flops 111 | bytes 336 | tf_op jit(solution)/shard_map/reduce_sum | solution.py:101
  12.2 1.8 %multiply_reduce_fusion.3 = (f32[]{:T(128)}, f32[]{:T(128)}, f32[16]{0:T(128)S(1)}) fusion(f32[16]{0:T(128)S(1)} %get-tuple-element.17, f32[16]{0:T(128)S(1)} %get-tuple-element.16, f32[]{:T(128)} %get-tuple-element.15, f32[16,1]{0,1:T(1,128)S(1)} %get-tuple-element.19, f32[]{:T(128)} %get-tuple-element.4, f32[16,4]{0,1:T(4,128)S(1)} %copy-done.3), kind=kLoop, calls=%fused_computation.498 | loop fusion | flops 126 | bytes 336 | tf_op jit(solution)/shard_map/reduce_sum | solution.py:101
  18.1 1.8 %multiply_reduce_fusion.2 = (f32[]{:T(128)}, f32[16]{0:T(128)S(1)}) fusion(f32[16]{0:T(128)S(1)} %get-tuple-element.14, f32[16]{0:T(128)S(1)} %get-tuple-element.17, f32[]{:T(128)} %get-tuple-element.7, f32[]{:T(128)S(6)} %sqrt.17, f32[16]{0:T(128)S(1)} %get-tuple-element.16, f32[]{:T(128)} %get-tuple-element.15), kind=kLoop, calls=%fused_computation.496 | loop fusion | flops 111 | bytes 272 | tf_op jit(solution)/shard_map/reduce_sum | solution.py:101
  20.3 3.2 %collective-permute-start.1 = (f32[16,62,30]{2,1,0:T(8,128)S(1)}, f32[16,62,30]{2,1,0:T(8,128)S(1)}, u32[]{:S(2)}, u32[]{:S(2)}) collective-permute-start(f32[16,62,30]{2,1,0:T(8,128)S(1)} %pad_maximum_fusion), channel_id=1, source_target_pairs={{0,1},{1,2},{2,3},{4,5},{5,6},{6,7},{8,9},{9,10},{10,11},{12,13},{... | collective-permute-start | bytes 357128 | tf_op jit(solution)/shard_map/ppermute | solution.py:40
  23.6 10.9 %collective-permute-done.1 = f32[16,62,30]{2,1,0:T(8,128)S(1)} collective-permute-done((f32[16,62,30]{2,1,0:T(8,128)S(1)}, f32[16,62,30]{2,1,0:T(8,128)S(1)}, u32[]{:S(2)}, u32[]{:S(2)}) %collective-permute-start.1) | collective-permute-done | bytes 119072 | tf_op jit(solution)/shard_map/ppermute | solution.py:40
  34.4 1.2 fusion.7
  36.6 1.2 fusion.11
  38.8 1.2 fusion.9
  40.6 0.7 convolution_bitcast_fusion.1
  41.3 0.7 fusion.27
  42.0 1.2 fusion.5
  43.8 0.7 convolution_bitcast_fusion
  44.5 0.7 fusion.26
  45.3 0.7 fusion.4
  46.0 1.1 fusion.87
  47.1 0.9 fusion.3
  48.0 1.1 fusion.126
  49.1 1.1 fusion.2
  50.2 1.1 fusion.1
  51.4 1.4 %collective-permute-start.2 = (f32[16,62,30]{2,1,0:T(8,128)S(1)}, f32[16,62,30]{2,1,0:T(8,128)S(1)}, u32[]{:S(2)}, u32[]{:S(2)}) collective-permute-start(f32[16,62,30]{2,1,0:T(8,128)S(1)} %slice.114), channel_id=1, source_target_pairs={{1,0},{2,1},{3,2},{5,4},{6,5},{7,6},{9,8},{10,9},{11,10},{13,12},{... | collective-permute-start | bytes 357128 | tf_op jit(solution)/shard_map/ppermute | solution.py:40
  52.8 0.7 multiply_reduce_fusion
  53.7 14.0 %collective-permute-done.2 = f32[16,62,30]{2,1,0:T(8,128)S(1)} collective-permute-done((f32[16,62,30]{2,1,0:T(8,128)S(1)}, f32[16,62,30]{2,1,0:T(8,128)S(1)}, u32[]{:S(2)}, u32[]{:S(2)}) %collective-permute-start.2) | collective-permute-done | bytes 119072 | tf_op jit(solution)/shard_map/ppermute | solution.py:40
  67.9 2.4 %collective-permute-start.3 = (f32[16,30,128]{2,1,0:T(8,128)S(1)}, f32[16,30,128]{2,1,0:T(8,128)S(1)}, u32[]{:S(2)}, u32[]{:S(2)}) collective-permute-start(f32[16,30,128]{2,1,0:T(8,128)S(1)} %pad_maximum_fusion.1), channel_id=1, source_target_pairs={{4,0},{8,4},{12,8},{16,12},{20,16},{24,20},{28,24},{5,1},{9,5},{13... | collective-permute-start | bytes 737288 | tf_op jit(solution)/shard_map/ppermute | solution.py:40
  70.3 1.9 %multiply_reduce_fusion.1 = f32[]{:T(128)} fusion(f32[16]{0:T(128)S(1)} %get-tuple-element.13, f32[]{:T(128)} %get-tuple-element.12, f32[16]{0:T(128)S(1)} %get-tuple-element.14, f32[16]{0:T(128)S(1)} %get-tuple-element.17, f32[]{:T(128)} %get-tuple-element.7), kind=kLoop, calls=%fused_computation.494 | loop fusion | flops 95 | bytes 204 | tf_op jit(solution)/shard_map/reduce_sum | solution.py:102
  72.2 39.4 %psum.7 = f32[]{:T(128)} all-reduce(f32[]{:T(128)} %multiply_reduce_fusion), channel_id=1, replica_groups=mesh['fy'=8,'fx'=4] {'fy','fx'}, use_global_device_ids=true, to_apply=%region_11.0 | all-reduce | flops 1 | bytes 8 | tf_op jit(solution)/shard_map/psum | solution.py:143
  113.0 3.8 %subtract_divide_fusion = (f32[16,1]{0,1:T(1,128)S(1)}, f32[16,1]{0,1:T(1,128)S(1)}, f32[16,1]{0,1:T(1,128)S(1)}) fusion(f32[16,1]{0,1:T(1,128)S(1)} %get-tuple-element.19, f32[]{:T(128)S(6)} %sqrt.18, f32[]{:T(128)} %get-tuple-element.12, f32[]{:T(128)} %get-tuple-element.7, f32[]{:T(128)} %get-tuple-element.4, f32[16,4]{0,1:T(4,128)S(1)} %copy-done.3, ...), kind=kLoop, calls=%fused_computation.495 | loop fusion | flops 240 | bytes 484 | tf_op jit(solution)/shard_map/div | solution.py:102
  116.9 0.8 fusion.25
  118.6 0.8 copy.7
  (38 shorter events, 6.4 us)
Async XLA Ops:
  0.6 19.4 %copy-start = (f32[16,32,128]{2,1,0:T(8,128)S(1)}, f32[16,32,128]{2,1,0:T(8,128)}, u32[]{:S(2)}) copy-start(f32[16,32,128]{2,1,0:T(8,128)} %param.5) | copy-start | bytes 786436
  0.6 5.6 %copy-start.3 = (f32[16,4]{0,1:T(4,128)S(1)}, f32[16,4]{0,1:T(4,128)}, u32[]{:S(2)}) copy-start(f32[16,4]{0,1:T(4,128)} %param.8) | copy-start | bytes 772
  1.7 18.4 %collective-permute-start = (f32[16,30,128]{2,1,0:T(8,128)S(1)}, f32[16,30,128]{2,1,0:T(8,128)S(1)}, u32[]{:S(2)}, u32[]{:S(2)}) collective-permute-start(f32[16,30,128]{2,1,0:T(8,128)S(1)} %slice.88), channel_id=1, source_target_pairs={{0,4},{4,8},{8,12},{12,16},{16,20},{20,24},{24,28},{1,5},{5,9},{9,... | collective-permute-start | bytes 737288 | tf_op jit(solution)/shard_map/ppermute | solution.py:40
  14.0 0.7 copy-start.4
  20.3 14.1 %collective-permute-start.1 = (f32[16,62,30]{2,1,0:T(8,128)S(1)}, f32[16,62,30]{2,1,0:T(8,128)S(1)}, u32[]{:S(2)}, u32[]{:S(2)}) collective-permute-start(f32[16,62,30]{2,1,0:T(8,128)S(1)} %pad_maximum_fusion), channel_id=1, source_target_pairs={{0,1},{1,2},{2,3},{4,5},{5,6},{6,7},{8,9},{9,10},{10,11},{12,13},{... | collective-permute-start | bytes 357128 | tf_op jit(solution)/shard_map/ppermute | solution.py:40
  51.3 1.5 %copy-start.1 = (f32[16,32,128]{2,1,0:T(8,128)S(1)}, f32[16,32,128]{2,1,0:T(8,128)}, u32[]{:S(2)}) copy-start(f32[16,32,128]{2,1,0:T(8,128)} %param.7) | copy-start | bytes 786436
  51.3 1.5 %copy-start.2 = (f32[16,32,128]{2,1,0:T(8,128)S(1)}, f32[16,32,128]{2,1,0:T(8,128)}, u32[]{:S(2)}) copy-start(f32[16,32,128]{2,1,0:T(8,128)} %param.6) | copy-start | bytes 786436
  51.4 16.3 %collective-permute-start.2 = (f32[16,62,30]{2,1,0:T(8,128)S(1)}, f32[16,62,30]{2,1,0:T(8,128)S(1)}, u32[]{:S(2)}, u32[]{:S(2)}) collective-permute-start(f32[16,62,30]{2,1,0:T(8,128)S(1)} %slice.114), channel_id=1, source_target_pairs={{1,0},{2,1},{3,2},{5,4},{6,5},{7,6},{9,8},{10,9},{11,10},{13,12},{... | collective-permute-start | bytes 357128 | tf_op jit(solution)/shard_map/ppermute | solution.py:40
  67.9 48.8 %collective-permute-start.3 = (f32[16,30,128]{2,1,0:T(8,128)S(1)}, f32[16,30,128]{2,1,0:T(8,128)S(1)}, u32[]{:S(2)}, u32[]{:S(2)}) collective-permute-start(f32[16,30,128]{2,1,0:T(8,128)S(1)} %pad_maximum_fusion.1), channel_id=1, source_target_pairs={{4,0},{8,4},{12,8},{16,12},{20,16},{24,20},{28,24},{5,1},{9,5},{13... | collective-permute-start | bytes 737288 | tf_op jit(solution)/shard_map/ppermute | solution.py:40
where the time goes:
time: 121 us; the launch traced here: 119 us
  blocking collectives  39.4 us (33%)
  waiting for transfers between devices  24.9 us (21%)
  matrix products  17.3 us (14%)
  other arithmetic  16.4 us (14%)
  starting transfers between devices  11.6 us (10%)
  between operations  7.06 us (6%)
  local copies, waits for them, and re-layouts  2.74 us (2%)
    psum x1, blocking collectives, per_device(): energy = lax.psum(jnp.sum(shifted * shifted), ('fy', 'fx'))  39.4 us
    ppermute x4, waiting for transfers between devices, passed_along(): lax.ppermute(value, axis, [(source, source + steps) for source in range(f...  24.9 us
    ppermute x4, starting transfers between devices, passed_along(): lax.ppermute(value, axis, [(source, source + steps) for source in range(f...  11.6 us
    reduce_sum x5, other arithmetic, orthonormal(): vector = vector - jnp.sum(previous * vector) * previous  7.67 us
    div x1, other arithmetic, orthonormal(): vector = vector / jnp.sqrt(jnp.sum(vector * vector))  3.78 us
    reduce_sum x2, other arithmetic, orthonormal(): vector = vector / jnp.sqrt(jnp.sum(vector * vector))  2.47 us
  transfers between devices with their start and end apart: 4, of which 2 were waited for; matrix products, arithmetic and copies ran while one was open for 13% of the time, Pallas kernels for 0%

commit v1 on v0

v1 whole, which is shorter than its diff:
```python
import math

import jax
import jax.numpy as jnp
import numpy as np
from jax import lax
from jax.experimental import pallas as pl
from jax.experimental.pallas import tpu as pltpu
from jax.sharding import PartitionSpec as P

LEVELS = 2
BORDER = 32
LANES = 128


DAUBECHIES = [
    -0.00011747678400228192,
    0.0006754494059985568,
    -0.0003917403729959771,
    -0.00487035299301066,
    0.008746094047015655,
    0.013981027917015516,
    -0.04408825393106472,
    -0.01736930100202211,
    0.128747426620186,
    0.00047248457399797254,
    -0.2840155429624281,
    -0.015829105256023893,
    0.5853546836548691,
    0.6756307362980128,
    0.3128715909144659,
    0.05441584224308161,
]
DUAL_STEP = 0.5
PRIMAL_STEP = 0.5
CLIP_LEVEL = 0.08
BALL_SCALE = 0.8
NORM_EPS = 1e-06
WEIGHT = 1.0 / math.sqrt(LEVELS)
BAND_STEP = DUAL_STEP * WEIGHT

LOW = [tap / math.sqrt(2.0) for tap in DAUBECHIES]
HIGH = [(-1.0) ** k * LOW[len(LOW) - 1 - k] for k in range(len(LOW))]


def band(taps, extent, dilation):
    matrix = np.zeros((BORDER + extent, extent), np.float32)
    for k, tap in enumerate(taps):
        for i in range(extent):
            matrix[i - k * dilation + BORDER, i] += np.float32(tap)
    return matrix


def row_table(rows):
    return np.concatenate(
        [band(taps, rows, 2**level).T for level in range(LEVELS) for taps in (LOW, HIGH)], axis=0
    )


def col_table(cols):
    table = np.zeros((LEVELS, cols + LANES, 2 * cols), np.float32)
    for level in range(LEVELS):
        for half, taps in enumerate((LOW, HIGH)):
            matrix = band(taps, cols, 2**level)
            table[level, :cols, half * cols : (half + 1) * cols] = matrix[BORDER:]
            table[level, cols : cols + BORDER, half * cols : (half + 1) * cols] = matrix[:BORDER]
    return table


def terms(value):
    high = value.astype(jnp.bfloat16)
    low = (value - high.astype(jnp.float32)).astype(jnp.bfloat16)
    return high, low


def dot(a, b):
    return lax.dot_general(a, b, (((1,), (0,)), ((), ())), preferred_element_type=jnp.float32)


def lane_iota(shape):
    return lax.broadcasted_iota(jnp.int32, shape, len(shape) - 1)


def row_iota(shape):
    return lax.broadcasted_iota(jnp.int32, shape, len(shape) - 2)


def pack_rows(strip, offset):
    groups = strip.shape[0] // 8
    lane = lane_iota((8, LANES))
    packed = None
    for q in range(groups):
        piece = strip[8 * q : 8 * q + 8]
        shift = (BORDER * q - offset) % LANES
        if shift:
            piece = pltpu.roll(piece, shift, 1)
        packed = piece if packed is None else jnp.where(lane >= BORDER * q, piece, packed)
    return packed


def unpack_rows(packed, offset, groups):
    pieces = []
    for q in range(groups):
        shift = (offset - BORDER * q) % LANES
        pieces.append(pltpu.roll(packed, shift, 1) if shift else packed)
    return jnp.concatenate(pieces, axis=0)


def first_kernel(start_ref, dirty_ref, sampling_ref, energy_ref, pack_ref):
    channels, rows, cols = start_ref.shape
    total = jnp.zeros((8, cols), jnp.float32)
    for c in range(channels):
        field = start_ref[c]
        shifted = DUAL_STEP * sampling_ref[c] * field - DUAL_STEP * dirty_ref[c]
        square = shifted * shifted
        for q in range(rows // 8):
            total = total + square[8 * q : 8 * q + 8]
        pack_ref[c] = pack_rows(field, cols - BORDER)
    energy_ref[...] = total


def basis_kernel(seed_ref, basis_ref):
    channels, rank = seed_ref.shape
    seed = seed_ref[...]
    columns = [jnp.broadcast_to(seed[:, r : r + 1], (channels, LANES)) for r in range(rank)]
    for r in range(rank):
        vector = columns[r]
        vector = vector / jnp.sqrt(jnp.sum(vector * vector, axis=0, keepdims=True))
        basis_ref[r] = vector
        for later in range(r + 1, rank):
            along = jnp.sum(vector * columns[later], axis=0, keepdims=True)
            columns[later] = columns[later] - along * vector


def bank_kernel(
    margin_ref, own_ref, above_ref, left_ref, corner_ref, rows_ref, rows_t_ref, cols_ref, cols_t_ref,
    own_out, above_out, left_out, corner_out, z_high, z_low, u_high, u_low,
):
    channels, rows, cols = own_ref.shape
    groups = rows // 8
    tall = rows + BORDER
    wide = cols + LANES
    half = 2 * rows

    position = lane_iota((half, tall)) - BORDER
    position_t = row_iota((tall, half)) - BORDER
    a_parts, at_parts = [], []
    for level in range(LEVELS):
        width = margin_ref[2 * level]
        a_parts.append(jnp.where(position >= -width, rows_ref[level * half : (level + 1) * half], 0.0))
        at_parts.append(jnp.where(position_t >= -width, rows_t_ref[level], 0.0))
    a_high, a_low = terms(jnp.concatenate(a_parts, axis=0))
    a_cat = jnp.concatenate([a_high, a_high, a_low], axis=1)
    at_pairs = [terms(part) for part in at_parts]
    at_cat = jnp.concatenate(
        [pair[0] for pair in at_pairs] * 2 + [pair[1] for pair in at_pairs], axis=1
    )

    for c in range(channels):
        upper = jnp.concatenate([above_ref[c], unpack_rows(corner_ref[c], 0, groups)], axis=1)
        lower = jnp.concatenate([own_ref[c], unpack_rows(left_ref[c], 0, groups)], axis=1)
        e_high, e_low = terms(jnp.concatenate([upper, lower], axis=0))
        z = dot(a_cat, jnp.concatenate([e_high, e_low, e_high], axis=0))
        part_high, part_low = terms(z)
        for level in range(LEVELS):
            z_high[level, c] = part_high[level * half : (level + 1) * half]
            z_low[level, c] = part_low[level * half : (level + 1) * half]

    low_rows = row_iota((half, 2 * cols)) < rows
    low_cols = lane_iota((half, 2 * cols)) < cols
    bound = jnp.where(low_rows & low_cols, 0.0, CLIP_LEVEL / BAND_STEP)
    bound = jnp.broadcast_to(bound[None], (channels, half, 2 * cols)).reshape(channels * half, 2 * cols)
    for level in range(LEVELS):
        width = margin_ref[2 * level + 1]
        at = row_iota((wide, 2 * cols))
        g = jnp.where((at < cols) | (at >= cols + BORDER - width), cols_ref[level], 0.0)
        at = lane_iota((2 * cols, wide))
        g_t = jnp.where((at < cols) | (at >= cols + BORDER - width), cols_t_ref[level], 0.0)
        g_high, g_low = terms(g)
        zh = z_high[level].reshape(channels * half, wide)
        zl = z_low[level].reshape(channels * half, wide)
        coef = dot(jnp.concatenate([zh, zl, zh], axis=1), jnp.concatenate([g_high, g_high, g_low], axis=0))
        coef = jnp.minimum(jnp.maximum(coef, -bound), bound)
        t_high, t_low = terms(coef)
        gt_high, gt_low = terms(g_t)
        u = dot(
            jnp.concatenate([t_high, t_low, t_high], axis=1),
            jnp.concatenate([gt_high, gt_high, gt_low], axis=0),
        )
        part_high, part_low = terms(u)
        u_high[level] = part_high.reshape(channels, half, wide)
        u_low[level] = part_low.reshape(channels, half, wide)

    for c in range(channels):
        highs = [u_high[level, c] for level in range(LEVELS)]
        lows = [u_low[level, c] for level in range(LEVELS)]
        back = dot(at_cat, jnp.concatenate(highs + lows + highs, axis=0))
        above_out[c] = back[:BORDER, :cols]
        own_out[c] = back[BORDER:, :cols]
        corner_out[c] = pack_rows(back[:BORDER, cols:], 0)
        left_out[c] = pack_rows(back[BORDER:, cols:], 0)


def last_kernel(
    radius, start_ref, dirty_ref, sampling_ref, basis_ref, energy_ref, own_ref, below_ref, right_ref, corner_ref,
    image_ref, dual_ref,
):
    channels, rows, cols = start_ref.shape
    rank = basis_ref.shape[0]
    groups = rows // 8
    energy = jnp.sum(jnp.sum(energy_ref[...], axis=0, keepdims=True), axis=1, keepdims=True)
    factor = jnp.maximum(0.0, 1.0 - DUAL_STEP * radius / jnp.sqrt(energy + NORM_EPS))
    factor = jnp.broadcast_to(factor, (rows, cols))
    edge = lane_iota((rows, cols)) >= cols - BORDER
    weights = [jnp.zeros((rows, cols), jnp.float32) for r in range(rank)]
    for c in range(channels):
        field = start_ref[c]
        gain = sampling_ref[c]
        dual = factor * (DUAL_STEP * gain * field - DUAL_STEP * dirty_ref[c])
        dual_ref[c] = dual
        strip = unpack_rows(right_ref[c] + corner_ref[c], cols - BORDER, groups)
        prior = own_ref[c] + below_ref[c] + jnp.where(edge, strip, 0.0)
        stepped = field - PRIMAL_STEP * (gain * dual + (WEIGHT * BAND_STEP) * prior)
        for r in range(rank):
            weights[r] = weights[r] + basis_ref[r, c : c + 1, :] * stepped
    for c in range(channels):
        total = basis_ref[0, c : c + 1, :] * weights[0]
        for r in range(1, rank):
            total = total + basis_ref[r, c : c + 1, :] * weights[r]
        image_ref[c] = jnp.maximum(total, 0.0)


def shift(axis_sizes, steps):
    pairs = []
    for a in range(axis_sizes[0]):
        for b in range(axis_sizes[1]):
            to_a, to_b = a + steps[0], b + steps[1]
            if 0 <= to_a < axis_sizes[0] and 0 <= to_b < axis_sizes[1]:
                pairs.append((a * axis_sizes[1] + b, to_a * axis_sizes[1] + to_b))
    return pairs


def whole_sum(value):
    for axis in ("fy", "fx"):
        count = lax.axis_size(axis)
        if count & (count - 1):
            value = lax.psum(value, axis)
        else:
            step = 1
            while step < count:
                value = value + lax.ppermute(value, axis, [(i, i ^ step) for i in range(count)])
                step *= 2
    return value


def per_device(start_image, dirty, sampling, basis_seed, margin):
    channels, rows, cols = start_image.shape
    sizes = (lax.axis_size("fy"), lax.axis_size("fx"))
    half = 2 * rows
    wide = cols + LANES
    radius = BALL_SCALE * math.sqrt(channels * rows * cols * sizes[0] * sizes[1])
    f32 = jnp.float32
    image_shape = jax.ShapeDtypeStruct((channels, rows, cols), f32)
    pack_shape = jax.ShapeDtypeStruct((channels, 8, LANES), f32)
    params = pltpu.CompilerParams(vmem_limit_bytes=48 * 1024 * 1024)

    def moved(value, steps):
        return lax.ppermute(value, ("fy", "fx"), shift(sizes, steps))

    above = moved(start_image, (1, 0))
    energy, pack = pl.pallas_call(
        first_kernel,
        out_shape=(jax.ShapeDtypeStruct((8, cols), f32), pack_shape),
        compiler_params=params,
        name="first",
    )(start_image, dirty, sampling)
    left = moved(pack, (0, 1))
    corner = moved(pack, (1, 1))
    basis = pl.pallas_call(
        basis_kernel,
        out_shape=jax.ShapeDtypeStruct((basis_seed.shape[1], channels, LANES), f32),
        compiler_params=params,
        name="basis",
    )(basis_seed)
    energy = whole_sum(energy)

    table = row_table(rows)
    table_t = np.ascontiguousarray(table.reshape(LEVELS, half, rows + BORDER).transpose(0, 2, 1))
    col = col_table(cols)
    col_t = np.ascontiguousarray(col.transpose(0, 2, 1))
    vmem = pl.BlockSpec(memory_space=pltpu.VMEM)
    own_part, above_part, left_part, corner_part = pl.pallas_call(
        bank_kernel,
        out_shape=(image_shape, image_shape, pack_shape, pack_shape),
        in_specs=[pl.BlockSpec(memory_space=pltpu.SMEM)] + [vmem] * 8,
        scratch_shapes=[
            pltpu.VMEM((LEVELS, channels, half, wide), jnp.bfloat16) for i in range(4)
        ],
        compiler_params=params,
        name="bank",
    )(margin.reshape(-1), start_image, above, left, corner, table, table_t, col, col_t)
    below = moved(above_part, (-1, 0))
    right = moved(left_part, (0, -1))
    corner_back = moved(corner_part, (-1, -1))

    def last(*refs):
        last_kernel(radius, *refs)

    return pl.pallas_call(
        last,
        out_shape=(image_shape, image_shape),
        compiler_params=params,
        name="last",
    )(start_image, dirty, sampling, basis, energy, own_part, below, right, corner_back)


def solution(mesh):
    return jax.shard_map(
        per_device,
        mesh=mesh,
        in_specs=(
            P(None, "fy", "fx"),
            P(None, "fy", "fx"),
            P(None, "fy", "fx"),
            P(),
            P("fy", "fx", None, None),
        ),
        out_specs=(P(None, "fy", "fx"), P(None, "fy", "fx")),
        check_vma=False,
    )
```

time: 121 us -> 49.1 us (0.41)
  the two profiles are of different devices: /device:TPU:1 before, /device:TPU:0 now
where the time goes in v1:
time: 49.1 us; the launch traced here: 48.6 us
  starting transfers between devices  27.2 us (55%)
  waiting for transfers between devices  9.72 us (20%)
  local copies, waits for them, and re-layouts  5.75 us (12%)
  Pallas kernels  5.18 us (11%)
  between operations  0.77 us (2%)
    ppermute x6, starting transfers between devices, moved(): return lax.ppermute(value, ('fy', 'fx'), shift(sizes, steps))  15.6 us
    ppermute x5, starting transfers between devices, whole_sum(): lax.ppermute(value, axis, [(i, i ^ step) for i in range(count)])  11.6 us
    ppermute x5, waiting for transfers between devices, whole_sum(): lax.ppermute(value, axis, [(i, i ^ step) for i in range(count)])  7.92 us
    unnamed x25, local copies, waits for them, and re-layouts  5.66 us
    pallas_call x1, Pallas kernels, per_device(): pl.pallas_call(bank_kernel, out_shape=(image_shape, image_shape, pack_sha...  3.81 us
    ppermute x6, waiting for transfers between devices, moved(): return lax.ppermute(value, ('fy', 'fx'), shift(sizes, steps))  1.8 us
    pallas_call x1, Pallas kernels, per_device(): pl.pallas_call(last, out_shape=(image_shape, image_shape), compiler_param...  1.07 us
  transfers between devices with their start and end apart: 11, of which 6 were waited for; matrix products, arithmetic and copies ran while one was open for 0% of the time, Pallas kernels for 1%

profile of v1, /device:TPU:0, one launch (start us, length us, event | category | flops | bytes accessed | tf_op | source)
XLA Modules:
  0.0 48.6 jit_solution(8298190976136386731)
XLA Ops:
  0.6 2.4 %collective-permute-start.5 = (f32[16,32,128]{2,1,0:T(8,128)}, f32[16,32,128]{2,1,0:T(8,128)S(1)}, u32[]{:S(2)}, u32[]{:S(2)}) collective-permute-start(f32[16,32,128]{2,1,0:T(8,128)} %refs_0_.1), channel_id=1, source_target_pairs={{0,4},{1,5},{2,6},{3,7},{4,8},{5,9},{6,10},{7,11},{8,12},{9,13},{1... | collective-permute-start | bytes 786440 | tf_op jit(solution)/shard_map/ppermute | solution.py:268
  3.0 0.9 %copy-done = f32[16,32,128]{2,1,0:T(8,128)S(1)} copy-done((f32[16,32,128]{2,1,0:T(8,128)S(1)}, f32[16,32,128]{2,1,0:T(8,128)}, u32[]{:S(2)}) %copy-start) | copy-done | bytes 262168
  4.0 0.9 %copy-done.2 = f32[16,32,128]{2,1,0:T(8,128)S(1)} copy-done((f32[16,32,128]{2,1,0:T(8,128)S(1)}, f32[16,32,128]{2,1,0:T(8,128)}, u32[]{:S(2)}) %copy-start.2) | copy-done | bytes 262168
  4.9 0.9 %copy-done.4 = f32[16,32,128]{2,1,0:T(8,128)S(1)} copy-done((f32[16,32,128]{2,1,0:T(8,128)S(1)}, f32[16,32,128]{2,1,0:T(8,128)}, u32[]{:S(2)}) %copy-start.4) | copy-done | bytes 262168
  5.9 0.1 first.1
  6.0 0.0 copy-start.11
  6.0 5.8 %collective-permute-start.7 = (f32[16,8,128]{2,1,0:T(8,128)S(1)}, f32[16,8,128]{2,1,0:T(8,128)S(1)}, u32[]{:S(2)}, u32[]{:S(2)}) collective-permute-start(f32[16,8,128]{2,1,0:T(8,128)S(1)} %get-tuple-element.9), channel_id=1, source_target_pairs={{0,5},{1,6},{2,7},{4,9},{5,10},{6,11},{8,13},{9,14},{10,15},{12,17... | collective-permute-start | bytes 196616 | tf_op jit(solution)/shard_map/ppermute | solution.py:268
  11.8 3.5 %collective-permute-start.6 = (f32[16,8,128]{2,1,0:T(8,128)S(1)}, f32[16,8,128]{2,1,0:T(8,128)S(1)}, u32[]{:S(2)}, u32[]{:S(2)}) collective-permute-start(f32[16,8,128]{2,1,0:T(8,128)S(1)} %get-tuple-element.9), channel_id=1, source_target_pairs={{0,1},{1,2},{2,3},{4,5},{5,6},{6,7},{8,9},{9,10},{10,11},{12,13},{... | collective-permute-start | bytes 196616 | tf_op jit(solution)/shard_map/ppermute | solution.py:268
  15.3 0.1 reshape.7.margin_ref
  15.4 1.8 %collective-permute-done.6.left_ref = f32[16,8,128]{2,1,0:T(8,128)S(1)} collective-permute-done((f32[16,8,128]{2,1,0:T(8,128)S(1)}, f32[16,8,128]{2,1,0:T(8,128)S(1)}, u32[]{:S(2)}, u32[]{:S(2)}) %collective-permute-start.6) | collective-permute-done | bytes 65568 | tf_op jit(solution)/shard_map/ppermute | solution.py:268
  17.2 0.0 collective-permute-done.5.above_ref
  17.2 1.0 %copy-done.7 = f32[2,256,256]{2,1,0:T(8,128)S(1)} copy-done((f32[2,256,256]{2,1,0:T(8,128)S(1)}, f32[2,256,256]{2,1,0:T(8,128)}, u32[]{:S(2)}) %copy-start.7) | copy-done | bytes 524312
  18.3 0.8 %copy-done.8 = f32[2,64,64]{2,1,0:T(8,128)S(1)} copy-done((f32[2,64,64]{2,1,0:T(8,128)S(1)}, f32[2,64,64]{2,1,0:T(8,128)}, u32[]{:S(2)}) %copy-start.8) | copy-done | bytes 32792
  19.1 0.8 %copy-done.9 = f32[128,64]{1,0:T(8,128)S(1)} copy-done((f32[128,64]{1,0:T(8,128)S(1)}, f32[128,64]{1,0:T(8,128)}, u32[]{:S(2)}) %copy-start.9) | copy-done | bytes 32792
  19.9 3.8 %bank.1 = (f32[16,32,128]{2,1,0:T(8,128)S(1)}, f32[16,32,128]{2,1,0:T(8,128)S(1)}, f32[16,8,128]{2,1,0:T(8,128)S(1)}, f32[16,8,128]{2,1,0:T(8,128)S(1)}) custom-call(s32[4]{0:T(128)S(1)} %reshape.7.margin_ref, f32[16,32,128]{2,1,0:T(8,128)S(1)} %copy-done.1, f32[16,32,128]{2,1,0:T(8,128)S(1)} %collective-permute-done.5.above_ref, ...), custom_call_target="tpu_custom_call" | custom-call | tf_op jit(solution)/shard_map/bank/pallas_call | solution.py:292
  23.8 1.3 %collective-permute-start.8 = (f32[16,32,128]{2,1,0:T(8,128)S(1)}, f32[16,32,128]{2,1,0:T(8,128)S(1)}, u32[]{:S(2)}, u32[]{:S(2)}) collective-permute-start(f32[16,32,128]{2,1,0:T(8,128)S(1)} %get-tuple-element.11), channel_id=1, source_target_pairs={{4,0},{5,1},{6,2},{7,3},{8,4},{9,5},{10,6},{11,7},{12,8},{13,9},{1... | collective-permute-start | bytes 786440 | tf_op jit(solution)/shard_map/ppermute | solution.py:268
  25.1 1.3 %collective-permute-start.9 = (f32[16,8,128]{2,1,0:T(8,128)S(1)}, f32[16,8,128]{2,1,0:T(8,128)S(1)}, u32[]{:S(2)}, u32[]{:S(2)}) collective-permute-start(f32[16,8,128]{2,1,0:T(8,128)S(1)} %get-tuple-element.12), channel_id=1, source_target_pairs={{1,0},{2,1},{3,2},{5,4},{6,5},{7,6},{9,8},{10,9},{11,10},{13,12},{... | collective-permute-start | bytes 196616 | tf_op jit(solution)/shard_map/ppermute | solution.py:268
  26.4 1.3 %collective-permute-start.10 = (f32[16,8,128]{2,1,0:T(8,128)S(1)}, f32[16,8,128]{2,1,0:T(8,128)S(1)}, u32[]{:S(2)}, u32[]{:S(2)}) collective-permute-start(f32[16,8,128]{2,1,0:T(8,128)S(1)} %get-tuple-element.13), channel_id=1, source_target_pairs={{5,0},{6,1},{7,2},{9,4},{10,5},{11,6},{13,8},{14,9},{15,10},{17,12... | collective-permute-start | bytes 196616 | tf_op jit(solution)/shard_map/ppermute | solution.py:268
  27.7 1.2 %collective-permute-start = (f32[8,128]{1,0:T(8,128)S(1)}, f32[8,128]{1,0:T(8,128)S(1)}, u32[]{:S(2)}, u32[]{:S(2)}) collective-permute-start(f32[8,128]{1,0:T(8,128)S(1)} %get-tuple-element.8), channel_id=1, source_target_pairs={{0,4},{4,0},{8,12},{12,8},{16,20},{20,16},{24,28},{28,24},{1,5},{5... | collective-permute-start | bytes 12296 | tf_op jit(solution)/shard_map/ppermute | solution.py:251
  28.8 0.8 %collective-permute-done = f32[8,128]{1,0:T(8,128)S(1)} collective-permute-done((f32[8,128]{1,0:T(8,128)S(1)}, f32[8,128]{1,0:T(8,128)S(1)}, u32[]{:S(2)}, u32[]{:S(2)}) %collective-permute-start) | collective-permute-done | bytes 4128 | tf_op jit(solution)/shard_map/ppermute | solution.py:251
  29.7 1.5 %collective-permute-start.1 = (f32[8,128]{1,0:T(8,128)S(1)}, f32[8,128]{1,0:T(8,128)S(1)}, u32[]{:S(2)}, u32[]{:S(2)}) collective-permute-start(f32[8,128]{1,0:T(8,128)S(1)} %add.15), channel_id=1, source_target_pairs={{0,8},{4,12},{8,0},{12,4},{16,24},{20,28},{24,16},{28,20},{1,9},{5... | collective-permute-start | bytes 12296 | tf_op jit(solution)/shard_map/ppermute | solution.py:251
  31.2 2.1 %collective-permute-done.1 = f32[8,128]{1,0:T(8,128)S(1)} collective-permute-done((f32[8,128]{1,0:T(8,128)S(1)}, f32[8,128]{1,0:T(8,128)S(1)}, u32[]{:S(2)}, u32[]{:S(2)}) %collective-permute-start.1) | collective-permute-done | bytes 4128 | tf_op jit(solution)/shard_map/ppermute | solution.py:251
  33.3 1.5 %collective-permute-start.2 = (f32[8,128]{1,0:T(8,128)S(1)}, f32[8,128]{1,0:T(8,128)S(1)}, u32[]{:S(2)}, u32[]{:S(2)}) collective-permute-start(f32[8,128]{1,0:T(8,128)S(1)} %add.16), channel_id=1, source_target_pairs={{0,16},{4,20},{8,24},{12,28},{16,0},{20,4},{24,8},{28,12},{1,17},{... | collective-permute-start | bytes 12296 | tf_op jit(solution)/shard_map/ppermute | solution.py:251
  34.8 2.1 %collective-permute-done.2 = f32[8,128]{1,0:T(8,128)S(1)} collective-permute-done((f32[8,128]{1,0:T(8,128)S(1)}, f32[8,128]{1,0:T(8,128)S(1)}, u32[]{:S(2)}, u32[]{:S(2)}) %collective-permute-start.2) | collective-permute-done | bytes 4128 | tf_op jit(solution)/shard_map/ppermute | solution.py:251
  36.9 4.0 %collective-permute-start.3 = (f32[8,128]{1,0:T(8,128)S(1)}, f32[8,128]{1,0:T(8,128)S(1)}, u32[]{:S(2)}, u32[]{:S(2)}) collective-permute-start(f32[8,128]{1,0:T(8,128)S(1)} %add.17), channel_id=1, source_target_pairs={{0,1},{1,0},{2,3},{3,2},{4,5},{5,4},{6,7},{7,6},{8,9},{9,8},{10,11... | collective-permute-start | bytes 12296 | tf_op jit(solution)/shard_map/ppermute | solution.py:251
  40.9 1.6 %collective-permute-done.3 = f32[8,128]{1,0:T(8,128)S(1)} collective-permute-done((f32[8,128]{1,0:T(8,128)S(1)}, f32[8,128]{1,0:T(8,128)S(1)}, u32[]{:S(2)}, u32[]{:S(2)}) %collective-permute-start.3) | collective-permute-done | bytes 4128 | tf_op jit(solution)/shard_map/ppermute | solution.py:251
  42.5 3.4 %collective-permute-start.4 = (f32[8,128]{1,0:T(8,128)S(1)}, f32[8,128]{1,0:T(8,128)S(1)}, u32[]{:S(2)}, u32[]{:S(2)}) collective-permute-start(f32[8,128]{1,0:T(8,128)S(1)} %add.18), channel_id=1, source_target_pairs={{0,2},{1,3},{2,0},{3,1},{4,6},{5,7},{6,4},{7,5},{8,10},{9,11},{10,... | collective-permute-start | bytes 12296 | tf_op jit(solution)/shard_map/ppermute | solution.py:251
  45.9 0.1 copy.11.seed_ref
  46.0 0.2 basis.1.refs_3_
  46.2 1.3 %collective-permute-done.4 = f32[8,128]{1,0:T(8,128)S(1)} collective-permute-done((f32[8,128]{1,0:T(8,128)S(1)}, f32[8,128]{1,0:T(8,128)S(1)}, u32[]{:S(2)}, u32[]{:S(2)}) %collective-permute-start.4) | collective-permute-done | bytes 4128 | tf_op jit(solution)/shard_map/ppermute | solution.py:251
  47.5 0.0 collective-permute-done.8.refs_6_
  47.5 1.1 %last.1 = (f32[16,32,128]{2,1,0:T(8,128)}, f32[16,32,128]{2,1,0:T(8,128)}) custom-call(f32[16,32,128]{2,1,0:T(8,128)S(1)} %copy-done.1, f32[16,32,128]{2,1,0:T(8,128)S(1)} %copy-done.3, f32[16,32,128]{2,1,0:T(8,128)S(1)} %copy-done.5, f32[4,16,128]{2,1,0:T(8,128)S(1)} %basis.1.refs_3_, f32[8,128]{1,0:T(8,128)S(1)} %add.19.refs_4_, ...), custom_call_target="tpu_custom_call" | custom-call | tf_op jit(solution)/shard_map/last/pallas_call | solution.py:309
  (25 shorter events, 0.1 us)
Async XLA Ops:
  0.6 16.6 %collective-permute-start.5 = (f32[16,32,128]{2,1,0:T(8,128)}, f32[16,32,128]{2,1,0:T(8,128)S(1)}, u32[]{:S(2)}, u32[]{:S(2)}) collective-permute-start(f32[16,32,128]{2,1,0:T(8,128)} %refs_0_.1), channel_id=1, source_target_pairs={{0,4},{1,5},{2,6},{3,7},{4,8},{5,9},{6,10},{7,11},{8,12},{9,13},{1... | collective-permute-start | bytes 786440 | tf_op jit(solution)/shard_map/ppermute | solution.py:268
  3.0 1.0 %copy-start = (f32[16,32,128]{2,1,0:T(8,128)S(1)}, f32[16,32,128]{2,1,0:T(8,128)}, u32[]{:S(2)}) copy-start(f32[16,32,128]{2,1,0:T(8,128)} %refs_0_.1) | copy-start | bytes 786436
  4.0 0.9 %copy-start.2 = (f32[16,32,128]{2,1,0:T(8,128)S(1)}, f32[16,32,128]{2,1,0:T(8,128)}, u32[]{:S(2)}) copy-start(f32[16,32,128]{2,1,0:T(8,128)} %refs_1_.1) | copy-start | bytes 786436
  4.9 0.9 %copy-start.4 = (f32[16,32,128]{2,1,0:T(8,128)S(1)}, f32[16,32,128]{2,1,0:T(8,128)}, u32[]{:S(2)}) copy-start(f32[16,32,128]{2,1,0:T(8,128)} %refs_2_.1) | copy-start | bytes 786436
  5.9 11.3 %copy-start.1 = (f32[16,32,128]{2,1,0:T(8,128)S(1)}, f32[16,32,128]{2,1,0:T(8,128)}, u32[]{:S(2)}) copy-start(f32[16,32,128]{2,1,0:T(8,128)} %refs_0_.1) | copy-start | bytes 786436
  5.9 11.3 %copy-start.6 = (f32[2,256,256]{2,1,0:T(8,128)S(1)}, f32[2,256,256]{2,1,0:T(8,128)}, u32[]{:S(2)}) copy-start(f32[2,256,256]{2,1,0:T(8,128)} %constant.11.clone.cols_t_ref) | copy-start | bytes 1572868
  6.0 9.3 %copy-start.11 = (s32[1,1,2,2]{3,2,1,0:T(2,128)S(1)}, s32[1,1,2,2]{3,2,1,0:T(2,128)}, u32[]{:S(2)}) copy-start(s32[1,1,2,2]{3,2,1,0:T(2,128)} %param.13) | copy-start | bytes 52
  6.0 9.4 %collective-permute-start.7 = (f32[16,8,128]{2,1,0:T(8,128)S(1)}, f32[16,8,128]{2,1,0:T(8,128)S(1)}, u32[]{:S(2)}, u32[]{:S(2)}) collective-permute-start(f32[16,8,128]{2,1,0:T(8,128)S(1)} %get-tuple-element.9), channel_id=1, source_target_pairs={{0,5},{1,6},{2,7},{4,9},{5,10},{6,11},{8,13},{9,14},{10,15},{12,17... | collective-permute-start | bytes 196616 | tf_op jit(solution)/shard_map/ppermute | solution.py:268
  11.8 5.4 %collective-permute-start.6 = (f32[16,8,128]{2,1,0:T(8,128)S(1)}, f32[16,8,128]{2,1,0:T(8,128)S(1)}, u32[]{:S(2)}, u32[]{:S(2)}) collective-permute-start(f32[16,8,128]{2,1,0:T(8,128)S(1)} %get-tuple-element.9), channel_id=1, source_target_pairs={{0,1},{1,2},{2,3},{4,5},{5,6},{6,7},{8,9},{9,10},{10,11},{12,13},{... | collective-permute-start | bytes 196616 | tf_op jit(solution)/shard_map/ppermute | solution.py:268
  17.2 1.0 %copy-start.7 = (f32[2,256,256]{2,1,0:T(8,128)S(1)}, f32[2,256,256]{2,1,0:T(8,128)}, u32[]{:S(2)}) copy-start(f32[2,256,256]{2,1,0:T(8,128)} %constant.10.clone.cols_ref) | copy-start | bytes 1572868
  18.3 0.8 %copy-start.8 = (f32[2,64,64]{2,1,0:T(8,128)S(1)}, f32[2,64,64]{2,1,0:T(8,128)}, u32[]{:S(2)}) copy-start(f32[2,64,64]{2,1,0:T(8,128)} %constant.9.clone.rows_t_ref) | copy-start | bytes 98308
  19.1 0.8 %copy-start.9 = (f32[128,64]{1,0:T(8,128)S(1)}, f32[128,64]{1,0:T(8,128)}, u32[]{:S(2)}) copy-start(f32[128,64]{1,0:T(8,128)} %constant.8.clone.rows_ref) | copy-start | bytes 98308
  19.9 27.6 %copy-start.3 = (f32[16,32,128]{2,1,0:T(8,128)S(1)}, f32[16,32,128]{2,1,0:T(8,128)}, u32[]{:S(2)}) copy-start(f32[16,32,128]{2,1,0:T(8,128)} %refs_1_.1) | copy-start | bytes 786436
  19.9 27.6 %copy-start.5 = (f32[16,32,128]{2,1,0:T(8,128)S(1)}, f32[16,32,128]{2,1,0:T(8,128)}, u32[]{:S(2)}) copy-start(f32[16,32,128]{2,1,0:T(8,128)} %refs_2_.1) | copy-start | bytes 786436
  23.8 23.7 %collective-permute-start.8 = (f32[16,32,128]{2,1,0:T(8,128)S(1)}, f32[16,32,128]{2,1,0:T(8,128)S(1)}, u32[]{:S(2)}, u32[]{:S(2)}) collective-permute-start(f32[16,32,128]{2,1,0:T(8,128)S(1)} %get-tuple-element.11), channel_id=1, source_target_pairs={{4,0},{5,1},{6,2},{7,3},{8,4},{9,5},{10,6},{11,7},{12,8},{13,9},{1... | collective-permute-start | bytes 786440 | tf_op jit(solution)/shard_map/ppermute | solution.py:268
  25.1 22.4 %collective-permute-start.9 = (f32[16,8,128]{2,1,0:T(8,128)S(1)}, f32[16,8,128]{2,1,0:T(8,128)S(1)}, u32[]{:S(2)}, u32[]{:S(2)}) collective-permute-start(f32[16,8,128]{2,1,0:T(8,128)S(1)} %get-tuple-element.12), channel_id=1, source_target_pairs={{1,0},{2,1},{3,2},{5,4},{6,5},{7,6},{9,8},{10,9},{11,10},{13,12},{... | collective-permute-start | bytes 196616 | tf_op jit(solution)/shard_map/ppermute | solution.py:268
  26.4 21.1 %collective-permute-start.10 = (f32[16,8,128]{2,1,0:T(8,128)S(1)}, f32[16,8,128]{2,1,0:T(8,128)S(1)}, u32[]{:S(2)}, u32[]{:S(2)}) collective-permute-start(f32[16,8,128]{2,1,0:T(8,128)S(1)} %get-tuple-element.13), channel_id=1, source_target_pairs={{5,0},{6,1},{7,2},{9,4},{10,5},{11,6},{13,8},{14,9},{15,10},{17,12... | collective-permute-start | bytes 196616 | tf_op jit(solution)/shard_map/ppermute | solution.py:268
  27.7 2.0 %collective-permute-start = (f32[8,128]{1,0:T(8,128)S(1)}, f32[8,128]{1,0:T(8,128)S(1)}, u32[]{:S(2)}, u32[]{:S(2)}) collective-permute-start(f32[8,128]{1,0:T(8,128)S(1)} %get-tuple-element.8), channel_id=1, source_target_pairs={{0,4},{4,0},{8,12},{12,8},{16,20},{20,16},{24,28},{28,24},{1,5},{5... | collective-permute-start | bytes 12296 | tf_op jit(solution)/shard_map/ppermute | solution.py:251
  29.7 3.6 %collective-permute-start.1 = (f32[8,128]{1,0:T(8,128)S(1)}, f32[8,128]{1,0:T(8,128)S(1)}, u32[]{:S(2)}, u32[]{:S(2)}) collective-permute-start(f32[8,128]{1,0:T(8,128)S(1)} %add.15), channel_id=1, source_target_pairs={{0,8},{4,12},{8,0},{12,4},{16,24},{20,28},{24,16},{28,20},{1,9},{5... | collective-permute-start | bytes 12296 | tf_op jit(solution)/shard_map/ppermute | solution.py:251
  33.3 3.6 %collective-permute-start.2 = (f32[8,128]{1,0:T(8,128)S(1)}, f32[8,128]{1,0:T(8,128)S(1)}, u32[]{:S(2)}, u32[]{:S(2)}) collective-permute-start(f32[8,128]{1,0:T(8,128)S(1)} %add.16), channel_id=1, source_target_pairs={{0,16},{4,20},{8,24},{12,28},{16,0},{20,4},{24,8},{28,12},{1,17},{... | collective-permute-start | bytes 12296 | tf_op jit(solution)/shard_map/ppermute | solution.py:251
  36.9 9.0 %copy-start.10 = (f32[16,4]{0,1:T(4,128)S(1)}, f32[16,4]{0,1:T(4,128)}, u32[]{:S(2)}) copy-start(f32[16,4]{0,1:T(4,128)} %param.12) | copy-start | bytes 772
  36.9 5.6 %collective-permute-start.3 = (f32[8,128]{1,0:T(8,128)S(1)}, f32[8,128]{1,0:T(8,128)S(1)}, u32[]{:S(2)}, u32[]{:S(2)}) collective-permute-start(f32[8,128]{1,0:T(8,128)S(1)} %add.17), channel_id=1, source_target_pairs={{0,1},{1,0},{2,3},{3,2},{4,5},{5,4},{6,7},{7,6},{8,9},{9,8},{10,11... | collective-permute-start | bytes 12296 | tf_op jit(solution)/shard_map/ppermute | solution.py:251
  42.5 5.0 %collective-permute-start.4 = (f32[8,128]{1,0:T(8,128)S(1)}, f32[8,128]{1,0:T(8,128)S(1)}, u32[]{:S(2)}, u32[]{:S(2)}) collective-permute-start(f32[8,128]{1,0:T(8,128)S(1)} %add.18), channel_id=1, source_target_pairs={{0,2},{1,3},{2,0},{3,1},{4,6},{5,7},{6,4},{7,5},{8,10},{9,11},{10,... | collective-permute-start | bytes 12296 | tf_op jit(solution)/shard_map/ppermute | solution.py:251

commit v2 on v1

--- a/solution.py
+++ b/solution.py
@@ -106,23 +106,65 @@
     return jnp.concatenate(pieces, axis=0)
 
 
-def first_kernel(start_ref, dirty_ref, sampling_ref, energy_ref, pack_ref):
-    channels, rows, cols = start_ref.shape
+def first_kernel(
+    start_hbm, dirty_hbm, sampling_hbm, energy_ref, pack_ref, own_ref, gain_ref, shifted_ref, dirty_ref, sems
+):
+    channels, rows, cols = own_ref.shape
+    parts = sems.shape[0]
+    size = channels // parts
+    copies = []
+    for part in range(parts):
+        at = pl.ds(part * size, size)
+        trio = [
+            pltpu.make_async_copy(source.at[at], target.at[at], sems.at[part, k])
+            for k, (source, target) in enumerate(
+                ((start_hbm, own_ref), (sampling_hbm, gain_ref), (dirty_hbm, dirty_ref))
+            )
+        ]
+        for copy in trio:
+            copy.start()
+        copies.append(trio)
     total = jnp.zeros((8, cols), jnp.float32)
-    for c in range(channels):
-        field = start_ref[c]
-        shifted = DUAL_STEP * sampling_ref[c] * field - DUAL_STEP * dirty_ref[c]
-        square = shifted * shifted
-        for q in range(rows // 8):
-            total = total + square[8 * q : 8 * q + 8]
-        pack_ref[c] = pack_rows(field, cols - BORDER)
+    for part in range(parts):
+        for copy in copies[part]:
+            copy.wait()
+        for c in range(part * size, (part + 1) * size):
+            field = own_ref[c]
+            shifted = DUAL_STEP * gain_ref[c] * field - DUAL_STEP * dirty_ref[c]
+            shifted_ref[c] = shifted
+            square = shifted * shifted
+            for q in range(rows // 8):
+                total = total + square[8 * q : 8 * q + 8]
+            pack_ref[c] = pack_rows(field, cols - BORDER)
     energy_ref[...] = total
 
 
-def basis_kernel(seed_ref, basis_ref):
-    channels, rank = seed_ref.shape
-    seed = seed_ref[...]
-    columns = [jnp.broadcast_to(seed[:, r : r + 1], (channels, LANES)) for r in range(rank)]
+def prepare_kernel(
+    margin_ref, seed_ref, after_ref, rows_hbm, rows_t_hbm, cols_hbm,
+    basis_ref, a_ref, at_ref, g_ref, rows_ref, rows_t_ref, cols_ref, sems,
+):
+    copies = [
+        pltpu.make_async_copy(rows_hbm, rows_ref, sems.at[0]),
+        pltpu.make_async_copy(rows_t_hbm, rows_t_ref, sems.at[1]),
+    ]
+    for level in range(LEVELS):
+        for k in range(2):
+            span = pl.ds(k * (cols_ref.shape[1] // 2), cols_ref.shape[1] // 2)
+            copies.append(
+                pltpu.make_async_copy(
+                    cols_hbm.at[level, span], cols_ref.at[level, span], sems.at[2 + 2 * level + k]
+                )
+            )
+    for copy in copies:
+        copy.start()
+
+    rank, channels = seed_ref.shape
+    eye = row_iota((channels, channels)) == lane_iota((channels, channels))
+    columns = []
+    for r in range(rank):
+        row = jnp.broadcast_to(seed_ref[r : r + 1, :], (channels, channels))
+        column = jnp.sum(jnp.where(eye, row, 0.0), axis=1, keepdims=True)
+        columns.append(jnp.broadcast_to(column, (channels, LANES)))
     for r in range(rank):
         vector = columns[r]
         vector = vector / jnp.sqrt(jnp.sum(vector * vector, axis=0, keepdims=True))
@@ -131,36 +173,53 @@
             along = jnp.sum(vector * columns[later], axis=0, keepdims=True)
             columns[later] = columns[later] - along * vector
 
+    for copy in copies:
+        copy.wait()
+    half, tall = rows_ref.shape[0] // LEVELS, rows_ref.shape[1]
+    wide, double = cols_ref.shape[1:]
+    cols = double // 2
+    first_row = lax.axis_index("fy") == 0
+    first_col = lax.axis_index("fx") == 0
+    position = lane_iota((half, tall)) - BORDER
+    position_t = row_iota((tall, half)) - BORDER
+    a_parts, at_parts = [], []
+    for level in range(LEVELS):
+        width = jnp.where(first_row, 0, margin_ref[0, 0, level, 0])
+        a_parts.append(jnp.where(position >= -width, rows_ref[level * half : (level + 1) * half], 0.0))
+        at_parts.append(jnp.where(position_t >= -width, rows_t_ref[level], 0.0))
+    a_high, a_low = terms(jnp.concatenate(a_parts, axis=0))
+    a_ref[...] = jnp.concatenate([a_high, a_high, a_low], axis=1)
+    at_pairs = [terms(part) for part in at_parts]
+    at_ref[...] = jnp.concatenate(
+        [pair[0] for pair in at_pairs] * 2 + [pair[1] for pair in at_pairs], axis=1
+    )
+    at = row_iota((wide, double))
+    for level in range(LEVELS):
+        width = jnp.where(first_col, 0, margin_ref[0, 0, level, 1])
+        g = jnp.where((at < cols) | (at >= cols + BORDER - width), cols_ref[level], 0.0)
+        g_high, g_low = terms(g)
+        g_ref[level, 0] = g_high
+        g_ref[level, 1] = g_low
+
+
+def dot_t(a, b):
+    return lax.dot_general(a, b, (((1,), (1,)), ((), ())), preferred_element_type=jnp.float32)
+
 
 def bank_kernel(
-    margin_ref, own_ref, above_ref, left_ref, corner_ref, rows_ref, rows_t_ref, cols_ref, cols_t_ref,
+    own_ref, above_ref, left_ref, corner_ref, a_ref, at_ref, g_ref,
     own_out, above_out, left_out, corner_out, z_high, z_low, u_high, u_low,
 ):
     channels, rows, cols = own_ref.shape
     groups = rows // 8
-    tall = rows + BORDER
     wide = cols + LANES
     half = 2 * rows
-
-    position = lane_iota((half, tall)) - BORDER
-    position_t = row_iota((tall, half)) - BORDER
-    a_parts, at_parts = [], []
-    for level in range(LEVELS):
-        width = margin_ref[2 * level]
-        a_parts.append(jnp.where(position >= -width, rows_ref[level * half : (level + 1) * half], 0.0))
-        at_parts.append(jnp.where(position_t >= -width, rows_t_ref[level], 0.0))
-    a_high, a_low = terms(jnp.concatenate(a_parts, axis=0))
-    a_cat = jnp.concatenate([a_high, a_high, a_low], axis=1)
-    at_pairs = [terms(part) for part in at_parts]
-    at_cat = jnp.concatenate(
-        [pair[0] for pair in at_pairs] * 2 + [pair[1] for pair in at_pairs], axis=1
-    )
 
     for c in range(channels):
         upper = jnp.concatenate([above_ref[c], unpack_rows(corner_ref[c], 0, groups)], axis=1)
         lower = jnp.concatenate([own_ref[c], unpack_rows(left_ref[c], 0, groups)], axis=1)
         e_high, e_low = terms(jnp.concatenate([upper, lower], axis=0))
-        z = dot(a_cat, jnp.concatenate([e_high, e_low, e_high], axis=0))
+        z = dot(a_ref[...], jnp.concatenate([e_high, e_low, e_high], axis=0))
         part_high, part_low = terms(z)
         for level in range(LEVELS):
             z_high[level, c] = part_high[level * half : (level + 1) * half]
@@ -171,21 +230,15 @@
     bound = jnp.where(low_rows & low_cols, 0.0, CLIP_LEVEL / BAND_STEP)
     bound = jnp.broadcast_to(bound[None], (channels, half, 2 * cols)).reshape(channels * half, 2 * cols)
     for level in range(LEVELS):
-        width = margin_ref[2 * level + 1]
-        at = row_iota((wide, 2 * cols))
-        g = jnp.where((at < cols) | (at >= cols + BORDER - width), cols_ref[level], 0.0)
-        at = lane_iota((2 * cols, wide))
-        g_t = jnp.where((at < cols) | (at >= cols + BORDER - width), cols_t_ref[level], 0.0)
-        g_high, g_low = terms(g)
         zh = z_high[level].reshape(channels * half, wide)
         zl = z_low[level].reshape(channels * half, wide)
+        g_high, g_low = g_ref[level, 0], g_ref[level, 1]
         coef = dot(jnp.concatenate([zh, zl, zh], axis=1), jnp.concatenate([g_high, g_high, g_low], axis=0))
         coef = jnp.minimum(jnp.maximum(coef, -bound), bound)
         t_high, t_low = terms(coef)
-        gt_high, gt_low = terms(g_t)
-        u = dot(
+        u = dot_t(
             jnp.concatenate([t_high, t_low, t_high], axis=1),
-            jnp.concatenate([gt_high, gt_high, gt_low], axis=0),
+            jnp.concatenate([g_high, g_high, g_low], axis=1),
         )
         part_high, part_low = terms(u)
         u_high[level] = part_high.reshape(channels, half, wide)
@@ -194,7 +247,7 @@
     for c in range(channels):
         highs = [u_high[level, c] for level in range(LEVELS)]
         lows = [u_low[level, c] for level in range(LEVELS)]
-        back = dot(at_cat, jnp.concatenate(highs + lows + highs, axis=0))
+        back = dot(at_ref[...], jnp.concatenate(highs + lows + highs, axis=0))
         above_out[c] = back[:BORDER, :cols]
         own_out[c] = back[BORDER:, :cols]
         corner_out[c] = pack_rows(back[:BORDER, cols:], 0)
@@ -202,7 +255,7 @@
 
 
 def last_kernel(
-    radius, start_ref, dirty_ref, sampling_ref, basis_ref, energy_ref, own_ref, below_ref, right_ref, corner_ref,
+    radius, start_ref, shifted_ref, sampling_ref, basis_ref, energy_ref, own_ref, below_ref, right_ref, corner_ref,
     image_ref, dual_ref,
 ):
     channels, rows, cols = start_ref.shape
@@ -216,7 +269,7 @@
     for c in range(channels):
         field = start_ref[c]
         gain = sampling_ref[c]
-        dual = factor * (DUAL_STEP * gain * field - DUAL_STEP * dirty_ref[c])
+        dual = factor * shifted_ref[c]
         dual_ref[c] = dual
         strip = unpack_rows(right_ref[c] + corner_ref[c], cols - BORDER, groups)
         prior = own_ref[c] + below_ref[c] + jnp.where(edge, strip, 0.0)
@@ -231,13 +284,14 @@
 
 
 def shift(axis_sizes, steps):
-    pairs = []
-    for a in range(axis_sizes[0]):
-        for b in range(axis_sizes[1]):
-            to_a, to_b = a + steps[0], b + steps[1]
-            if 0 <= to_a < axis_sizes[0] and 0 <= to_b < axis_sizes[1]:
-                pairs.append((a * axis_sizes[1] + b, to_a * axis_sizes[1] + to_b))
-    return pairs
+    return [
+        (
+            a * axis_sizes[1] + b,
+            (a + steps[0]) % axis_sizes[0] * axis_sizes[1] + (b + steps[1]) % axis_sizes[1],
+        )
+        for a in range(axis_sizes[0])
+        for b in range(axis_sizes[1])
+    ]
 
 
 def whole_sum(value):
@@ -255,50 +309,72 @@
 
 def per_device(start_image, dirty, sampling, basis_seed, margin):
     channels, rows, cols = start_image.shape
+    rank = basis_seed.shape[1]
     sizes = (lax.axis_size("fy"), lax.axis_size("fx"))
     half = 2 * rows
+    tall = rows + BORDER
     wide = cols + LANES
     radius = BALL_SCALE * math.sqrt(channels * rows * cols * sizes[0] * sizes[1])
-    f32 = jnp.float32
+    f32, bf16 = jnp.float32, jnp.bfloat16
     image_shape = jax.ShapeDtypeStruct((channels, rows, cols), f32)
     pack_shape = jax.ShapeDtypeStruct((channels, 8, LANES), f32)
     params = pltpu.CompilerParams(vmem_limit_bytes=48 * 1024 * 1024)
+    vmem = pl.BlockSpec(memory_space=pltpu.VMEM)
+    smem = pl.BlockSpec(memory_space=pltpu.SMEM)
+    hbm = pl.BlockSpec(memory_space=pltpu.HBM)
+    anywhere = pl.BlockSpec(memory_space=pl.ANY)
+
+    def kept(value):
+        return pltpu.with_memory_space_constraint(value, pltpu.HBM)
 
     def moved(value, steps):
         return lax.ppermute(value, ("fy", "fx"), shift(sizes, steps))
 
     above = moved(start_image, (1, 0))
-    energy, pack = pl.pallas_call(
+    energy, pack, own, gain, shifted = pl.pallas_call(
         first_kernel,
-        out_shape=(jax.ShapeDtypeStruct((8, cols), f32), pack_shape),
+        out_shape=(jax.ShapeDtypeStruct((8, cols), f32), pack_shape, image_shape, image_shape, image_shape),
+        in_specs=[hbm] * 3,
+        out_specs=(vmem,) * 5,
+        scratch_shapes=[pltpu.VMEM((channels, rows, cols), f32), pltpu.SemaphoreType.DMA((4, 3))],
         compiler_params=params,
         name="first",
-    )(start_image, dirty, sampling)
+    )(kept(start_image), kept(dirty), kept(sampling))
     left = moved(pack, (0, 1))
     corner = moved(pack, (1, 1))
-    basis = pl.pallas_call(
-        basis_kernel,
-        out_shape=jax.ShapeDtypeStruct((basis_seed.shape[1], channels, LANES), f32),
+
+    table = row_table(rows)
+    table_t = np.ascontiguousarray(table.reshape(LEVELS, half, tall).transpose(0, 2, 1))
+    basis, a, a_t, g = pl.pallas_call(
+        prepare_kernel,
+        out_shape=(
+            jax.ShapeDtypeStruct((rank, channels, LANES), f32),
+            jax.ShapeDtypeStruct((LEVELS * half, 3 * tall), bf16),
+            jax.ShapeDtypeStruct((tall, 3 * LEVELS * half), bf16),
+            jax.ShapeDtypeStruct((LEVELS, 2, wide, 2 * cols), bf16),
+        ),
+        in_specs=[smem, vmem, anywhere, hbm, hbm, hbm],
+        out_specs=(vmem,) * 4,
+        scratch_shapes=[
+            pltpu.VMEM((LEVELS * half, tall), f32),
+            pltpu.VMEM((LEVELS, tall, half), f32),
+            pltpu.VMEM((LEVELS, wide, 2 * cols), f32),
+            pltpu.SemaphoreType.DMA((2 + 2 * LEVELS,)),
+        ],
         compiler_params=params,
-        name="basis",
-    )(basis_seed)
+        name="prepare",
+    )(margin, basis_seed.T, pack, kept(jnp.asarray(table)), kept(jnp.asarray(table_t)), kept(jnp.asarray(col_table(cols))))
     energy = whole_sum(energy)
 
-    table = row_table(rows)
-    table_t = np.ascontiguousarray(table.reshape(LEVELS, half, rows + BORDER).transpose(0, 2, 1))
-    col = col_table(cols)
-    col_t = np.ascontiguousarray(col.transpose(0, 2, 1))
-    vmem = pl.BlockSpec(memory_space=pltpu.VMEM)
     own_part, above_part, left_part, corner_part = pl.pallas_call(
         bank_kernel,
         out_shape=(image_shape, image_shape, pack_shape, pack_shape),
-        in_specs=[pl.BlockSpec(memory_space=pltpu.SMEM)] + [vmem] * 8,
-        scratch_shapes=[
-            pltpu.VMEM((LEVELS, channels, half, wide), jnp.bfloat16) for i in range(4)
-        ],
+        in_specs=[vmem] * 7,
+        out_specs=(vmem,) * 4,
+        scratch_shapes=[pltpu.VMEM((LEVELS, channels, half, wide), bf16) for i in range(4)],
         compiler_params=params,
         name="bank",
-    )(margin.reshape(-1), start_image, above, left, corner, table, table_t, col, col_t)
+    )(own, above, left, corner, a, a_t, g)
     below = moved(above_part, (-1, 0))
     right = moved(left_part, (0, -1))
     corner_back = moved(corner_part, (-1, -1))
@@ -309,9 +385,10 @@
     return pl.pallas_call(
         last,
         out_shape=(image_shape, image_shape),
+        in_specs=[vmem] * 9,
         compiler_params=params,
         name="last",
-    )(start_image, dirty, sampling, basis, energy, own_part, below, right, corner_back)
+    )(own, shifted, gain, basis, energy, own_part, below, right, corner_back)
 
 
 def solution(mesh):

time: 49.1 us -> 36.5 us (0.74)
  starting transfers between devices: 27.2 us -> 13.5 us
  local copies, waits for them, and re-layouts: 5.75 us -> 0.01 us
  waiting for transfers between devices: 9.72 us -> 14.4 us
  Pallas kernels: 5.18 us -> 7.63 us
    ppermute x5, starting transfers between devices: 11.6 us -> 4.67 us  [whole_sum(): lax.ppermute(value, axis, [(i, i ^ step) for i in range(count)])]
    ppermute x6, starting transfers between devices: 15.6 us -> 8.87 us  [moved(): return lax.ppermute(value, ('fy', 'fx'), shift(sizes, steps))]
    unnamed x25 -> x4, local copies, waits for them, and re-layouts: 5.66 us -> 0.01 us
    ppermute x5, waiting for transfers between devices: 7.92 us -> 11.8 us  [whole_sum(): lax.ppermute(value, axis, [(i, i ^ step) for i in range(count)])]
    pallas_call x2, Pallas kernels: 1.25 us -> 3 us  [the longest x1 1.95 us: per_device(): pl.pallas_call(prepare_kernel, out_shape=(jax.ShapeDtypeStruct((rank, cha...]
    pallas_call x1, Pallas kernels: 0.11 us -> 1.36 us  [per_device(): pl.pallas_call(first_kernel, out_shape=(jax.ShapeDtypeStruct((8, cols), f...]
    ppermute x6, waiting for transfers between devices: 1.8 us -> 2.55 us  [moved(): return lax.ppermute(value, ('fy', 'fx'), shift(sizes, steps))]
    pallas_call x1, Pallas kernels: 3.81 us -> 3.27 us  [per_device(): pl.pallas_call(bank_kernel, out_shape=(image_shape, image_shape, pack_sha...]
  transfers between devices with their start and end apart: 11 -> 11, of which waited for: 6 -> 7; matrix products, arithmetic and copies ran while one was open for 0% -> 0% of each run, Pallas kernels for 1% -> 9%
where the time goes in v2:
time: 36.5 us; the launch traced here: 36.3 us
  waiting for transfers between devices  14.4 us (39%)
  starting transfers between devices  13.5 us (37%)
  Pallas kernels  7.63 us (21%)
  between operations  0.69 us (2%)
    ppermute x5, waiting for transfers between devices, whole_sum(): lax.ppermute(value, axis, [(i, i ^ step) for i in range(count)])  11.8 us
    ppermute x6, starting transfers between devices, moved(): return lax.ppermute(value, ('fy', 'fx'), shift(sizes, steps))  8.87 us
    ppermute x5, starting transfers between devices, whole_sum(): lax.ppermute(value, axis, [(i, i ^ step) for i in range(count)])  4.67 us
    pallas_call x1, Pallas kernels, per_device(): pl.pallas_call(bank_kernel, out_shape=(image_shape, image_shape, pack_sha...  3.27 us
    ppermute x6, waiting for transfers between devices, moved(): return lax.ppermute(value, ('fy', 'fx'), shift(sizes, steps))  2.55 us
    pallas_call x1, Pallas kernels, per_device(): pl.pallas_call(prepare_kernel, out_shape=(jax.ShapeDtypeStruct((rank, cha...  1.95 us
    pallas_call x1, Pallas kernels, per_device(): pl.pallas_call(first_kernel, out_shape=(jax.ShapeDtypeStruct((8, cols), f...  1.36 us
    pallas_call x1, Pallas kernels, per_device(): pl.pallas_call(last, out_shape=(image_shape, image_shape), in_specs=[vmem...  1.05 us
  transfers between devices with their start and end apart: 11, of which 7 were waited for; matrix products, arithmetic and copies ran while one was open for 0% of the time, Pallas kernels for 9%

profile of v2, /device:TPU:0, one launch (start us, length us, event | category | flops | bytes accessed | tf_op | source)
XLA Modules:
  0.0 36.3 jit_solution(2236638322455695070)
XLA Ops:
  0.6 0.5 %collective-permute-start.5 = (f32[16,32,128]{2,1,0:T(8,128)}, f32[16,32,128]{2,1,0:T(8,128)S(1)}, u32[]{:S(2)}, u32[]{:S(2)}) collective-permute-start(f32[16,32,128]{2,1,0:T(8,128)} %start_hbm.1), channel_id=1, source_target_pairs={{0,4},{1,5},{2,6},{3,7},{4,8},{5,9},{6,10},{7,11},{8,12},{9,13},{1... | collective-permute-start | bytes 786440 | tf_op jit(solution)/shard_map/ppermute | solution.py:331
  1.1 1.4 %first.1 = (f32[8,128]{1,0:T(8,128)S(1)}, f32[16,8,128]{2,1,0:T(8,128)S(1)}, f32[16,32,128]{2,1,0:T(8,128)S(1)}, f32[16,32,128]{2,1,0:T(8,128)S(1)}, f32[16,32,128]{2,1,0:T(8,128)S(1)}) custom-call(f32[16,32,128]{2,1,0:T(8,128)} %start_hbm.1, f32[16,32,128]{2,1,0:T(8,128)} %dirty_hbm.1, f32[16,32,128]{2,1,0:T(8,128)} %sampling_hbm.1), custom_call_target="tpu_custom_call" | custom-call | tf_op jit(solution)/shard_map/first/pallas_call | solution.py:334
  2.5 0.0 copy-start
  2.5 0.0 copy-start.1
  2.5 3.8 %collective-permute-start.7 = (f32[16,8,128]{2,1,0:T(8,128)S(1)}, f32[16,8,128]{2,1,0:T(8,128)S(1)}, u32[]{:S(2)}, u32[]{:S(2)}) collective-permute-start(f32[16,8,128]{2,1,0:T(8,128)S(1)} %get-tuple-element.18.after_ref), channel_id=1, source_target_pairs={{0,5},{1,6},{2,7},{3,4},{4,9},{5,10},{6,11},{7,8},{8,13},{9,14},{1... | collective-permute-start | bytes 196616 | tf_op jit(solution)/shard_map/ppermute | solution.py:331
  6.4 1.6 %collective-permute-start.6 = (f32[16,8,128]{2,1,0:T(8,128)S(1)}, f32[16,8,128]{2,1,0:T(8,128)S(1)}, u32[]{:S(2)}, u32[]{:S(2)}) collective-permute-start(f32[16,8,128]{2,1,0:T(8,128)S(1)} %get-tuple-element.18.after_ref), channel_id=1, source_target_pairs={{0,1},{1,2},{2,3},{3,0},{4,5},{5,6},{6,7},{7,4},{8,9},{9,10},{10,1... | collective-permute-start | bytes 196616 | tf_op jit(solution)/shard_map/ppermute | solution.py:331
  7.9 0.0 copy-done
  7.9 0.0 copy-done.1
  7.9 1.9 %prepare.1 = (f32[4,16,128]{2,1,0:T(8,128)S(1)}, bf16[128,192]{1,0:T(8,128)(2,1)S(1)}, bf16[64,384]{1,0:T(8,128)(2,1)S(1)}, bf16[2,2,256,256]{3,2,1,0:T(8,128)(2,1)S(1)}) custom-call(s32[1,1,2,2]{3,2,1,0:T(2,128)S(1)} %copy-done.1, f32[4,16]{1,0:T(4,128)S(1)} %bitcast.1, f32[16,8,128]{2,1,0:T(8,128)S(1)} %get-tuple-element.18.after_ref, ...), custom_call_target="tpu_custom_call" | custom-call | tf_op jit(solution)/shard_map/prepare/pallas_call | solution.py:348
  9.9 1.9 %collective-permute-done.7.corner_ref = f32[16,8,128]{2,1,0:T(8,128)S(1)} collective-permute-done((f32[16,8,128]{2,1,0:T(8,128)S(1)}, f32[16,8,128]{2,1,0:T(8,128)S(1)}, u32[]{:S(2)}, u32[]{:S(2)}) %collective-permute-start.7) | collective-permute-done | bytes 65568 | tf_op jit(solution)/shard_map/ppermute | solution.py:331
  11.8 0.7 %collective-permute-done.6.left_ref = f32[16,8,128]{2,1,0:T(8,128)S(1)} collective-permute-done((f32[16,8,128]{2,1,0:T(8,128)S(1)}, f32[16,8,128]{2,1,0:T(8,128)S(1)}, u32[]{:S(2)}, u32[]{:S(2)}) %collective-permute-start.6) | collective-permute-done | bytes 65568 | tf_op jit(solution)/shard_map/ppermute | solution.py:331
  12.4 0.0 collective-permute-done.5.above_ref
  12.4 3.3 %bank.1 = (f32[16,32,128]{2,1,0:T(8,128)S(1)}, f32[16,32,128]{2,1,0:T(8,128)S(1)}, f32[16,8,128]{2,1,0:T(8,128)S(1)}, f32[16,8,128]{2,1,0:T(8,128)S(1)}) custom-call(f32[16,32,128]{2,1,0:T(8,128)S(1)} %get-tuple-element.15.own_ref.refs_0_, f32[16,32,128]{2,1,0:T(8,128)S(1)} %collective-permute-done.5.above_ref, ...), custom_call_target="tpu_custom_call" | custom-call | tf_op jit(solution)/shard_map/bank/pallas_call | solution.py:369
  15.7 0.3 collective-permute-start.8
  16.0 1.6 %collective-permute-start.9 = (f32[16,8,128]{2,1,0:T(8,128)S(1)}, f32[16,8,128]{2,1,0:T(8,128)S(1)}, u32[]{:S(2)}, u32[]{:S(2)}) collective-permute-start(f32[16,8,128]{2,1,0:T(8,128)S(1)} %get-tuple-element.26), channel_id=1, source_target_pairs={{0,3},{1,0},{2,1},{3,2},{4,7},{5,4},{6,5},{7,6},{8,11},{9,8},{10,9... | collective-permute-start | bytes 196616 | tf_op jit(solution)/shard_map/ppermute | solution.py:331
  17.7 1.0 %collective-permute-start.10 = (f32[16,8,128]{2,1,0:T(8,128)S(1)}, f32[16,8,128]{2,1,0:T(8,128)S(1)}, u32[]{:S(2)}, u32[]{:S(2)}) collective-permute-start(f32[16,8,128]{2,1,0:T(8,128)S(1)} %get-tuple-element.27), channel_id=1, source_target_pairs={{0,31},{1,28},{2,29},{3,30},{4,3},{5,0},{6,1},{7,2},{8,7},{9,4},{1... | collective-permute-start | bytes 196616 | tf_op jit(solution)/shard_map/ppermute | solution.py:331
  18.7 0.0 collective-permute-start
  18.7 1.2 %collective-permute-done = f32[8,128]{1,0:T(8,128)S(1)} collective-permute-done((f32[8,128]{1,0:T(8,128)S(1)}, f32[8,128]{1,0:T(8,128)S(1)}, u32[]{:S(2)}, u32[]{:S(2)}) %collective-permute-start) | collective-permute-done | bytes 4128 | tf_op jit(solution)/shard_map/ppermute | solution.py:305
  19.8 0.6 %collective-permute-start.1 = (f32[8,128]{1,0:T(8,128)S(1)}, f32[8,128]{1,0:T(8,128)S(1)}, u32[]{:S(2)}, u32[]{:S(2)}) collective-permute-start(f32[8,128]{1,0:T(8,128)S(1)} %add.15), channel_id=1, source_target_pairs={{0,8},{4,12},{8,0},{12,4},{16,24},{20,28},{24,16},{28,20},{1,9},{5... | collective-permute-start | bytes 12296 | tf_op jit(solution)/shard_map/ppermute | solution.py:305
  20.5 3.0 %collective-permute-done.1 = f32[8,128]{1,0:T(8,128)S(1)} collective-permute-done((f32[8,128]{1,0:T(8,128)S(1)}, f32[8,128]{1,0:T(8,128)S(1)}, u32[]{:S(2)}, u32[]{:S(2)}) %collective-permute-start.1) | collective-permute-done | bytes 4128 | tf_op jit(solution)/shard_map/ppermute | solution.py:305
  23.5 1.5 %collective-permute-start.2 = (f32[8,128]{1,0:T(8,128)S(1)}, f32[8,128]{1,0:T(8,128)S(1)}, u32[]{:S(2)}, u32[]{:S(2)}) collective-permute-start(f32[8,128]{1,0:T(8,128)S(1)} %add.16), channel_id=1, source_target_pairs={{0,16},{4,20},{8,24},{12,28},{16,0},{20,4},{24,8},{28,12},{1,17},{... | collective-permute-start | bytes 12296 | tf_op jit(solution)/shard_map/ppermute | solution.py:305
  25.0 2.1 %collective-permute-done.2 = f32[8,128]{1,0:T(8,128)S(1)} collective-permute-done((f32[8,128]{1,0:T(8,128)S(1)}, f32[8,128]{1,0:T(8,128)S(1)}, u32[]{:S(2)}, u32[]{:S(2)}) %collective-permute-start.2) | collective-permute-done | bytes 4128 | tf_op jit(solution)/shard_map/ppermute | solution.py:305
  27.1 1.3 %collective-permute-start.3 = (f32[8,128]{1,0:T(8,128)S(1)}, f32[8,128]{1,0:T(8,128)S(1)}, u32[]{:S(2)}, u32[]{:S(2)}) collective-permute-start(f32[8,128]{1,0:T(8,128)S(1)} %add.17), channel_id=1, source_target_pairs={{0,1},{1,0},{2,3},{3,2},{4,5},{5,4},{6,7},{7,6},{8,9},{9,8},{10,11... | collective-permute-start | bytes 12296 | tf_op jit(solution)/shard_map/ppermute | solution.py:305
  28.3 2.3 %collective-permute-done.3 = f32[8,128]{1,0:T(8,128)S(1)} collective-permute-done((f32[8,128]{1,0:T(8,128)S(1)}, f32[8,128]{1,0:T(8,128)S(1)}, u32[]{:S(2)}, u32[]{:S(2)}) %collective-permute-start.3) | collective-permute-done | bytes 4128 | tf_op jit(solution)/shard_map/ppermute | solution.py:305
  30.7 1.3 %collective-permute-start.4 = (f32[8,128]{1,0:T(8,128)S(1)}, f32[8,128]{1,0:T(8,128)S(1)}, u32[]{:S(2)}, u32[]{:S(2)}) collective-permute-start(f32[8,128]{1,0:T(8,128)S(1)} %add.18), channel_id=1, source_target_pairs={{0,2},{1,3},{2,0},{3,1},{4,6},{5,7},{6,4},{7,5},{8,10},{9,11},{10,... | collective-permute-start | bytes 12296 | tf_op jit(solution)/shard_map/ppermute | solution.py:305
  31.9 3.3 %collective-permute-done.4 = f32[8,128]{1,0:T(8,128)S(1)} collective-permute-done((f32[8,128]{1,0:T(8,128)S(1)}, f32[8,128]{1,0:T(8,128)S(1)}, u32[]{:S(2)}, u32[]{:S(2)}) %collective-permute-start.4) | collective-permute-done | bytes 4128 | tf_op jit(solution)/shard_map/ppermute | solution.py:305
  35.2 0.0 collective-permute-done.9.refs_7_
  35.2 0.0 collective-permute-done.10.refs_8_
  35.2 0.0 collective-permute-done.8.refs_6_
  35.2 1.1 %last.1 = (f32[16,32,128]{2,1,0:T(8,128)}, f32[16,32,128]{2,1,0:T(8,128)}) custom-call(f32[16,32,128]{2,1,0:T(8,128)S(1)} %get-tuple-element.15.own_ref.refs_0_, f32[16,32,128]{2,1,0:T(8,128)S(1)} %get-tuple-element.16.refs_1_, f32[16,32,128]{2,1,0:T(8,128)S(1)} %get-tuple-element.17.refs_2_, f32[4,16,128]{2,1,0:T(8,128)S(1)} %get-tuple-element.19.refs_3_, ...), custom_call_target="tpu_custom_call" | custom-call | tf_op jit(solution)/shard_map/last/pallas_call | solution.py:385
  (5 shorter events, 0.0 us)
Async XLA Ops:
  0.6 11.8 %collective-permute-start.5 = (f32[16,32,128]{2,1,0:T(8,128)}, f32[16,32,128]{2,1,0:T(8,128)S(1)}, u32[]{:S(2)}, u32[]{:S(2)}) collective-permute-start(f32[16,32,128]{2,1,0:T(8,128)} %start_hbm.1), channel_id=1, source_target_pairs={{0,4},{1,5},{2,6},{3,7},{4,8},{5,9},{6,10},{7,11},{8,12},{9,13},{1... | collective-permute-start | bytes 786440 | tf_op jit(solution)/shard_map/ppermute | solution.py:331
  2.5 5.4 %copy-start = (f32[16,4]{0,1:T(4,128)S(1)}, f32[16,4]{0,1:T(4,128)}, u32[]{:S(2)}) copy-start(f32[16,4]{0,1:T(4,128)} %param.11) | copy-start | bytes 772
  2.5 5.4 %copy-start.1 = (s32[1,1,2,2]{3,2,1,0:T(2,128)S(1)}, s32[1,1,2,2]{3,2,1,0:T(2,128)}, u32[]{:S(2)}) copy-start(s32[1,1,2,2]{3,2,1,0:T(2,128)} %margin_ref.1) | copy-start | bytes 52
  2.5 9.3 %collective-permute-start.7 = (f32[16,8,128]{2,1,0:T(8,128)S(1)}, f32[16,8,128]{2,1,0:T(8,128)S(1)}, u32[]{:S(2)}, u32[]{:S(2)}) collective-permute-start(f32[16,8,128]{2,1,0:T(8,128)S(1)} %get-tuple-element.18.after_ref), channel_id=1, source_target_pairs={{0,5},{1,6},{2,7},{3,4},{4,9},{5,10},{6,11},{7,8},{8,13},{9,14},{1... | collective-permute-start | bytes 196616 | tf_op jit(solution)/shard_map/ppermute | solution.py:331
  6.4 6.1 %collective-permute-start.6 = (f32[16,8,128]{2,1,0:T(8,128)S(1)}, f32[16,8,128]{2,1,0:T(8,128)S(1)}, u32[]{:S(2)}, u32[]{:S(2)}) collective-permute-start(f32[16,8,128]{2,1,0:T(8,128)S(1)} %get-tuple-element.18.after_ref), channel_id=1, source_target_pairs={{0,1},{1,2},{2,3},{3,0},{4,5},{5,6},{6,7},{7,4},{8,9},{9,10},{10,1... | collective-permute-start | bytes 196616 | tf_op jit(solution)/shard_map/ppermute | solution.py:331
  15.7 19.5 %collective-permute-start.8 = (f32[16,32,128]{2,1,0:T(8,128)S(1)}, f32[16,32,128]{2,1,0:T(8,128)S(1)}, u32[]{:S(2)}, u32[]{:S(2)}) collective-permute-start(f32[16,32,128]{2,1,0:T(8,128)S(1)} %get-tuple-element.25), channel_id=1, source_target_pairs={{0,28},{1,29},{2,30},{3,31},{4,0},{5,1},{6,2},{7,3},{8,4},{9,5},{1... | collective-permute-start | bytes 786440 | tf_op jit(solution)/shard_map/ppermute | solution.py:331
  16.0 19.2 %collective-permute-start.9 = (f32[16,8,128]{2,1,0:T(8,128)S(1)}, f32[16,8,128]{2,1,0:T(8,128)S(1)}, u32[]{:S(2)}, u32[]{:S(2)}) collective-permute-start(f32[16,8,128]{2,1,0:T(8,128)S(1)} %get-tuple-element.26), channel_id=1, source_target_pairs={{0,3},{1,0},{2,1},{3,2},{4,7},{5,4},{6,5},{7,6},{8,11},{9,8},{10,9... | collective-permute-start | bytes 196616 | tf_op jit(solution)/shard_map/ppermute | solution.py:331
  17.7 17.5 %collective-permute-start.10 = (f32[16,8,128]{2,1,0:T(8,128)S(1)}, f32[16,8,128]{2,1,0:T(8,128)S(1)}, u32[]{:S(2)}, u32[]{:S(2)}) collective-permute-start(f32[16,8,128]{2,1,0:T(8,128)S(1)} %get-tuple-element.27), channel_id=1, source_target_pairs={{0,31},{1,28},{2,29},{3,30},{4,3},{5,0},{6,1},{7,2},{8,7},{9,4},{1... | collective-permute-start | bytes 196616 | tf_op jit(solution)/shard_map/ppermute | solution.py:331
  18.7 1.2 %collective-permute-start = (f32[8,128]{1,0:T(8,128)S(1)}, f32[8,128]{1,0:T(8,128)S(1)}, u32[]{:S(2)}, u32[]{:S(2)}) collective-permute-start(f32[8,128]{1,0:T(8,128)S(1)} %get-tuple-element.20), channel_id=1, source_target_pairs={{0,4},{4,0},{8,12},{12,8},{16,20},{20,16},{24,28},{28,24},{1,5},{5... | collective-permute-start | bytes 12296 | tf_op jit(solution)/shard_map/ppermute | solution.py:305
  19.8 3.6 %collective-permute-start.1 = (f32[8,128]{1,0:T(8,128)S(1)}, f32[8,128]{1,0:T(8,128)S(1)}, u32[]{:S(2)}, u32[]{:S(2)}) collective-permute-start(f32[8,128]{1,0:T(8,128)S(1)} %add.15), channel_id=1, source_target_pairs={{0,8},{4,12},{8,0},{12,4},{16,24},{20,28},{24,16},{28,20},{1,9},{5... | collective-permute-start | bytes 12296 | tf_op jit(solution)/shard_map/ppermute | solution.py:305
  23.5 3.6 %collective-permute-start.2 = (f32[8,128]{1,0:T(8,128)S(1)}, f32[8,128]{1,0:T(8,128)S(1)}, u32[]{:S(2)}, u32[]{:S(2)}) collective-permute-start(f32[8,128]{1,0:T(8,128)S(1)} %add.16), channel_id=1, source_target_pairs={{0,16},{4,20},{8,24},{12,28},{16,0},{20,4},{24,8},{28,12},{1,17},{... | collective-permute-start | bytes 12296 | tf_op jit(solution)/shard_map/ppermute | solution.py:305
  27.1 3.6 %collective-permute-start.3 = (f32[8,128]{1,0:T(8,128)S(1)}, f32[8,128]{1,0:T(8,128)S(1)}, u32[]{:S(2)}, u32[]{:S(2)}) collective-permute-start(f32[8,128]{1,0:T(8,128)S(1)} %add.17), channel_id=1, source_target_pairs={{0,1},{1,0},{2,3},{3,2},{4,5},{5,4},{6,7},{7,6},{8,9},{9,8},{10,11... | collective-permute-start | bytes 12296 | tf_op jit(solution)/shard_map/ppermute | solution.py:305
  30.7 4.5 %collective-permute-start.4 = (f32[8,128]{1,0:T(8,128)S(1)}, f32[8,128]{1,0:T(8,128)S(1)}, u32[]{:S(2)}, u32[]{:S(2)}) collective-permute-start(f32[8,128]{1,0:T(8,128)S(1)} %add.18), channel_id=1, source_target_pairs={{0,2},{1,3},{2,0},{3,1},{4,6},{5,7},{6,4},{7,5},{8,10},{9,11},{10,... | collective-permute-start | bytes 12296 | tf_op jit(solution)/shard_map/ppermute | solution.py:305

commit v3 on v2

--- a/solution.py
+++ b/solution.py
@@ -207,7 +207,7 @@
 
 
 def bank_kernel(
-    own_ref, above_ref, left_ref, corner_ref, a_ref, at_ref, g_ref,
+    own_ref, above_ref, left_ref, corner_ref, a_ref, at_ref, g_ref, after_ref,
     own_out, above_out, left_out, corner_out, z_high, z_low, u_high, u_low,
 ):
     channels, rows, cols = own_ref.shape
@@ -248,10 +248,10 @@
         highs = [u_high[level, c] for level in range(LEVELS)]
         lows = [u_low[level, c] for level in range(LEVELS)]
         back = dot(at_ref[...], jnp.concatenate(highs + lows + highs, axis=0))
-        above_out[c] = back[:BORDER, :cols]
+        above_out[BORDER * c : BORDER * (c + 1)] = back[:BORDER, :cols]
         own_out[c] = back[BORDER:, :cols]
-        corner_out[c] = pack_rows(back[:BORDER, cols:], 0)
-        left_out[c] = pack_rows(back[BORDER:, cols:], 0)
+        corner_out[8 * c : 8 * (c + 1)] = pack_rows(back[:BORDER, cols:], 0)
+        left_out[8 * c : 8 * (c + 1)] = pack_rows(back[BORDER:, cols:], 0)
 
 
 def last_kernel(
@@ -261,7 +261,10 @@
     channels, rows, cols = start_ref.shape
     rank = basis_ref.shape[0]
     groups = rows // 8
-    energy = jnp.sum(jnp.sum(energy_ref[...], axis=0, keepdims=True), axis=1, keepdims=True)
+    energy = energy_ref[...]
+    for ref in (below_ref, right_ref, corner_ref):
+        energy = energy + ref[pl.ds(ref.shape[0] - 8, 8)]
+    energy = jnp.sum(jnp.sum(energy, axis=0, keepdims=True), axis=1, keepdims=True)
     factor = jnp.maximum(0.0, 1.0 - DUAL_STEP * radius / jnp.sqrt(energy + NORM_EPS))
     factor = jnp.broadcast_to(factor, (rows, cols))
     edge = lane_iota((rows, cols)) >= cols - BORDER
@@ -271,8 +274,9 @@
         gain = sampling_ref[c]
         dual = factor * shifted_ref[c]
         dual_ref[c] = dual
-        strip = unpack_rows(right_ref[c] + corner_ref[c], cols - BORDER, groups)
-        prior = own_ref[c] + below_ref[c] + jnp.where(edge, strip, 0.0)
+        strip = right_ref[8 * c : 8 * (c + 1)] + corner_ref[8 * c : 8 * (c + 1)]
+        strip = unpack_rows(strip, cols - BORDER, groups)
+        prior = own_ref[c] + below_ref[BORDER * c : BORDER * (c + 1)] + jnp.where(edge, strip, 0.0)
         stepped = field - PRIMAL_STEP * (gain * dual + (WEIGHT * BAND_STEP) * prior)
         for r in range(rank):
             weights[r] = weights[r] + basis_ref[r, c : c + 1, :] * stepped
@@ -294,17 +298,41 @@
     ]
 
 
-def whole_sum(value):
-    for axis in ("fy", "fx"):
-        count = lax.axis_size(axis)
-        if count & (count - 1):
-            value = lax.psum(value, axis)
-        else:
-            step = 1
-            while step < count:
-                value = value + lax.ppermute(value, axis, [(i, i ^ step) for i in range(count)])
-                step *= 2
-    return value
+def add_kernel(value_ref, arrived_ref, *refs):
+    refs[-1][...] = value_ref[...] + arrived_ref[...]
+
+
+def doubling():
+    rounds = []
+    for axis in ("fx", "fy"):
+        step = 2
+        while step < lax.axis_size(axis):
+            rounds.append((axis, step))
+            step *= 2
+    return rounds
+
+
+def partner(value, round_):
+    axis, step = round_
+    return lax.ppermute(value, axis, [(i, i ^ step) for i in range(lax.axis_size(axis))])
+
+
+def stamp_kernel(value_ref, arrived_ref, above_in, left_in, corner_in, total_ref, above_ref, left_ref, corner_ref):
+    total = value_ref[...] + arrived_ref[...]
+    total_ref[...] = total
+    for ref in (above_ref, left_ref, corner_ref):
+        ref[pl.ds(ref.shape[0] - 8, 8)] = total
+
+
+def added(value, arrived, *after):
+    return pl.pallas_call(
+        add_kernel,
+        out_shape=jax.ShapeDtypeStruct(value.shape, value.dtype),
+        in_specs=[pl.BlockSpec(memory_space=pltpu.VMEM)] * 2 + [pl.BlockSpec(memory_space=pl.ANY)] * len(after),
+        out_specs=pl.BlockSpec(memory_space=pltpu.VMEM),
+        compiler_params=pltpu.CompilerParams(vmem_limit_bytes=1024 * 1024),
+        name="add",
+    )(value, arrived, *after)
 
 
 def per_device(start_image, dirty, sampling, basis_seed, margin):
@@ -318,7 +346,7 @@
     f32, bf16 = jnp.float32, jnp.bfloat16
     image_shape = jax.ShapeDtypeStruct((channels, rows, cols), f32)
     pack_shape = jax.ShapeDtypeStruct((channels, 8, LANES), f32)
-    params = pltpu.CompilerParams(vmem_limit_bytes=48 * 1024 * 1024)
+    params = pltpu.CompilerParams(vmem_limit_bytes=24 * 1024 * 1024)
     vmem = pl.BlockSpec(memory_space=pltpu.VMEM)
     smem = pl.BlockSpec(memory_space=pltpu.SMEM)
     hbm = pl.BlockSpec(memory_space=pltpu.HBM)
@@ -363,21 +391,34 @@
         ],
         compiler_params=params,
         name="prepare",
-    )(margin, basis_seed.T, pack, kept(jnp.asarray(table)), kept(jnp.asarray(table_t)), kept(jnp.asarray(col_table(cols))))
-    energy = whole_sum(energy)
-
-    own_part, above_part, left_part, corner_part = pl.pallas_call(
+    )(margin, basis_seed.T, energy, kept(jnp.asarray(table)), kept(jnp.asarray(table_t)), kept(jnp.asarray(col_table(cols))))
+    rounds = doubling()
+    for round_ in rounds[:-1]:
+        energy = added(energy, partner(energy, round_), basis)
+
+    above_shape = jax.ShapeDtypeStruct((channels * BORDER + 8, cols), f32)
+    strip_shape = jax.ShapeDtypeStruct((channels * 8 + 8, LANES), f32)
+    own_part, *parts = pl.pallas_call(
         bank_kernel,
-        out_shape=(image_shape, image_shape, pack_shape, pack_shape),
-        in_specs=[vmem] * 7,
+        out_shape=(image_shape, above_shape, strip_shape, strip_shape),
+        in_specs=[vmem] * 7 + [anywhere],
         out_specs=(vmem,) * 4,
         scratch_shapes=[pltpu.VMEM((LEVELS, channels, half, wide), bf16) for i in range(4)],
         compiler_params=params,
         name="bank",
-    )(own, above, left, corner, a, a_t, g)
-    below = moved(above_part, (-1, 0))
-    right = moved(left_part, (0, -1))
-    corner_back = moved(corner_part, (-1, -1))
+    )(own, above, left, corner, a, a_t, g, energy)
+    energy, *parts = pl.pallas_call(
+        stamp_kernel,
+        out_shape=(jax.ShapeDtypeStruct(energy.shape, f32), above_shape, strip_shape, strip_shape),
+        in_specs=[vmem] * 5,
+        out_specs=(vmem,) * 4,
+        input_output_aliases={2: 1, 3: 2, 4: 3},
+        compiler_params=pltpu.CompilerParams(vmem_limit_bytes=1024 * 1024),
+        name="stamp",
+    )(energy, partner(energy, rounds[-1]), *parts)
+    below = moved(parts[0], (-1, 0))
+    right = moved(parts[1], (0, -1))
+    corner_back = moved(parts[2], (-1, -1))
 
     def last(*refs):
         last_kernel(radius, *refs)

time: 36.5 us -> 28.9 us (0.79)
  the two profiles are of different devices: /device:TPU:0 before, /device:TPU:1 now
where the time goes in v3:
time: 28.9 us; the launch traced here: 28.7 us
  starting transfers between devices  13.8 us (48%)
  Pallas kernels  7.68 us (27%)
  waiting for transfers between devices  6.54 us (23%)
  between operations  0.68 us (2%)
    ppermute x6, starting transfers between devices, moved(): return lax.ppermute(value, ('fy', 'fx'), shift(sizes, steps))  10.3 us
    ppermute x6, waiting for transfers between devices, moved(): return lax.ppermute(value, ('fy', 'fx'), shift(sizes, steps))  4.24 us
    ppermute x3, starting transfers between devices, partner(): lax.ppermute(value, axis, [(i, i ^ step) for i in range(lax.axis_size(axi...  3.5 us
    pallas_call x1, Pallas kernels, per_device(): pl.pallas_call(bank_kernel, out_shape=(image_shape, above_shape, strip_sh...  3.29 us
    ppermute x3, waiting for transfers between devices, partner(): lax.ppermute(value, axis, [(i, i ^ step) for i in range(lax.axis_size(axi...  2.29 us
    pallas_call x1, Pallas kernels, per_device(): pl.pallas_call(prepare_kernel, out_shape=(jax.ShapeDtypeStruct((rank, cha...  1.95 us
    pallas_call x1, Pallas kernels, per_device(): pl.pallas_call(first_kernel, out_shape=(jax.ShapeDtypeStruct((8, cols), f...  1.36 us
    pallas_call x1, Pallas kernels, per_device(): pl.pallas_call(last, out_shape=(image_shape, image_shape), in_specs=[vmem...  1.06 us
  transfers between devices with their start and end apart: 9, of which 4 were waited for; matrix products, arithmetic and copies ran while one was open for 0% of the time, Pallas kernels for 23%

profile of v3, /device:TPU:1, one launch (start us, length us, event | category | flops | bytes accessed | tf_op | source)
XLA Modules:
  0.0 28.7 jit_solution(15798110211738008057)
XLA Ops:
  0.6 2.7 %collective-permute-start.3 = (f32[16,32,128]{2,1,0:T(8,128)}, f32[16,32,128]{2,1,0:T(8,128)S(1)}, u32[]{:S(2)}, u32[]{:S(2)}) collective-permute-start(f32[16,32,128]{2,1,0:T(8,128)} %start_hbm.1), channel_id=1, source_target_pairs={{0,4},{1,5},{2,6},{3,7},{4,8},{5,9},{6,10},{7,11},{8,12},{9,13},{1... | collective-permute-start | bytes 786440 | tf_op jit(solution)/shard_map/ppermute | solution.py:359
  3.3 1.4 %first.1 = (f32[8,128]{1,0:T(8,128)S(1)}, f32[16,8,128]{2,1,0:T(8,128)S(1)}, f32[16,32,128]{2,1,0:T(8,128)S(1)}, f32[16,32,128]{2,1,0:T(8,128)S(1)}, f32[16,32,128]{2,1,0:T(8,128)S(1)}) custom-call(f32[16,32,128]{2,1,0:T(8,128)} %start_hbm.1, f32[16,32,128]{2,1,0:T(8,128)} %dirty_hbm.1, f32[16,32,128]{2,1,0:T(8,128)} %sampling_hbm.1), custom_call_target="tpu_custom_call" | custom-call | tf_op jit(solution)/shard_map/first/pallas_call | solution.py:362
  4.7 0.0 copy-start
  4.7 1.1 %collective-permute-start.5 = (f32[16,8,128]{2,1,0:T(8,128)S(1)}, f32[16,8,128]{2,1,0:T(8,128)S(1)}, u32[]{:S(2)}, u32[]{:S(2)}) collective-permute-start(f32[16,8,128]{2,1,0:T(8,128)S(1)} %get-tuple-element.24), channel_id=1, source_target_pairs={{0,5},{1,6},{2,7},{3,4},{4,9},{5,10},{6,11},{7,8},{8,13},{9,14},{1... | collective-permute-start | bytes 196616 | tf_op jit(solution)/shard_map/ppermute | solution.py:359
  5.8 1.3 %collective-permute-start.4 = (f32[16,8,128]{2,1,0:T(8,128)S(1)}, f32[16,8,128]{2,1,0:T(8,128)S(1)}, u32[]{:S(2)}, u32[]{:S(2)}) collective-permute-start(f32[16,8,128]{2,1,0:T(8,128)S(1)} %get-tuple-element.24), channel_id=1, source_target_pairs={{0,1},{1,2},{2,3},{3,0},{4,5},{5,6},{6,7},{7,4},{8,9},{9,10},{10,1... | collective-permute-start | bytes 196616 | tf_op jit(solution)/shard_map/ppermute | solution.py:359
  7.1 0.0 copy-start.1
  7.1 1.3 %collective-permute-start = (f32[8,128]{1,0:T(8,128)S(1)}, f32[8,128]{1,0:T(8,128)S(1)}, u32[]{:S(2)}, u32[]{:S(2)}) collective-permute-start(f32[8,128]{1,0:T(8,128)S(1)} %get-tuple-element.22.after_ref.value_ref), channel_id=1, source_target_pairs={{0,2},{1,3},{2,0},{3,1},{4,6},{5,7},{6,4},{7,5},{8,10},{9,11},{10,... | collective-permute-start | bytes 12296 | tf_op jit(solution)/shard_map/ppermute | solution.py:317
  8.4 0.0 copy-done
  8.4 0.0 copy-done.1
  8.4 1.9 %prepare.1 = (f32[4,16,128]{2,1,0:T(8,128)S(1)}, bf16[128,192]{1,0:T(8,128)(2,1)S(1)}, bf16[64,384]{1,0:T(8,128)(2,1)S(1)}, bf16[2,2,256,256]{3,2,1,0:T(8,128)(2,1)S(1)}) custom-call(s32[1,1,2,2]{3,2,1,0:T(2,128)S(1)} %copy-done.1, f32[4,16]{1,0:T(4,128)S(1)} %bitcast.1, f32[8,128]{1,0:T(8,128)S(1)} %get-tuple-element.22.after_ref.value_ref, ...), custom_call_target="tpu_custom_call" | custom-call | tf_op jit(solution)/shard_map/prepare/pallas_call | solution.py:376
  10.4 0.8 %collective-permute-done.arrived_ref = f32[8,128]{1,0:T(8,128)S(1)} collective-permute-done((f32[8,128]{1,0:T(8,128)S(1)}, f32[8,128]{1,0:T(8,128)S(1)}, u32[]{:S(2)}, u32[]{:S(2)}) %collective-permute-start) | collective-permute-done | bytes 4128 | tf_op jit(solution)/shard_map/ppermute | solution.py:317
  11.1 0.9 %collective-permute-start.1 = (f32[8,128]{1,0:T(8,128)S(1)}, f32[8,128]{1,0:T(8,128)S(1)}, u32[]{:S(2)}, u32[]{:S(2)}) collective-permute-start(f32[8,128]{1,0:T(8,128)S(1)} %add.2.value_ref), channel_id=1, source_target_pairs={{0,8},{4,12},{8,0},{12,4},{16,24},{20,28},{24,16},{28,20},{1,9},{5... | collective-permute-start | bytes 12296 | tf_op jit(solution)/shard_map/ppermute | solution.py:317
  12.0 1.5 %collective-permute-done.1.arrived_ref = f32[8,128]{1,0:T(8,128)S(1)} collective-permute-done((f32[8,128]{1,0:T(8,128)S(1)}, f32[8,128]{1,0:T(8,128)S(1)}, u32[]{:S(2)}, u32[]{:S(2)}) %collective-permute-start.1) | collective-permute-done | bytes 4128 | tf_op jit(solution)/shard_map/ppermute | solution.py:317
  13.6 1.2 %collective-permute-start.2 = (f32[8,128]{1,0:T(8,128)S(1)}, f32[8,128]{1,0:T(8,128)S(1)}, u32[]{:S(2)}, u32[]{:S(2)}) collective-permute-start(f32[8,128]{1,0:T(8,128)S(1)} %add.3.after_ref.value_ref), channel_id=1, source_target_pairs={{0,16},{4,20},{8,24},{12,28},{16,0},{20,4},{24,8},{28,12},{1,17},{... | collective-permute-start | bytes 12296 | tf_op jit(solution)/shard_map/ppermute | solution.py:317
  14.8 0.0 collective-permute-done.5.corner_ref
  14.8 0.0 collective-permute-done.4.left_ref
  14.8 0.0 collective-permute-done.3.above_ref
  14.8 3.3 %bank.1 = (f32[16,32,128]{2,1,0:T(8,128)S(1)}, f32[520,128]{1,0:T(8,128)S(1)}, f32[136,128]{1,0:T(8,128)S(1)}, f32[136,128]{1,0:T(8,128)S(1)}) custom-call(f32[16,32,128]{2,1,0:T(8,128)S(1)} %get-tuple-element.19.own_ref.refs_0_, f32[16,32,128]{2,1,0:T(8,128)S(1)} %collective-permute-done.3.above_ref, f32[16,8,128]{2,1,0:T(8,128)S(1)} %collective-permute-done.4.left_ref, ...), custom_call_target="tpu_custom_call" | custom-call | tf_op jit(solution)/shard_map/bank/pallas_call | solution.py:401
  18.1 0.0 collective-permute-done.2.arrived_ref
  18.1 3.0 %collective-permute-start.6 = (f32[520,128]{1,0:T(8,128)S(1)}, f32[520,128]{1,0:T(8,128)S(1)}, u32[]{:S(2)}, u32[]{:S(2)}) collective-permute-start(f32[520,128]{1,0:T(8,128)S(1)} %get-tuple-element.33), channel_id=1, source_target_pairs={{0,28},{1,29},{2,30},{3,31},{4,0},{5,1},{6,2},{7,3},{8,4},{9,5},{1... | collective-permute-start | bytes 798728 | tf_op jit(solution)/shard_map/ppermute | solution.py:359
  21.1 1.8 %collective-permute-start.7 = (f32[136,128]{1,0:T(8,128)S(1)}, f32[136,128]{1,0:T(8,128)S(1)}, u32[]{:S(2)}, u32[]{:S(2)}) collective-permute-start(f32[136,128]{1,0:T(8,128)S(1)} %get-tuple-element.34), channel_id=1, source_target_pairs={{0,3},{1,0},{2,1},{3,2},{4,7},{5,4},{6,5},{7,6},{8,11},{9,8},{10,9... | collective-permute-start | bytes 208904 | tf_op jit(solution)/shard_map/ppermute | solution.py:359
  23.0 0.4 %collective-permute-start.8 = (f32[136,128]{1,0:T(8,128)S(1)}, f32[136,128]{1,0:T(8,128)S(1)}, u32[]{:S(2)}, u32[]{:S(2)}) collective-permute-start(f32[136,128]{1,0:T(8,128)S(1)} %get-tuple-element.35), channel_id=1, source_target_pairs={{0,31},{1,28},{2,29},{3,30},{4,3},{5,0},{6,1},{7,2},{8,7},{9,4},{1... | collective-permute-start | bytes 208904 | tf_op jit(solution)/shard_map/ppermute | solution.py:359
  23.4 1.5 %collective-permute-done.7.refs_7_ = f32[136,128]{1,0:T(8,128)S(1)} collective-permute-done((f32[136,128]{1,0:T(8,128)S(1)}, f32[136,128]{1,0:T(8,128)S(1)}, u32[]{:S(2)}, u32[]{:S(2)}) %collective-permute-start.7) | collective-permute-done | bytes 69664 | tf_op jit(solution)/shard_map/ppermute | solution.py:359
  24.9 2.7 %collective-permute-done.8.refs_8_ = f32[136,128]{1,0:T(8,128)S(1)} collective-permute-done((f32[136,128]{1,0:T(8,128)S(1)}, f32[136,128]{1,0:T(8,128)S(1)}, u32[]{:S(2)}, u32[]{:S(2)}) %collective-permute-start.8) | collective-permute-done | bytes 69664 | tf_op jit(solution)/shard_map/ppermute | solution.py:359
  27.6 0.0 collective-permute-done.6.refs_6_
  27.6 1.1 %last.1 = (f32[16,32,128]{2,1,0:T(8,128)}, f32[16,32,128]{2,1,0:T(8,128)}) custom-call(f32[16,32,128]{2,1,0:T(8,128)S(1)} %get-tuple-element.19.own_ref.refs_0_, f32[16,32,128]{2,1,0:T(8,128)S(1)} %get-tuple-element.20.refs_1_, f32[16,32,128]{2,1,0:T(8,128)S(1)} %get-tuple-element.21.refs_2_, f32[4,16,128]{2,1,0:T(8,128)S(1)} %get-tuple-element.23.refs_0_.refs_3_, ...), custom_call_target="tpu_custom_call" | custom-call | tf_op jit(solution)/shard_map/last/pallas_call | solution.py:426
  (3 shorter events, 0.0 us)
Async XLA Ops:
  0.6 14.2 %collective-permute-start.3 = (f32[16,32,128]{2,1,0:T(8,128)}, f32[16,32,128]{2,1,0:T(8,128)S(1)}, u32[]{:S(2)}, u32[]{:S(2)}) collective-permute-start(f32[16,32,128]{2,1,0:T(8,128)} %start_hbm.1), channel_id=1, source_target_pairs={{0,4},{1,5},{2,6},{3,7},{4,8},{5,9},{6,10},{7,11},{8,12},{9,13},{1... | collective-permute-start | bytes 786440 | tf_op jit(solution)/shard_map/ppermute | solution.py:359
  4.7 3.7 %copy-start = (f32[16,4]{0,1:T(4,128)S(1)}, f32[16,4]{0,1:T(4,128)}, u32[]{:S(2)}) copy-start(f32[16,4]{0,1:T(4,128)} %param.11) | copy-start | bytes 772
  4.7 10.1 %collective-permute-start.5 = (f32[16,8,128]{2,1,0:T(8,128)S(1)}, f32[16,8,128]{2,1,0:T(8,128)S(1)}, u32[]{:S(2)}, u32[]{:S(2)}) collective-permute-start(f32[16,8,128]{2,1,0:T(8,128)S(1)} %get-tuple-element.24), channel_id=1, source_target_pairs={{0,5},{1,6},{2,7},{3,4},{4,9},{5,10},{6,11},{7,8},{8,13},{9,14},{1... | collective-permute-start | bytes 196616 | tf_op jit(solution)/shard_map/ppermute | solution.py:359
  5.8 9.1 %collective-permute-start.4 = (f32[16,8,128]{2,1,0:T(8,128)S(1)}, f32[16,8,128]{2,1,0:T(8,128)S(1)}, u32[]{:S(2)}, u32[]{:S(2)}) collective-permute-start(f32[16,8,128]{2,1,0:T(8,128)S(1)} %get-tuple-element.24), channel_id=1, source_target_pairs={{0,1},{1,2},{2,3},{3,0},{4,5},{5,6},{6,7},{7,4},{8,9},{9,10},{10,1... | collective-permute-start | bytes 196616 | tf_op jit(solution)/shard_map/ppermute | solution.py:359
  7.1 1.3 %copy-start.1 = (s32[1,1,2,2]{3,2,1,0:T(2,128)S(1)}, s32[1,1,2,2]{3,2,1,0:T(2,128)}, u32[]{:S(2)}) copy-start(s32[1,1,2,2]{3,2,1,0:T(2,128)} %margin_ref.1) | copy-start | bytes 52
  7.1 4.1 %collective-permute-start = (f32[8,128]{1,0:T(8,128)S(1)}, f32[8,128]{1,0:T(8,128)S(1)}, u32[]{:S(2)}, u32[]{:S(2)}) collective-permute-start(f32[8,128]{1,0:T(8,128)S(1)} %get-tuple-element.22.after_ref.value_ref), channel_id=1, source_target_pairs={{0,2},{1,3},{2,0},{3,1},{4,6},{5,7},{6,4},{7,5},{8,10},{9,11},{10,... | collective-permute-start | bytes 12296 | tf_op jit(solution)/shard_map/ppermute | solution.py:317
  11.1 2.5 %collective-permute-start.1 = (f32[8,128]{1,0:T(8,128)S(1)}, f32[8,128]{1,0:T(8,128)S(1)}, u32[]{:S(2)}, u32[]{:S(2)}) collective-permute-start(f32[8,128]{1,0:T(8,128)S(1)} %add.2.value_ref), channel_id=1, source_target_pairs={{0,8},{4,12},{8,0},{12,4},{16,24},{20,28},{24,16},{28,20},{1,9},{5... | collective-permute-start | bytes 12296 | tf_op jit(solution)/shard_map/ppermute | solution.py:317
  13.6 4.5 %collective-permute-start.2 = (f32[8,128]{1,0:T(8,128)S(1)}, f32[8,128]{1,0:T(8,128)S(1)}, u32[]{:S(2)}, u32[]{:S(2)}) collective-permute-start(f32[8,128]{1,0:T(8,128)S(1)} %add.3.after_ref.value_ref), channel_id=1, source_target_pairs={{0,16},{4,20},{8,24},{12,28},{16,0},{20,4},{24,8},{28,12},{1,17},{... | collective-permute-start | bytes 12296 | tf_op jit(solution)/shard_map/ppermute | solution.py:317
  18.1 9.5 %collective-permute-start.6 = (f32[520,128]{1,0:T(8,128)S(1)}, f32[520,128]{1,0:T(8,128)S(1)}, u32[]{:S(2)}, u32[]{:S(2)}) collective-permute-start(f32[520,128]{1,0:T(8,128)S(1)} %get-tuple-element.33), channel_id=1, source_target_pairs={{0,28},{1,29},{2,30},{3,31},{4,0},{5,1},{6,2},{7,3},{8,4},{9,5},{1... | collective-permute-start | bytes 798728 | tf_op jit(solution)/shard_map/ppermute | solution.py:359
  21.1 3.7 %collective-permute-start.7 = (f32[136,128]{1,0:T(8,128)S(1)}, f32[136,128]{1,0:T(8,128)S(1)}, u32[]{:S(2)}, u32[]{:S(2)}) collective-permute-start(f32[136,128]{1,0:T(8,128)S(1)} %get-tuple-element.34), channel_id=1, source_target_pairs={{0,3},{1,0},{2,1},{3,2},{4,7},{5,4},{6,5},{7,6},{8,11},{9,8},{10,9... | collective-permute-start | bytes 208904 | tf_op jit(solution)/shard_map/ppermute | solution.py:359
  23.0 4.6 %collective-permute-start.8 = (f32[136,128]{1,0:T(8,128)S(1)}, f32[136,128]{1,0:T(8,128)S(1)}, u32[]{:S(2)}, u32[]{:S(2)}) collective-permute-start(f32[136,128]{1,0:T(8,128)S(1)} %get-tuple-element.35), channel_id=1, source_target_pairs={{0,31},{1,28},{2,29},{3,30},{4,3},{5,0},{6,1},{7,2},{8,7},{9,4},{1... | collective-permute-start | bytes 208904 | tf_op jit(solution)/shard_map/ppermute | solution.py:359

commit v4 on v3

--- a/solution.py
+++ b/solution.py
@@ -136,28 +136,13 @@
             for q in range(rows // 8):
                 total = total + square[8 * q : 8 * q + 8]
             pack_ref[c] = pack_rows(field, cols - BORDER)
-    energy_ref[...] = total
+    energy_ref[:8] = total
 
 
 def prepare_kernel(
-    margin_ref, seed_ref, after_ref, rows_hbm, rows_t_hbm, cols_hbm,
-    basis_ref, a_ref, at_ref, g_ref, rows_ref, rows_t_ref, cols_ref, sems,
+    margin_ref, seed_ref, after_ref, rows_ref, rows_t_ref, cols_ref,
+    basis_ref, a_ref, at_ref, g_ref,
 ):
-    copies = [
-        pltpu.make_async_copy(rows_hbm, rows_ref, sems.at[0]),
-        pltpu.make_async_copy(rows_t_hbm, rows_t_ref, sems.at[1]),
-    ]
-    for level in range(LEVELS):
-        for k in range(2):
-            span = pl.ds(k * (cols_ref.shape[1] // 2), cols_ref.shape[1] // 2)
-            copies.append(
-                pltpu.make_async_copy(
-                    cols_hbm.at[level, span], cols_ref.at[level, span], sems.at[2 + 2 * level + k]
-                )
-            )
-    for copy in copies:
-        copy.start()
-
     rank, channels = seed_ref.shape
     eye = row_iota((channels, channels)) == lane_iota((channels, channels))
     columns = []
@@ -173,8 +158,6 @@
             along = jnp.sum(vector * columns[later], axis=0, keepdims=True)
             columns[later] = columns[later] - along * vector
 
-    for copy in copies:
-        copy.wait()
     half, tall = rows_ref.shape[0] // LEVELS, rows_ref.shape[1]
     wide, double = cols_ref.shape[1:]
     cols = double // 2
@@ -206,15 +189,10 @@
     return lax.dot_general(a, b, (((1,), (1,)), ((), ())), preferred_element_type=jnp.float32)
 
 
-def bank_kernel(
-    own_ref, above_ref, left_ref, corner_ref, a_ref, at_ref, g_ref, after_ref,
-    own_out, above_out, left_out, corner_out, z_high, z_low, u_high, u_low,
-):
+def rows_kernel(own_ref, above_ref, left_ref, corner_ref, a_ref, after_ref, z_high, z_low):
     channels, rows, cols = own_ref.shape
     groups = rows // 8
-    wide = cols + LANES
     half = 2 * rows
-
     for c in range(channels):
         upper = jnp.concatenate([above_ref[c], unpack_rows(corner_ref[c], 0, groups)], axis=1)
         lower = jnp.concatenate([own_ref[c], unpack_rows(left_ref[c], 0, groups)], axis=1)
@@ -225,24 +203,34 @@
             z_high[level, c] = part_high[level * half : (level + 1) * half]
             z_low[level, c] = part_low[level * half : (level + 1) * half]
 
+def bank_kernel(
+    z_high, z_low, at_ref, g_ref, own_out, above_out, left_out, corner_out, u_high, u_low,
+):
+    channels, rows, cols = own_out.shape
+    wide = cols + LANES
+    half = 2 * rows
+    size = channels // 4
+
     low_rows = row_iota((half, 2 * cols)) < rows
     low_cols = lane_iota((half, 2 * cols)) < cols
     bound = jnp.where(low_rows & low_cols, 0.0, CLIP_LEVEL / BAND_STEP)
-    bound = jnp.broadcast_to(bound[None], (channels, half, 2 * cols)).reshape(channels * half, 2 * cols)
     for level in range(LEVELS):
-        zh = z_high[level].reshape(channels * half, wide)
-        zl = z_low[level].reshape(channels * half, wide)
         g_high, g_low = g_ref[level, 0], g_ref[level, 1]
-        coef = dot(jnp.concatenate([zh, zl, zh], axis=1), jnp.concatenate([g_high, g_high, g_low], axis=0))
-        coef = jnp.minimum(jnp.maximum(coef, -bound), bound)
-        t_high, t_low = terms(coef)
-        u = dot_t(
-            jnp.concatenate([t_high, t_low, t_high], axis=1),
-            jnp.concatenate([g_high, g_high, g_low], axis=1),
-        )
-        part_high, part_low = terms(u)
-        u_high[level] = part_high.reshape(channels, half, wide)
-        u_low[level] = part_low.reshape(channels, half, wide)
+        for start in range(0, channels, size):
+            span = slice(start, start + size)
+            zh = z_high[level, span].reshape(size * half, wide)
+            zl = z_low[level, span].reshape(size * half, wide)
+            coef = dot(jnp.concatenate([zh, zl, zh], axis=1), jnp.concatenate([g_high, g_high, g_low], axis=0))
+            coef = coef.reshape(size, half, 2 * cols)
+            coef = jnp.minimum(jnp.maximum(coef, -bound), bound).reshape(size * half, 2 * cols)
+            t_high, t_low = terms(coef)
+            u = dot_t(
+                jnp.concatenate([t_high, t_low, t_high], axis=1),
+                jnp.concatenate([g_high, g_high, g_low], axis=1),
+            )
+            part_high, part_low = terms(u)
+            u_high[level, span] = part_high.reshape(size, half, wide)
+            u_low[level, span] = part_low.reshape(size, half, wide)
 
     for c in range(channels):
         highs = [u_high[level, c] for level in range(LEVELS)]
@@ -299,12 +287,12 @@
 
 
 def add_kernel(value_ref, arrived_ref, *refs):
-    refs[-1][...] = value_ref[...] + arrived_ref[...]
+    refs[-1][...] = value_ref[:8] + arrived_ref[:8]
 
 
 def doubling():
     rounds = []
-    for axis in ("fx", "fy"):
+    for axis in ("fy", "fx"):
         step = 2
         while step < lax.axis_size(axis):
             rounds.append((axis, step))
@@ -327,7 +315,7 @@
 def added(value, arrived, *after):
     return pl.pallas_call(
         add_kernel,
-        out_shape=jax.ShapeDtypeStruct(value.shape, value.dtype),
+        out_shape=jax.ShapeDtypeStruct((8, value.shape[1]), value.dtype),
         in_specs=[pl.BlockSpec(memory_space=pltpu.VMEM)] * 2 + [pl.BlockSpec(memory_space=pl.ANY)] * len(after),
         out_specs=pl.BlockSpec(memory_space=pltpu.VMEM),
         compiler_params=pltpu.CompilerParams(vmem_limit_bytes=1024 * 1024),
@@ -346,7 +334,7 @@
     f32, bf16 = jnp.float32, jnp.bfloat16
     image_shape = jax.ShapeDtypeStruct((channels, rows, cols), f32)
     pack_shape = jax.ShapeDtypeStruct((channels, 8, LANES), f32)
-    params = pltpu.CompilerParams(vmem_limit_bytes=24 * 1024 * 1024)
+    params = pltpu.CompilerParams(vmem_limit_bytes=16 * 1024 * 1024)
     vmem = pl.BlockSpec(memory_space=pltpu.VMEM)
     smem = pl.BlockSpec(memory_space=pltpu.SMEM)
     hbm = pl.BlockSpec(memory_space=pltpu.HBM)
@@ -361,7 +349,7 @@
     above = moved(start_image, (1, 0))
     energy, pack, own, gain, shifted = pl.pallas_call(
         first_kernel,
-        out_shape=(jax.ShapeDtypeStruct((8, cols), f32), pack_shape, image_shape, image_shape, image_shape),
+        out_shape=(jax.ShapeDtypeStruct((128, cols), f32), pack_shape, image_shape, image_shape, image_shape),
         in_specs=[hbm] * 3,
         out_specs=(vmem,) * 5,
         scratch_shapes=[pltpu.VMEM((channels, rows, cols), f32), pltpu.SemaphoreType.DMA((4, 3))],
@@ -370,6 +358,9 @@
     )(kept(start_image), kept(dirty), kept(sampling))
     left = moved(pack, (0, 1))
     corner = moved(pack, (1, 1))
+
+    rounds = doubling()
+    energy = added(energy, partner(energy, rounds[0]))
 
     table = row_table(rows)
     table_t = np.ascontiguousarray(table.reshape(LEVELS, half, tall).transpose(0, 2, 1))
@@ -381,32 +372,35 @@
             jax.ShapeDtypeStruct((tall, 3 * LEVELS * half), bf16),
             jax.ShapeDtypeStruct((LEVELS, 2, wide, 2 * cols), bf16),
         ),
-        in_specs=[smem, vmem, anywhere, hbm, hbm, hbm],
+        in_specs=[smem, vmem, anywhere, vmem, vmem, vmem],
         out_specs=(vmem,) * 4,
-        scratch_shapes=[
-            pltpu.VMEM((LEVELS * half, tall), f32),
-            pltpu.VMEM((LEVELS, tall, half), f32),
-            pltpu.VMEM((LEVELS, wide, 2 * cols), f32),
-            pltpu.SemaphoreType.DMA((2 + 2 * LEVELS,)),
-        ],
         compiler_params=params,
         name="prepare",
-    )(margin, basis_seed.T, energy, kept(jnp.asarray(table)), kept(jnp.asarray(table_t)), kept(jnp.asarray(col_table(cols))))
-    rounds = doubling()
-    for round_ in rounds[:-1]:
+    )(margin, basis_seed.T, energy, table, table_t, col_table(cols))
+    for round_ in rounds[1:-1]:
         energy = added(energy, partner(energy, round_), basis)
+    arriving = partner(energy, rounds[-1])
+    bank_shape = jax.ShapeDtypeStruct((LEVELS, channels, half, wide), bf16)
+    z_high, z_low = pl.pallas_call(
+        rows_kernel,
+        out_shape=(bank_shape, bank_shape),
+        in_specs=[vmem] * 5 + [anywhere],
+        out_specs=(vmem,) * 2,
+        compiler_params=params,
+        name="rows",
+    )(own, above, left, corner, a, energy)
 
     above_shape = jax.ShapeDtypeStruct((channels * BORDER + 8, cols), f32)
     strip_shape = jax.ShapeDtypeStruct((channels * 8 + 8, LANES), f32)
     own_part, *parts = pl.pallas_call(
         bank_kernel,
         out_shape=(image_shape, above_shape, strip_shape, strip_shape),
-        in_specs=[vmem] * 7 + [anywhere],
+        in_specs=[vmem] * 4,
         out_specs=(vmem,) * 4,
-        scratch_shapes=[pltpu.VMEM((LEVELS, channels, half, wide), bf16) for i in range(4)],
+        scratch_shapes=[pltpu.VMEM(bank_shape.shape, bf16)] * 2,
         compiler_params=params,
         name="bank",
-    )(own, above, left, corner, a, a_t, g, energy)
+    )(z_high, z_low, a_t, g)
     energy, *parts = pl.pallas_call(
         stamp_kernel,
         out_shape=(jax.ShapeDtypeStruct(energy.shape, f32), above_shape, strip_shape, strip_shape),
@@ -415,7 +409,7 @@
         input_output_aliases={2: 1, 3: 2, 4: 3},
         compiler_params=pltpu.CompilerParams(vmem_limit_bytes=1024 * 1024),
         name="stamp",
-    )(energy, partner(energy, rounds[-1]), *parts)
+    )(energy, arriving, *parts)
     below = moved(parts[0], (-1, 0))
     right = moved(parts[1], (0, -1))
     corner_back = moved(parts[2], (-1, -1))

time: 28.9 us -> 26.7 us (0.924)
  starting transfers between devices: 13.8 us -> 11.3 us
  Pallas kernels: 7.68 us -> 6.32 us
  waiting for transfers between devices: 6.54 us -> 7.34 us
  local copies, waits for them, and re-layouts: 0.01 us -> 0.6 us
    ppermute x6, starting transfers between devices: 10.3 us -> 8.29 us  [moved(): return lax.ppermute(value, ('fy', 'fx'), shift(sizes, steps))]
    ppermute x3, waiting for transfers between devices: 2.29 us -> 3.6 us  [partner(): lax.ppermute(value, axis, [(i, i ^ step) for i in range(lax.axis_size(axi...]
    pallas_call x1, Pallas kernels: 1.95 us -> 0.78 us  [per_device(): pl.pallas_call(prepare_kernel, out_shape=(jax.ShapeDtypeStruct((rank, cha...]
    pallas_call x1, Pallas kernels: 3.29 us -> 2.57 us  [per_device(): pl.pallas_call(bank_kernel, out_shape=(image_shape, above_shape, strip_sh...]
    unnamed x4 -> x10, local copies, waits for them, and re-layouts: 0.01 us -> 0.6 us
    pallas_call x3 -> x4, Pallas kernels: 1.37 us -> 1.9 us  [the longest x1 1.37 us: per_device(): pl.pallas_call(first_kernel, out_shape=(jax.ShapeDtypeStruct((128, cols),...]
    ppermute x6, waiting for transfers between devices: 4.24 us -> 3.73 us  [moved(): return lax.ppermute(value, ('fy', 'fx'), shift(sizes, steps))]
    ppermute x3, starting transfers between devices: 3.5 us -> 3.05 us  [partner(): lax.ppermute(value, axis, [(i, i ^ step) for i in range(lax.axis_size(axi...]
  transfers between devices with their start and end apart: 9 -> 9, of which waited for: 4 -> 4; matrix products, arithmetic and copies ran while one was open for 0% -> 0% of each run, Pallas kernels for 23% -> 20%
where the time goes in v4:
time: 26.7 us; the launch traced here: 26.3 us
  starting transfers between devices  11.3 us (42%)
  waiting for transfers between devices  7.34 us (27%)
  Pallas kernels  6.32 us (24%)
  between operations  0.72 us (3%)
  local copies, waits for them, and re-layouts  0.6 us (2%)
    ppermute x6, starting transfers between devices, moved(): return lax.ppermute(value, ('fy', 'fx'), shift(sizes, steps))  8.29 us
    ppermute x6, waiting for transfers between devices, moved(): return lax.ppermute(value, ('fy', 'fx'), shift(sizes, steps))  3.73 us
    ppermute x3, waiting for transfers between devices, partner(): lax.ppermute(value, axis, [(i, i ^ step) for i in range(lax.axis_size(axi...  3.6 us
    ppermute x3, starting transfers between devices, partner(): lax.ppermute(value, axis, [(i, i ^ step) for i in range(lax.axis_size(axi...  3.05 us
    pallas_call x1, Pallas kernels, per_device(): pl.pallas_call(bank_kernel, out_shape=(image_shape, above_shape, strip_sh...  2.57 us
    pallas_call x1, Pallas kernels, per_device(): pl.pallas_call(first_kernel, out_shape=(jax.ShapeDtypeStruct((128, cols),...  1.37 us
    pallas_call x1, Pallas kernels, per_device(): pl.pallas_call(last, out_shape=(image_shape, image_shape), in_specs=[vmem...  1.06 us
    pallas_call x1, Pallas kernels, per_device(): pl.pallas_call(prepare_kernel, out_shape=(jax.ShapeDtypeStruct((rank, cha...  0.78 us
  transfers between devices with their start and end apart: 9, of which 4 were waited for; matrix products, arithmetic and copies ran while one was open for 0% of the time, Pallas kernels for 20%

profile of v4, /device:TPU:1, one launch (start us, length us, event | category | flops | bytes accessed | tf_op | source)
XLA Modules:
  0.0 26.3 jit_solution(18388960112405389638)
XLA Ops:
  0.6 0.0 copy-start
  0.6 2.7 %collective-permute-start.3 = (f32[16,32,128]{2,1,0:T(8,128)}, f32[16,32,128]{2,1,0:T(8,128)S(1)}, u32[]{:S(2)}, u32[]{:S(2)}) collective-permute-start(f32[16,32,128]{2,1,0:T(8,128)} %start_hbm.1), channel_id=1, source_target_pairs={{0,4},{1,5},{2,6},{3,7},{4,8},{5,9},{6,10},{7,11},{8,12},{9,13},{1... | collective-permute-start | bytes 786440 | tf_op jit(solution)/shard_map/ppermute | solution.py:347
  3.3 1.4 %first.1 = (f32[128,128]{1,0:T(8,128)S(1)}, f32[16,8,128]{2,1,0:T(8,128)S(1)}, f32[16,32,128]{2,1,0:T(8,128)S(1)}, f32[16,32,128]{2,1,0:T(8,128)S(1)}, f32[16,32,128]{2,1,0:T(8,128)S(1)}) custom-call(f32[16,32,128]{2,1,0:T(8,128)} %start_hbm.1, f32[16,32,128]{2,1,0:T(8,128)} %dirty_hbm.1, f32[16,32,128]{2,1,0:T(8,128)} %sampling_hbm.1), custom_call_target="tpu_custom_call" | custom-call | tf_op jit(solution)/shard_map/first/pallas_call | solution.py:350
  4.7 1.3 %collective-permute-start = (f32[128,128]{1,0:T(8,128)S(1)}, f32[128,128]{1,0:T(8,128)S(1)}, u32[]{:S(2)}, u32[]{:S(2)}) collective-permute-start(f32[128,128]{1,0:T(8,128)S(1)} %get-tuple-element.24.value_ref), channel_id=1, source_target_pairs={{0,8},{4,12},{8,0},{12,4},{16,24},{20,28},{24,16},{28,20},{1,9},{5... | collective-permute-start | bytes 196616 | tf_op jit(solution)/shard_map/ppermute | solution.py:305
  5.9 0.0 copy-start.1
  5.9 0.0 copy-start.2
  6.0 1.3 %collective-permute-start.4 = (f32[16,8,128]{2,1,0:T(8,128)S(1)}, f32[16,8,128]{2,1,0:T(8,128)S(1)}, u32[]{:S(2)}, u32[]{:S(2)}) collective-permute-start(f32[16,8,128]{2,1,0:T(8,128)S(1)} %get-tuple-element.26), channel_id=1, source_target_pairs={{0,1},{1,2},{2,3},{3,0},{4,5},{5,6},{6,7},{7,4},{8,9},{9,10},{10,1... | collective-permute-start | bytes 196616 | tf_op jit(solution)/shard_map/ppermute | solution.py:347
  7.2 0.7 %collective-permute-start.5 = (f32[16,8,128]{2,1,0:T(8,128)S(1)}, f32[16,8,128]{2,1,0:T(8,128)S(1)}, u32[]{:S(2)}, u32[]{:S(2)}) collective-permute-start(f32[16,8,128]{2,1,0:T(8,128)S(1)} %get-tuple-element.26), channel_id=1, source_target_pairs={{0,5},{1,6},{2,7},{3,4},{4,9},{5,10},{6,11},{7,8},{8,13},{9,14},{1... | collective-permute-start | bytes 196616 | tf_op jit(solution)/shard_map/ppermute | solution.py:347
  7.9 2.2 %collective-permute-done.arrived_ref = f32[128,128]{1,0:T(8,128)S(1)} collective-permute-done((f32[128,128]{1,0:T(8,128)S(1)}, f32[128,128]{1,0:T(8,128)S(1)}, u32[]{:S(2)}, u32[]{:S(2)}) %collective-permute-start) | collective-permute-done | bytes 65568 | tf_op jit(solution)/shard_map/ppermute | solution.py:305
  10.2 0.0 copy-start.3
  10.2 0.1 collective-permute-start.1
  10.3 0.0 copy-done
  10.3 0.0 copy-done.1
  10.3 0.0 copy-done.2
  10.3 0.6 %copy-done.3 = f32[16,4]{0,1:T(4,128)S(1)} copy-done((f32[16,4]{0,1:T(4,128)S(1)}, f32[16,4]{0,1:T(4,128)}, u32[]{:S(2)}) %copy-start.3) | copy-done | bytes 280
  10.9 0.0 copy-done.4
  10.9 0.8 %prepare.1 = (f32[4,16,128]{2,1,0:T(8,128)S(1)}, bf16[128,192]{1,0:T(8,128)(2,1)S(1)}, bf16[64,384]{1,0:T(8,128)(2,1)S(1)}, bf16[2,2,256,256]{3,2,1,0:T(8,128)(2,1)S(1)}) custom-call(s32[1,1,2,2]{3,2,1,0:T(2,128)S(1)} %copy-done.4, f32[4,16]{1,0:T(4,128)S(1)} %bitcast.1, f32[8,128]{1,0:T(8,128)S(1)} %add.2.after_ref.value_ref, f32[128,64]{1,0:T(8,128)S(1)} %copy-done.1, ...), custom_call_target="tpu_custom_call" | custom-call | tf_op jit(solution)/shard_map/prepare/pallas_call | solution.py:367
  11.7 1.4 %collective-permute-done.1.arrived_ref = f32[8,128]{1,0:T(8,128)S(1)} collective-permute-done((f32[8,128]{1,0:T(8,128)S(1)}, f32[8,128]{1,0:T(8,128)S(1)}, u32[]{:S(2)}, u32[]{:S(2)}) %collective-permute-start.1) | collective-permute-done | bytes 4128 | tf_op jit(solution)/shard_map/ppermute | solution.py:305
  13.0 1.7 %collective-permute-start.2 = (f32[8,128]{1,0:T(8,128)S(1)}, f32[8,128]{1,0:T(8,128)S(1)}, u32[]{:S(2)}, u32[]{:S(2)}) collective-permute-start(f32[8,128]{1,0:T(8,128)S(1)} %add.3.after_ref.value_ref), channel_id=1, source_target_pairs={{0,2},{1,3},{2,0},{3,1},{4,6},{5,7},{6,4},{7,5},{8,10},{9,11},{10,... | collective-permute-start | bytes 12296 | tf_op jit(solution)/shard_map/ppermute | solution.py:305
  14.7 0.0 collective-permute-done.4.left_ref
  14.7 0.0 collective-permute-done.5.corner_ref
  14.7 0.0 collective-permute-done.3.above_ref
  14.7 0.5 %rows.1 = (bf16[2,16,64,256]{3,2,1,0:T(8,128)(2,1)S(1)}, bf16[2,16,64,256]{3,2,1,0:T(8,128)(2,1)S(1)}) custom-call(f32[16,32,128]{2,1,0:T(8,128)S(1)} %get-tuple-element.21.own_ref.refs_0_, f32[16,32,128]{2,1,0:T(8,128)S(1)} %collective-permute-done.3.above_ref, f32[16,8,128]{2,1,0:T(8,128)S(1)} %collective-permute-done.4.left_ref, ...), custom_call_target="tpu_custom_call" | custom-call | tf_op jit(solution)/shard_map/rows/pallas_call | solution.py:384
  15.3 2.6 %bank.1 = (f32[16,32,128]{2,1,0:T(8,128)S(1)}, f32[520,128]{1,0:T(8,128)S(1)}, f32[136,128]{1,0:T(8,128)S(1)}, f32[136,128]{1,0:T(8,128)S(1)}) custom-call(bf16[2,16,64,256]{3,2,1,0:T(8,128)(2,1)S(1)} %get-tuple-element.28.z_high, bf16[2,16,64,256]{3,2,1,0:T(8,128)(2,1)S(1)} %get-tuple-element.29.z_low, bf16[64,384]{1,0:T(8,128)(2,1)S(1)} %get-tuple-element.30.at_ref, ...), custom_call_target="tpu_custom_call" | custom-call | tf_op jit(solution)/shard_map/bank/pallas_call | solution.py:395
  17.8 0.0 collective-permute-done.2.arrived_ref
  17.9 0.3 %collective-permute-start.6 = (f32[520,128]{1,0:T(8,128)S(1)}, f32[520,128]{1,0:T(8,128)S(1)}, u32[]{:S(2)}, u32[]{:S(2)}) collective-permute-start(f32[520,128]{1,0:T(8,128)S(1)} %get-tuple-element.37), channel_id=1, source_target_pairs={{0,28},{1,29},{2,30},{3,31},{4,0},{5,1},{6,2},{7,3},{8,4},{9,5},{1... | collective-permute-start | bytes 798728 | tf_op jit(solution)/shard_map/ppermute | solution.py:347
  18.1 2.2 %collective-permute-start.7 = (f32[136,128]{1,0:T(8,128)S(1)}, f32[136,128]{1,0:T(8,128)S(1)}, u32[]{:S(2)}, u32[]{:S(2)}) collective-permute-start(f32[136,128]{1,0:T(8,128)S(1)} %get-tuple-element.38), channel_id=1, source_target_pairs={{0,3},{1,0},{2,1},{3,2},{4,7},{5,4},{6,5},{7,6},{8,11},{9,8},{10,9... | collective-permute-start | bytes 208904 | tf_op jit(solution)/shard_map/ppermute | solution.py:347
  20.4 1.1 %collective-permute-start.8 = (f32[136,128]{1,0:T(8,128)S(1)}, f32[136,128]{1,0:T(8,128)S(1)}, u32[]{:S(2)}, u32[]{:S(2)}) collective-permute-start(f32[136,128]{1,0:T(8,128)S(1)} %get-tuple-element.39), channel_id=1, source_target_pairs={{0,31},{1,28},{2,29},{3,30},{4,3},{5,0},{6,1},{7,2},{8,7},{9,4},{1... | collective-permute-start | bytes 208904 | tf_op jit(solution)/shard_map/ppermute | solution.py:347
  21.5 0.2 collective-permute-done.7.refs_7_
  21.7 3.5 %collective-permute-done.8.refs_8_ = f32[136,128]{1,0:T(8,128)S(1)} collective-permute-done((f32[136,128]{1,0:T(8,128)S(1)}, f32[136,128]{1,0:T(8,128)S(1)}, u32[]{:S(2)}, u32[]{:S(2)}) %collective-permute-start.8) | collective-permute-done | bytes 69664 | tf_op jit(solution)/shard_map/ppermute | solution.py:347
  25.2 0.0 collective-permute-done.6.refs_6_
  25.2 1.1 %last.1 = (f32[16,32,128]{2,1,0:T(8,128)}, f32[16,32,128]{2,1,0:T(8,128)}) custom-call(f32[16,32,128]{2,1,0:T(8,128)S(1)} %get-tuple-element.21.own_ref.refs_0_, f32[16,32,128]{2,1,0:T(8,128)S(1)} %get-tuple-element.22.refs_1_, f32[16,32,128]{2,1,0:T(8,128)S(1)} %get-tuple-element.23.refs_2_, f32[4,16,128]{2,1,0:T(8,128)S(1)} %get-tuple-element.25.refs_0_.refs_3_, ...), custom_call_target="tpu_custom_call" | custom-call | tf_op jit(solution)/shard_map/last/pallas_call | solution.py:420
  (4 shorter events, 0.0 us)
Async XLA Ops:
  0.6 9.6 %copy-start = (f32[2,256,256]{2,1,0:T(8,128)S(1)}, f32[2,256,256]{2,1,0:T(8,128)}, u32[]{:S(2)}) copy-start(f32[2,256,256]{2,1,0:T(8,128)} %constant.8.clone.cols_ref) | copy-start | bytes 1572868
  0.6 14.1 %collective-permute-start.3 = (f32[16,32,128]{2,1,0:T(8,128)}, f32[16,32,128]{2,1,0:T(8,128)S(1)}, u32[]{:S(2)}, u32[]{:S(2)}) collective-permute-start(f32[16,32,128]{2,1,0:T(8,128)} %start_hbm.1), channel_id=1, source_target_pairs={{0,4},{1,5},{2,6},{3,7},{4,8},{5,9},{6,10},{7,11},{8,12},{9,13},{1... | collective-permute-start | bytes 786440 | tf_op jit(solution)/shard_map/ppermute | solution.py:347
  4.7 5.5 %collective-permute-start = (f32[128,128]{1,0:T(8,128)S(1)}, f32[128,128]{1,0:T(8,128)S(1)}, u32[]{:S(2)}, u32[]{:S(2)}) collective-permute-start(f32[128,128]{1,0:T(8,128)S(1)} %get-tuple-element.24.value_ref), channel_id=1, source_target_pairs={{0,8},{4,12},{8,0},{12,4},{16,24},{20,28},{24,16},{28,20},{1,9},{5... | collective-permute-start | bytes 196616 | tf_op jit(solution)/shard_map/ppermute | solution.py:305
  5.9 4.3 %copy-start.1 = (f32[128,64]{1,0:T(8,128)S(1)}, f32[128,64]{1,0:T(8,128)}, u32[]{:S(2)}) copy-start(f32[128,64]{1,0:T(8,128)} %constant.6.clone.rows_ref) | copy-start | bytes 98308
  5.9 4.3 %copy-start.2 = (f32[2,64,64]{2,1,0:T(8,128)S(1)}, f32[2,64,64]{2,1,0:T(8,128)}, u32[]{:S(2)}) copy-start(f32[2,64,64]{2,1,0:T(8,128)} %constant.7.clone.rows_t_ref) | copy-start | bytes 98308
  6.0 8.8 %collective-permute-start.4 = (f32[16,8,128]{2,1,0:T(8,128)S(1)}, f32[16,8,128]{2,1,0:T(8,128)S(1)}, u32[]{:S(2)}, u32[]{:S(2)}) collective-permute-start(f32[16,8,128]{2,1,0:T(8,128)S(1)} %get-tuple-element.26), channel_id=1, source_target_pairs={{0,1},{1,2},{2,3},{3,0},{4,5},{5,6},{6,7},{7,4},{8,9},{9,10},{10,1... | collective-permute-start | bytes 196616 | tf_op jit(solution)/shard_map/ppermute | solution.py:347
  7.2 7.5 %collective-permute-start.5 = (f32[16,8,128]{2,1,0:T(8,128)S(1)}, f32[16,8,128]{2,1,0:T(8,128)S(1)}, u32[]{:S(2)}, u32[]{:S(2)}) collective-permute-start(f32[16,8,128]{2,1,0:T(8,128)S(1)} %get-tuple-element.26), channel_id=1, source_target_pairs={{0,5},{1,6},{2,7},{3,4},{4,9},{5,10},{6,11},{7,8},{8,13},{9,14},{1... | collective-permute-start | bytes 196616 | tf_op jit(solution)/shard_map/ppermute | solution.py:347
  10.2 0.7 %copy-start.3 = (f32[16,4]{0,1:T(4,128)S(1)}, f32[16,4]{0,1:T(4,128)}, u32[]{:S(2)}) copy-start(f32[16,4]{0,1:T(4,128)} %param.11) | copy-start | bytes 772
  10.2 0.7 %copy-start.4 = (s32[1,1,2,2]{3,2,1,0:T(2,128)S(1)}, s32[1,1,2,2]{3,2,1,0:T(2,128)}, u32[]{:S(2)}) copy-start(s32[1,1,2,2]{3,2,1,0:T(2,128)} %margin_ref.1) | copy-start | bytes 52
  10.2 2.8 %collective-permute-start.1 = (f32[8,128]{1,0:T(8,128)S(1)}, f32[8,128]{1,0:T(8,128)S(1)}, u32[]{:S(2)}, u32[]{:S(2)}) collective-permute-start(f32[8,128]{1,0:T(8,128)S(1)} %add.2.after_ref.value_ref), channel_id=1, source_target_pairs={{0,16},{4,20},{8,24},{12,28},{16,0},{20,4},{24,8},{28,12},{1,17},{... | collective-permute-start | bytes 12296 | tf_op jit(solution)/shard_map/ppermute | solution.py:305
  13.0 4.8 %collective-permute-start.2 = (f32[8,128]{1,0:T(8,128)S(1)}, f32[8,128]{1,0:T(8,128)S(1)}, u32[]{:S(2)}, u32[]{:S(2)}) collective-permute-start(f32[8,128]{1,0:T(8,128)S(1)} %add.3.after_ref.value_ref), channel_id=1, source_target_pairs={{0,2},{1,3},{2,0},{3,1},{4,6},{5,7},{6,4},{7,5},{8,10},{9,11},{10,... | collective-permute-start | bytes 12296 | tf_op jit(solution)/shard_map/ppermute | solution.py:305
  17.9 7.4 %collective-permute-start.6 = (f32[520,128]{1,0:T(8,128)S(1)}, f32[520,128]{1,0:T(8,128)S(1)}, u32[]{:S(2)}, u32[]{:S(2)}) collective-permute-start(f32[520,128]{1,0:T(8,128)S(1)} %get-tuple-element.37), channel_id=1, source_target_pairs={{0,28},{1,29},{2,30},{3,31},{4,0},{5,1},{6,2},{7,3},{8,4},{9,5},{1... | collective-permute-start | bytes 798728 | tf_op jit(solution)/shard_map/ppermute | solution.py:347
  18.1 3.6 %collective-permute-start.7 = (f32[136,128]{1,0:T(8,128)S(1)}, f32[136,128]{1,0:T(8,128)S(1)}, u32[]{:S(2)}, u32[]{:S(2)}) collective-permute-start(f32[136,128]{1,0:T(8,128)S(1)} %get-tuple-element.38), channel_id=1, source_target_pairs={{0,3},{1,0},{2,1},{3,2},{4,7},{5,4},{6,5},{7,6},{8,11},{9,8},{10,9... | collective-permute-start | bytes 208904 | tf_op jit(solution)/shard_map/ppermute | solution.py:347
  20.4 4.9 %collective-permute-start.8 = (f32[136,128]{1,0:T(8,128)S(1)}, f32[136,128]{1,0:T(8,128)S(1)}, u32[]{:S(2)}, u32[]{:S(2)}) collective-permute-start(f32[136,128]{1,0:T(8,128)S(1)} %get-tuple-element.39), channel_id=1, source_target_pairs={{0,31},{1,28},{2,29},{3,30},{4,3},{5,0},{6,1},{7,2},{8,7},{9,4},{1... | collective-permute-start | bytes 208904 | tf_op jit(solution)/shard_map/ppermute | solution.py:347

commit v5 on v4

--- a/solution.py
+++ b/solution.py
@@ -242,11 +242,27 @@
         left_out[8 * c : 8 * (c + 1)] = pack_rows(back[BORDER:, cols:], 0)
 
 
+def begin_kernel(own_ref, shifted_ref, gain_ref, basis_ref, part_ref, after_ref, plain_ref, scaled_ref):
+    channels, rows, cols = own_ref.shape
+    rank = basis_ref.shape[0]
+    plain = [jnp.zeros((rows, cols), jnp.float32) for r in range(rank)]
+    scaled = [jnp.zeros((rows, cols), jnp.float32) for r in range(rank)]
+    for c in range(channels):
+        first = own_ref[c] - (PRIMAL_STEP * WEIGHT * BAND_STEP) * part_ref[c]
+        second = PRIMAL_STEP * gain_ref[c] * shifted_ref[c]
+        for r in range(rank):
+            plain[r] = plain[r] + basis_ref[r, c : c + 1, :] * first
+            scaled[r] = scaled[r] + basis_ref[r, c : c + 1, :] * second
+    for r in range(rank):
+        plain_ref[r] = plain[r]
+        scaled_ref[r] = scaled[r]
+
+
 def last_kernel(
-    radius, start_ref, shifted_ref, sampling_ref, basis_ref, energy_ref, own_ref, below_ref, right_ref, corner_ref,
+    radius, shifted_ref, basis_ref, energy_ref, plain_ref, scaled_ref, below_ref, right_ref, corner_ref,
     image_ref, dual_ref,
 ):
-    channels, rows, cols = start_ref.shape
+    channels, rows, cols = shifted_ref.shape
     rank = basis_ref.shape[0]
     groups = rows // 8
     energy = energy_ref[...]
@@ -258,16 +274,14 @@
     edge = lane_iota((rows, cols)) >= cols - BORDER
     weights = [jnp.zeros((rows, cols), jnp.float32) for r in range(rank)]
     for c in range(channels):
-        field = start_ref[c]
-        gain = sampling_ref[c]
-        dual = factor * shifted_ref[c]
-        dual_ref[c] = dual
+        dual_ref[c] = factor * shifted_ref[c]
         strip = right_ref[8 * c : 8 * (c + 1)] + corner_ref[8 * c : 8 * (c + 1)]
         strip = unpack_rows(strip, cols - BORDER, groups)
-        prior = own_ref[c] + below_ref[BORDER * c : BORDER * (c + 1)] + jnp.where(edge, strip, 0.0)
-        stepped = field - PRIMAL_STEP * (gain * dual + (WEIGHT * BAND_STEP) * prior)
+        prior = below_ref[BORDER * c : BORDER * (c + 1)] + jnp.where(edge, strip, 0.0)
         for r in range(rank):
-            weights[r] = weights[r] + basis_ref[r, c : c + 1, :] * stepped
+            weights[r] = weights[r] + basis_ref[r, c : c + 1, :] * prior
+    for r in range(rank):
+        weights[r] = (plain_ref[r] - factor * scaled_ref[r]) - (PRIMAL_STEP * WEIGHT * BAND_STEP) * weights[r]
     for c in range(channels):
         total = basis_ref[0, c : c + 1, :] * weights[0]
         for r in range(1, rank):
@@ -352,7 +366,7 @@
         out_shape=(jax.ShapeDtypeStruct((128, cols), f32), pack_shape, image_shape, image_shape, image_shape),
         in_specs=[hbm] * 3,
         out_specs=(vmem,) * 5,
-        scratch_shapes=[pltpu.VMEM((channels, rows, cols), f32), pltpu.SemaphoreType.DMA((4, 3))],
+        scratch_shapes=[pltpu.VMEM((channels, rows, cols), f32), pltpu.SemaphoreType.DMA((1, 3))],
         compiler_params=params,
         name="first",
     )(kept(start_image), kept(dirty), kept(sampling))
@@ -414,16 +428,26 @@
     right = moved(parts[1], (0, -1))
     corner_back = moved(parts[2], (-1, -1))
 
+    weight_shape = jax.ShapeDtypeStruct((rank, rows, cols), f32)
+    plain, scaled = pl.pallas_call(
+        begin_kernel,
+        out_shape=(weight_shape, weight_shape),
+        in_specs=[vmem] * 5 + [anywhere],
+        out_specs=(vmem,) * 2,
+        compiler_params=params,
+        name="begin",
+    )(own, shifted, gain, basis, own_part, energy)
+
     def last(*refs):
         last_kernel(radius, *refs)
 
     return pl.pallas_call(
         last,
         out_shape=(image_shape, image_shape),
-        in_specs=[vmem] * 9,
+        in_specs=[vmem] * 8,
         compiler_params=params,
         name="last",
-    )(own, shifted, gain, basis, energy, own_part, below, right, corner_back)
+    )(shifted, basis, energy, plain, scaled, below, right, corner_back)
 
 
 def solution(mesh):

time: 26.7 us -> 26.6 us (level)
    ppermute x3, waiting for transfers between devices: 3.6 us -> 3.94 us  [partner(): lax.ppermute(value, axis, [(i, i ^ step) for i in range(lax.axis_size(axi...]
    ppermute x6, waiting for transfers between devices: 3.73 us -> 3.44 us  [moved(): return lax.ppermute(value, ('fy', 'fx'), shift(sizes, steps))]
  transfers between devices with their start and end apart: 9 -> 9, of which waited for: 4 -> 3; matrix products, arithmetic and copies ran while one was open for 0% -> 0% of each run, Pallas kernels for 20% -> 20%
where the time goes in v5:
time: 26.6 us; the launch traced here: 26.2 us
  starting transfers between devices  11.1 us (42%)
  waiting for transfers between devices  7.38 us (28%)
  Pallas kernels  6.39 us (24%)
  between operations  0.72 us (3%)
  local copies, waits for them, and re-layouts  0.6 us (2%)
    ppermute x6, starting transfers between devices, moved(): return lax.ppermute(value, ('fy', 'fx'), shift(sizes, steps))  8.27 us
    ppermute x3, waiting for transfers between devices, partner(): lax.ppermute(value, axis, [(i, i ^ step) for i in range(lax.axis_size(axi...  3.94 us
    ppermute x6, waiting for transfers between devices, moved(): return lax.ppermute(value, ('fy', 'fx'), shift(sizes, steps))  3.44 us
    ppermute x3, starting transfers between devices, partner(): lax.ppermute(value, axis, [(i, i ^ step) for i in range(lax.axis_size(axi...  2.81 us
    pallas_call x1, Pallas kernels, per_device(): pl.pallas_call(bank_kernel, out_shape=(image_shape, above_shape, strip_sh...  2.57 us
    pallas_call x1, Pallas kernels, per_device(): pl.pallas_call(first_kernel, out_shape=(jax.ShapeDtypeStruct((128, cols),...  1.27 us
    pallas_call x1, Pallas kernels, per_device(): pl.pallas_call(last, out_shape=(image_shape, image_shape), in_specs=[vmem...  1.03 us
    pallas_call x1, Pallas kernels, per_device(): pl.pallas_call(prepare_kernel, out_shape=(jax.ShapeDtypeStruct((rank, cha...  0.78 us
  transfers between devices with their start and end apart: 9, of which 3 were waited for; matrix products, arithmetic and copies ran while one was open for 0% of the time, Pallas kernels for 20%

profile of v5, /device:TPU:1, one launch (start us, length us, event | category | flops | bytes accessed | tf_op | source)
XLA Modules:
  0.0 26.2 jit_solution(2282980797383729729)
XLA Ops:
  0.6 0.0 copy-start
  0.6 2.7 %collective-permute-start.3 = (f32[16,32,128]{2,1,0:T(8,128)}, f32[16,32,128]{2,1,0:T(8,128)S(1)}, u32[]{:S(2)}, u32[]{:S(2)}) collective-permute-start(f32[16,32,128]{2,1,0:T(8,128)} %start_hbm.1), channel_id=1, source_target_pairs={{0,4},{1,5},{2,6},{3,7},{4,8},{5,9},{6,10},{7,11},{8,12},{9,13},{1... | collective-permute-start | bytes 786440 | tf_op jit(solution)/shard_map/ppermute | solution.py:361
  3.3 1.3 %first.1 = (f32[128,128]{1,0:T(8,128)S(1)}, f32[16,8,128]{2,1,0:T(8,128)S(1)}, f32[16,32,128]{2,1,0:T(8,128)S(1)}, f32[16,32,128]{2,1,0:T(8,128)S(1)}, f32[16,32,128]{2,1,0:T(8,128)S(1)}) custom-call(f32[16,32,128]{2,1,0:T(8,128)} %start_hbm.1, f32[16,32,128]{2,1,0:T(8,128)} %dirty_hbm.1, f32[16,32,128]{2,1,0:T(8,128)} %sampling_hbm.1), custom_call_target="tpu_custom_call" | custom-call | tf_op jit(solution)/shard_map/first/pallas_call | solution.py:364
  4.6 1.3 %collective-permute-start = (f32[128,128]{1,0:T(8,128)S(1)}, f32[128,128]{1,0:T(8,128)S(1)}, u32[]{:S(2)}, u32[]{:S(2)}) collective-permute-start(f32[128,128]{1,0:T(8,128)S(1)} %get-tuple-element.24.value_ref), channel_id=1, source_target_pairs={{0,8},{4,12},{8,0},{12,4},{16,24},{20,28},{24,16},{28,20},{1,9},{5... | collective-permute-start | bytes 196616 | tf_op jit(solution)/shard_map/ppermute | solution.py:319
  5.8 0.0 copy-start.1
  5.9 0.0 copy-start.2
  5.9 1.3 %collective-permute-start.4 = (f32[16,8,128]{2,1,0:T(8,128)S(1)}, f32[16,8,128]{2,1,0:T(8,128)S(1)}, u32[]{:S(2)}, u32[]{:S(2)}) collective-permute-start(f32[16,8,128]{2,1,0:T(8,128)S(1)} %get-tuple-element.27), channel_id=1, source_target_pairs={{0,1},{1,2},{2,3},{3,0},{4,5},{5,6},{6,7},{7,4},{8,9},{9,10},{10,1... | collective-permute-start | bytes 196616 | tf_op jit(solution)/shard_map/ppermute | solution.py:361
  7.2 0.7 %collective-permute-start.5 = (f32[16,8,128]{2,1,0:T(8,128)S(1)}, f32[16,8,128]{2,1,0:T(8,128)S(1)}, u32[]{:S(2)}, u32[]{:S(2)}) collective-permute-start(f32[16,8,128]{2,1,0:T(8,128)S(1)} %get-tuple-element.27), channel_id=1, source_target_pairs={{0,5},{1,6},{2,7},{3,4},{4,9},{5,10},{6,11},{7,8},{8,13},{9,14},{1... | collective-permute-start | bytes 196616 | tf_op jit(solution)/shard_map/ppermute | solution.py:361
  7.8 2.3 %collective-permute-done.arrived_ref = f32[128,128]{1,0:T(8,128)S(1)} collective-permute-done((f32[128,128]{1,0:T(8,128)S(1)}, f32[128,128]{1,0:T(8,128)S(1)}, u32[]{:S(2)}, u32[]{:S(2)}) %collective-permute-start) | collective-permute-done | bytes 65568 | tf_op jit(solution)/shard_map/ppermute | solution.py:319
  10.2 0.1 collective-permute-start.1
  10.3 0.0 copy-done
  10.3 0.0 copy-done.1
  10.3 0.0 copy-done.2
  10.3 0.6 %copy-done.3 = f32[16,4]{0,1:T(4,128)S(1)} copy-done((f32[16,4]{0,1:T(4,128)S(1)}, f32[16,4]{0,1:T(4,128)}, u32[]{:S(2)}) %copy-start.3) | copy-done | bytes 280
  10.9 0.0 copy-done.4
  10.9 0.8 %prepare.1 = (f32[4,16,128]{2,1,0:T(8,128)S(1)}, bf16[128,192]{1,0:T(8,128)(2,1)S(1)}, bf16[64,384]{1,0:T(8,128)(2,1)S(1)}, bf16[2,2,256,256]{3,2,1,0:T(8,128)(2,1)S(1)}) custom-call(s32[1,1,2,2]{3,2,1,0:T(2,128)S(1)} %copy-done.4, f32[4,16]{1,0:T(4,128)S(1)} %bitcast.1, f32[8,128]{1,0:T(8,128)S(1)} %add.2.after_ref.value_ref, f32[128,64]{1,0:T(8,128)S(1)} %copy-done.1, ...), custom_call_target="tpu_custom_call" | custom-call | tf_op jit(solution)/shard_map/prepare/pallas_call | solution.py:381
  11.7 1.6 %collective-permute-done.1.arrived_ref = f32[8,128]{1,0:T(8,128)S(1)} collective-permute-done((f32[8,128]{1,0:T(8,128)S(1)}, f32[8,128]{1,0:T(8,128)S(1)}, u32[]{:S(2)}, u32[]{:S(2)}) %collective-permute-start.1) | collective-permute-done | bytes 4128 | tf_op jit(solution)/shard_map/ppermute | solution.py:319
  13.2 1.5 %collective-permute-start.2 = (f32[8,128]{1,0:T(8,128)S(1)}, f32[8,128]{1,0:T(8,128)S(1)}, u32[]{:S(2)}, u32[]{:S(2)}) collective-permute-start(f32[8,128]{1,0:T(8,128)S(1)} %add.3.after_ref.value_ref), channel_id=1, source_target_pairs={{0,2},{1,3},{2,0},{3,1},{4,6},{5,7},{6,4},{7,5},{8,10},{9,11},{10,... | collective-permute-start | bytes 12296 | tf_op jit(solution)/shard_map/ppermute | solution.py:319
  14.7 0.0 collective-permute-done.4.left_ref
  14.7 0.0 collective-permute-done.5.corner_ref
  14.7 0.0 collective-permute-done.3.above_ref
  14.7 0.5 %rows.1 = (bf16[2,16,64,256]{3,2,1,0:T(8,128)(2,1)S(1)}, bf16[2,16,64,256]{3,2,1,0:T(8,128)(2,1)S(1)}) custom-call(f32[16,32,128]{2,1,0:T(8,128)S(1)} %get-tuple-element.26.own_ref, f32[16,32,128]{2,1,0:T(8,128)S(1)} %collective-permute-done.3.above_ref, f32[16,8,128]{2,1,0:T(8,128)S(1)} %collective-permute-done.4.left_ref, ...), custom_call_target="tpu_custom_call" | custom-call | tf_op jit(solution)/shard_map/rows/pallas_call | solution.py:398
  15.3 2.6 %bank.1 = (f32[16,32,128]{2,1,0:T(8,128)S(1)}, f32[520,128]{1,0:T(8,128)S(1)}, f32[136,128]{1,0:T(8,128)S(1)}, f32[136,128]{1,0:T(8,128)S(1)}) custom-call(bf16[2,16,64,256]{3,2,1,0:T(8,128)(2,1)S(1)} %get-tuple-element.29.z_high, bf16[2,16,64,256]{3,2,1,0:T(8,128)(2,1)S(1)} %get-tuple-element.30.z_low, bf16[64,384]{1,0:T(8,128)(2,1)S(1)} %get-tuple-element.31.at_ref, ...), custom_call_target="tpu_custom_call" | custom-call | tf_op jit(solution)/shard_map/bank/pallas_call | solution.py:409
  17.8 0.0 collective-permute-done.2.arrived_ref
  17.9 0.2 collective-permute-start.6
  18.0 2.2 %collective-permute-start.7 = (f32[136,128]{1,0:T(8,128)S(1)}, f32[136,128]{1,0:T(8,128)S(1)}, u32[]{:S(2)}, u32[]{:S(2)}) collective-permute-start(f32[136,128]{1,0:T(8,128)S(1)} %get-tuple-element.42), channel_id=1, source_target_pairs={{0,3},{1,0},{2,1},{3,2},{4,7},{5,4},{6,5},{7,6},{8,11},{9,8},{10,9... | collective-permute-start | bytes 208904 | tf_op jit(solution)/shard_map/ppermute | solution.py:361
  20.3 1.2 %collective-permute-start.8 = (f32[136,128]{1,0:T(8,128)S(1)}, f32[136,128]{1,0:T(8,128)S(1)}, u32[]{:S(2)}, u32[]{:S(2)}) collective-permute-start(f32[136,128]{1,0:T(8,128)S(1)} %get-tuple-element.43), channel_id=1, source_target_pairs={{0,31},{1,28},{2,29},{3,30},{4,3},{5,0},{6,1},{7,2},{8,7},{9,4},{1... | collective-permute-start | bytes 208904 | tf_op jit(solution)/shard_map/ppermute | solution.py:361
  21.5 0.2 begin.1
  21.7 0.0 collective-permute-done.7.refs_6_
  21.7 3.4 %collective-permute-done.8.refs_7_ = f32[136,128]{1,0:T(8,128)S(1)} collective-permute-done((f32[136,128]{1,0:T(8,128)S(1)}, f32[136,128]{1,0:T(8,128)S(1)}, u32[]{:S(2)}, u32[]{:S(2)}) %collective-permute-start.8) | collective-permute-done | bytes 69664 | tf_op jit(solution)/shard_map/ppermute | solution.py:361
  25.2 0.0 collective-permute-done.6.refs_5_
  25.2 1.0 %last.1 = (f32[16,32,128]{2,1,0:T(8,128)}, f32[16,32,128]{2,1,0:T(8,128)}) custom-call(f32[16,32,128]{2,1,0:T(8,128)S(1)} %get-tuple-element.23.shifted_ref.refs_0_, f32[4,16,128]{2,1,0:T(8,128)S(1)} %get-tuple-element.25.refs_0_.basis_ref.refs_1_, f32[8,128]{1,0:T(8,128)S(1)} %get-tuple-element.36.after_ref.refs_2_, ...), custom_call_target="tpu_custom_call" | custom-call | tf_op jit(solution)/shard_map/last/pallas_call | solution.py:444
  (5 shorter events, 0.0 us)
Async XLA Ops:
  0.6 9.6 %copy-start = (f32[2,256,256]{2,1,0:T(8,128)S(1)}, f32[2,256,256]{2,1,0:T(8,128)}, u32[]{:S(2)}) copy-start(f32[2,256,256]{2,1,0:T(8,128)} %constant.8.clone.cols_ref) | copy-start | bytes 1572868
  0.6 14.1 %collective-permute-start.3 = (f32[16,32,128]{2,1,0:T(8,128)}, f32[16,32,128]{2,1,0:T(8,128)S(1)}, u32[]{:S(2)}, u32[]{:S(2)}) collective-permute-start(f32[16,32,128]{2,1,0:T(8,128)} %start_hbm.1), channel_id=1, source_target_pairs={{0,4},{1,5},{2,6},{3,7},{4,8},{5,9},{6,10},{7,11},{8,12},{9,13},{1... | collective-permute-start | bytes 786440 | tf_op jit(solution)/shard_map/ppermute | solution.py:361
  4.6 5.6 %collective-permute-start = (f32[128,128]{1,0:T(8,128)S(1)}, f32[128,128]{1,0:T(8,128)S(1)}, u32[]{:S(2)}, u32[]{:S(2)}) collective-permute-start(f32[128,128]{1,0:T(8,128)S(1)} %get-tuple-element.24.value_ref), channel_id=1, source_target_pairs={{0,8},{4,12},{8,0},{12,4},{16,24},{20,28},{24,16},{28,20},{1,9},{5... | collective-permute-start | bytes 196616 | tf_op jit(solution)/shard_map/ppermute | solution.py:319
  5.8 4.4 %copy-start.1 = (f32[128,64]{1,0:T(8,128)S(1)}, f32[128,64]{1,0:T(8,128)}, u32[]{:S(2)}) copy-start(f32[128,64]{1,0:T(8,128)} %constant.6.clone.rows_ref) | copy-start | bytes 98308
  5.9 4.4 %copy-start.2 = (f32[2,64,64]{2,1,0:T(8,128)S(1)}, f32[2,64,64]{2,1,0:T(8,128)}, u32[]{:S(2)}) copy-start(f32[2,64,64]{2,1,0:T(8,128)} %constant.7.clone.rows_t_ref) | copy-start | bytes 98308
  5.9 8.9 %collective-permute-start.4 = (f32[16,8,128]{2,1,0:T(8,128)S(1)}, f32[16,8,128]{2,1,0:T(8,128)S(1)}, u32[]{:S(2)}, u32[]{:S(2)}) collective-permute-start(f32[16,8,128]{2,1,0:T(8,128)S(1)} %get-tuple-element.27), channel_id=1, source_target_pairs={{0,1},{1,2},{2,3},{3,0},{4,5},{5,6},{6,7},{7,4},{8,9},{9,10},{10,1... | collective-permute-start | bytes 196616 | tf_op jit(solution)/shard_map/ppermute | solution.py:361
  7.2 7.6 %collective-permute-start.5 = (f32[16,8,128]{2,1,0:T(8,128)S(1)}, f32[16,8,128]{2,1,0:T(8,128)S(1)}, u32[]{:S(2)}, u32[]{:S(2)}) collective-permute-start(f32[16,8,128]{2,1,0:T(8,128)S(1)} %get-tuple-element.27), channel_id=1, source_target_pairs={{0,5},{1,6},{2,7},{3,4},{4,9},{5,10},{6,11},{7,8},{8,13},{9,14},{1... | collective-permute-start | bytes 196616 | tf_op jit(solution)/shard_map/ppermute | solution.py:361
  10.2 0.7 %copy-start.3 = (f32[16,4]{0,1:T(4,128)S(1)}, f32[16,4]{0,1:T(4,128)}, u32[]{:S(2)}) copy-start(f32[16,4]{0,1:T(4,128)} %param.11) | copy-start | bytes 772
  10.2 0.7 %copy-start.4 = (s32[1,1,2,2]{3,2,1,0:T(2,128)S(1)}, s32[1,1,2,2]{3,2,1,0:T(2,128)}, u32[]{:S(2)}) copy-start(s32[1,1,2,2]{3,2,1,0:T(2,128)} %margin_ref.1) | copy-start | bytes 52
  10.2 3.1 %collective-permute-start.1 = (f32[8,128]{1,0:T(8,128)S(1)}, f32[8,128]{1,0:T(8,128)S(1)}, u32[]{:S(2)}, u32[]{:S(2)}) collective-permute-start(f32[8,128]{1,0:T(8,128)S(1)} %add.2.after_ref.value_ref), channel_id=1, source_target_pairs={{0,16},{4,20},{8,24},{12,28},{16,0},{20,4},{24,8},{28,12},{1,17},{... | collective-permute-start | bytes 12296 | tf_op jit(solution)/shard_map/ppermute | solution.py:319
  13.2 4.6 %collective-permute-start.2 = (f32[8,128]{1,0:T(8,128)S(1)}, f32[8,128]{1,0:T(8,128)S(1)}, u32[]{:S(2)}, u32[]{:S(2)}) collective-permute-start(f32[8,128]{1,0:T(8,128)S(1)} %add.3.after_ref.value_ref), channel_id=1, source_target_pairs={{0,2},{1,3},{2,0},{3,1},{4,6},{5,7},{6,4},{7,5},{8,10},{9,11},{10,... | collective-permute-start | bytes 12296 | tf_op jit(solution)/shard_map/ppermute | solution.py:319
  17.9 7.3 %collective-permute-start.6 = (f32[520,128]{1,0:T(8,128)S(1)}, f32[520,128]{1,0:T(8,128)S(1)}, u32[]{:S(2)}, u32[]{:S(2)}) collective-permute-start(f32[520,128]{1,0:T(8,128)S(1)} %get-tuple-element.41), channel_id=1, source_target_pairs={{0,28},{1,29},{2,30},{3,31},{4,0},{5,1},{6,2},{7,3},{8,4},{9,5},{1... | collective-permute-start | bytes 798728 | tf_op jit(solution)/shard_map/ppermute | solution.py:361
  18.0 3.7 %collective-permute-start.7 = (f32[136,128]{1,0:T(8,128)S(1)}, f32[136,128]{1,0:T(8,128)S(1)}, u32[]{:S(2)}, u32[]{:S(2)}) collective-permute-start(f32[136,128]{1,0:T(8,128)S(1)} %get-tuple-element.42), channel_id=1, source_target_pairs={{0,3},{1,0},{2,1},{3,2},{4,7},{5,4},{6,5},{7,6},{8,11},{9,8},{10,9... | collective-permute-start | bytes 208904 | tf_op jit(solution)/shard_map/ppermute | solution.py:361
  20.3 4.9 %collective-permute-start.8 = (f32[136,128]{1,0:T(8,128)S(1)}, f32[136,128]{1,0:T(8,128)S(1)}, u32[]{:S(2)}, u32[]{:S(2)}) collective-permute-start(f32[136,128]{1,0:T(8,128)S(1)} %get-tuple-element.43), channel_id=1, source_target_pairs={{0,31},{1,28},{2,29},{3,30},{4,3},{5,0},{6,1},{7,2},{8,7},{9,4},{1... | collective-permute-start | bytes 208904 | tf_op jit(solution)/shard_map/ppermute | solution.py:361

commit v6 on v5

--- a/solution.py
+++ b/solution.py
@@ -36,6 +36,7 @@
 CLIP_LEVEL = 0.08
 BALL_SCALE = 0.8
 NORM_EPS = 1e-06
+AHEAD = pl.CostEstimate(flops=10**9, transcendentals=0, bytes_accessed=10**8)
 WEIGHT = 1.0 / math.sqrt(LEVELS)
 BAND_STEP = DUAL_STEP * WEIGHT
 
@@ -307,10 +308,10 @@
 def doubling():
     rounds = []
     for axis in ("fy", "fx"):
-        step = 2
-        while step < lax.axis_size(axis):
+        step = lax.axis_size(axis) // 2
+        while step > 1:
             rounds.append((axis, step))
-            step *= 2
+            step //= 2
     return rounds
 
 
@@ -363,7 +364,7 @@
     above = moved(start_image, (1, 0))
     energy, pack, own, gain, shifted = pl.pallas_call(
         first_kernel,
-        out_shape=(jax.ShapeDtypeStruct((128, cols), f32), pack_shape, image_shape, image_shape, image_shape),
+        out_shape=(jax.ShapeDtypeStruct((8, cols), f32), pack_shape, image_shape, image_shape, image_shape),
         in_specs=[hbm] * 3,
         out_specs=(vmem,) * 5,
         scratch_shapes=[pltpu.VMEM((channels, rows, cols), f32), pltpu.SemaphoreType.DMA((1, 3))],
@@ -389,6 +390,7 @@
         in_specs=[smem, vmem, anywhere, vmem, vmem, vmem],
         out_specs=(vmem,) * 4,
         compiler_params=params,
+        cost_estimate=AHEAD,
         name="prepare",
     )(margin, basis_seed.T, energy, table, table_t, col_table(cols))
     for round_ in rounds[1:-1]:

time: 26.6 us -> 25.3 us (0.951)
  waiting for transfers between devices: 7.38 us -> 5.89 us
  starting transfers between devices: 11.1 us -> 11.7 us
    ppermute x3, waiting for transfers between devices: 3.94 us -> 1.07 us  [partner(): lax.ppermute(value, axis, [(i, i ^ step) for i in range(lax.axis_size(axi...]
    ppermute x6, waiting for transfers between devices: 3.44 us -> 4.82 us  [moved(): return lax.ppermute(value, ('fy', 'fx'), shift(sizes, steps))]
    ppermute x6, starting transfers between devices: 8.27 us -> 8.94 us  [moved(): return lax.ppermute(value, ('fy', 'fx'), shift(sizes, steps))]
  transfers between devices with their start and end apart: 9 -> 9, of which waited for: 3 -> 4; matrix products, arithmetic and copies ran while one was open for 0% -> 0% of each run, Pallas kernels for 20% -> 21%
where the time goes in v6:
time: 25.3 us; the launch traced here: 25.1 us
  starting transfers between devices  11.7 us (46%)
  Pallas kernels  6.39 us (25%)
  waiting for transfers between devices  5.89 us (23%)
  between operations  0.7 us (3%)
  local copies, waits for them, and re-layouts  0.42 us (2%)
    ppermute x6, starting transfers between devices, moved(): return lax.ppermute(value, ('fy', 'fx'), shift(sizes, steps))  8.94 us
    ppermute x6, waiting for transfers between devices, moved(): return lax.ppermute(value, ('fy', 'fx'), shift(sizes, steps))  4.82 us
    ppermute x3, starting transfers between devices, partner(): lax.ppermute(value, axis, [(i, i ^ step) for i in range(lax.axis_size(axi...  2.77 us
    pallas_call x1, Pallas kernels, per_device(): pl.pallas_call(bank_kernel, out_shape=(image_shape, above_shape, strip_sh...  2.57 us
    pallas_call x1, Pallas kernels, per_device(): pl.pallas_call(first_kernel, out_shape=(jax.ShapeDtypeStruct((8, cols), f...  1.27 us
    ppermute x3, waiting for transfers between devices, partner(): lax.ppermute(value, axis, [(i, i ^ step) for i in range(lax.axis_size(axi...  1.07 us
    pallas_call x1, Pallas kernels, per_device(): pl.pallas_call(last, out_shape=(image_shape, image_shape), in_specs=[vmem...  1.03 us
    pallas_call x1, Pallas kernels, per_device(): pl.pallas_call(prepare_kernel, out_shape=(jax.ShapeDtypeStruct((rank, cha...  0.78 us
  transfers between devices with their start and end apart: 9, of which 4 were waited for; matrix products, arithmetic and copies ran while one was open for 0% of the time, Pallas kernels for 21%

profile of v6, /device:TPU:1, one launch (start us, length us, event | category | flops | bytes accessed | tf_op | source)
XLA Modules:
  0.0 25.1 jit_solution(4108749159940699167)
XLA Ops:
  0.6 0.0 copy-start.2
  0.6 0.0 copy-start.3
  0.7 0.0 copy-start.4
  0.7 2.7 %collective-permute-start.3 = (f32[16,32,128]{2,1,0:T(8,128)}, f32[16,32,128]{2,1,0:T(8,128)S(1)}, u32[]{:S(2)}, u32[]{:S(2)}) collective-permute-start(f32[16,32,128]{2,1,0:T(8,128)} %start_hbm.1), channel_id=1, source_target_pairs={{0,4},{1,5},{2,6},{3,7},{4,8},{5,9},{6,10},{7,11},{8,12},{9,13},{1... | collective-permute-start | bytes 786440 | tf_op jit(solution)/shard_map/ppermute | solution.py:362
  3.3 1.3 %first.1 = (f32[8,128]{1,0:T(8,128)S(1)}, f32[16,8,128]{2,1,0:T(8,128)S(1)}, f32[16,32,128]{2,1,0:T(8,128)S(1)}, f32[16,32,128]{2,1,0:T(8,128)S(1)}, f32[16,32,128]{2,1,0:T(8,128)S(1)}) custom-call(f32[16,32,128]{2,1,0:T(8,128)} %start_hbm.1, f32[16,32,128]{2,1,0:T(8,128)} %dirty_hbm.1, f32[16,32,128]{2,1,0:T(8,128)} %sampling_hbm.1), custom_call_target="tpu_custom_call" | custom-call | tf_op jit(solution)/shard_map/first/pallas_call | solution.py:365
  4.6 1.3 %collective-permute-start = (f32[8,128]{1,0:T(8,128)S(1)}, f32[8,128]{1,0:T(8,128)S(1)}, u32[]{:S(2)}, u32[]{:S(2)}) collective-permute-start(f32[8,128]{1,0:T(8,128)S(1)} %get-tuple-element.24.value_ref), channel_id=1, source_target_pairs={{0,16},{4,20},{8,24},{12,28},{16,0},{20,4},{24,8},{28,12},{1,17},{... | collective-permute-start | bytes 12296 | tf_op jit(solution)/shard_map/ppermute | solution.py:320
  5.9 1.3 %collective-permute-start.4 = (f32[16,8,128]{2,1,0:T(8,128)S(1)}, f32[16,8,128]{2,1,0:T(8,128)S(1)}, u32[]{:S(2)}, u32[]{:S(2)}) collective-permute-start(f32[16,8,128]{2,1,0:T(8,128)S(1)} %get-tuple-element.27), channel_id=1, source_target_pairs={{0,1},{1,2},{2,3},{3,0},{4,5},{5,6},{6,7},{7,4},{8,9},{9,10},{10,1... | collective-permute-start | bytes 196616 | tf_op jit(solution)/shard_map/ppermute | solution.py:362
  7.2 1.6 %collective-permute-start.5 = (f32[16,8,128]{2,1,0:T(8,128)S(1)}, f32[16,8,128]{2,1,0:T(8,128)S(1)}, u32[]{:S(2)}, u32[]{:S(2)}) collective-permute-start(f32[16,8,128]{2,1,0:T(8,128)S(1)} %get-tuple-element.27), channel_id=1, source_target_pairs={{0,5},{1,6},{2,7},{3,4},{4,9},{5,10},{6,11},{7,8},{8,13},{9,14},{1... | collective-permute-start | bytes 196616 | tf_op jit(solution)/shard_map/ppermute | solution.py:362
  8.8 0.0 collective-permute-done.arrived_ref
  8.9 0.3 %collective-permute-start.1 = (f32[8,128]{1,0:T(8,128)S(1)}, f32[8,128]{1,0:T(8,128)S(1)}, u32[]{:S(2)}, u32[]{:S(2)}) collective-permute-start(f32[8,128]{1,0:T(8,128)S(1)} %add.2.after_ref.value_ref), channel_id=1, source_target_pairs={{0,8},{4,12},{8,0},{12,4},{16,24},{20,28},{24,16},{28,20},{1,9},{5... | collective-permute-start | bytes 12296 | tf_op jit(solution)/shard_map/ppermute | solution.py:320
  9.1 0.0 copy-done.2
  9.1 0.0 copy-done.3
  9.1 0.0 copy-done.4
  9.1 0.0 copy-done
  9.1 0.4 %copy-done.1 = s32[1,1,2,2]{3,2,1,0:T(2,128)S(1)} copy-done((s32[1,1,2,2]{3,2,1,0:T(2,128)S(1)}, s32[1,1,2,2]{3,2,1,0:T(2,128)}, u32[]{:S(2)}) %copy-start.1) | copy-done | bytes 40
  9.5 0.8 %prepare.1 = (f32[4,16,128]{2,1,0:T(8,128)S(1)}, bf16[128,192]{1,0:T(8,128)(2,1)S(1)}, bf16[64,384]{1,0:T(8,128)(2,1)S(1)}, bf16[2,2,256,256]{3,2,1,0:T(8,128)(2,1)S(1)}) custom-call(s32[1,1,2,2]{3,2,1,0:T(2,128)S(1)} %copy-done.1, f32[4,16]{1,0:T(4,128)S(1)} %bitcast.1, f32[8,128]{1,0:T(8,128)S(1)} %add.2.after_ref.value_ref, f32[128,64]{1,0:T(8,128)S(1)} %copy-done.3, ...), custom_call_target="tpu_custom_call" | custom-call | flops 1000000000 | bytes 100000000 | tf_op jit(solution)/shard_map/prepare/pallas_call | solution.py:382
  10.3 1.1 %collective-permute-done.1.arrived_ref = f32[8,128]{1,0:T(8,128)S(1)} collective-permute-done((f32[8,128]{1,0:T(8,128)S(1)}, f32[8,128]{1,0:T(8,128)S(1)}, u32[]{:S(2)}, u32[]{:S(2)}) %collective-permute-start.1) | collective-permute-done | bytes 4128 | tf_op jit(solution)/shard_map/ppermute | solution.py:320
  11.4 1.2 %collective-permute-start.2 = (f32[8,128]{1,0:T(8,128)S(1)}, f32[8,128]{1,0:T(8,128)S(1)}, u32[]{:S(2)}, u32[]{:S(2)}) collective-permute-start(f32[8,128]{1,0:T(8,128)S(1)} %add.3.after_ref.value_ref), channel_id=1, source_target_pairs={{0,2},{1,3},{2,0},{3,1},{4,6},{5,7},{6,4},{7,5},{8,10},{9,11},{10,... | collective-permute-start | bytes 12296 | tf_op jit(solution)/shard_map/ppermute | solution.py:320
  12.6 0.0 collective-permute-done.4.left_ref
  12.6 0.9 %collective-permute-done.5.corner_ref = f32[16,8,128]{2,1,0:T(8,128)S(1)} collective-permute-done((f32[16,8,128]{2,1,0:T(8,128)S(1)}, f32[16,8,128]{2,1,0:T(8,128)S(1)}, u32[]{:S(2)}, u32[]{:S(2)}) %collective-permute-start.5) | collective-permute-done | bytes 65568 | tf_op jit(solution)/shard_map/ppermute | solution.py:362
  13.5 0.0 collective-permute-done.3.above_ref
  13.5 0.5 %rows.1 = (bf16[2,16,64,256]{3,2,1,0:T(8,128)(2,1)S(1)}, bf16[2,16,64,256]{3,2,1,0:T(8,128)(2,1)S(1)}) custom-call(f32[16,32,128]{2,1,0:T(8,128)S(1)} %get-tuple-element.26.own_ref, f32[16,32,128]{2,1,0:T(8,128)S(1)} %collective-permute-done.3.above_ref, f32[16,8,128]{2,1,0:T(8,128)S(1)} %collective-permute-done.4.left_ref, ...), custom_call_target="tpu_custom_call" | custom-call | tf_op jit(solution)/shard_map/rows/pallas_call | solution.py:400
  14.0 2.6 %bank.1 = (f32[16,32,128]{2,1,0:T(8,128)S(1)}, f32[520,128]{1,0:T(8,128)S(1)}, f32[136,128]{1,0:T(8,128)S(1)}, f32[136,128]{1,0:T(8,128)S(1)}) custom-call(bf16[2,16,64,256]{3,2,1,0:T(8,128)(2,1)S(1)} %get-tuple-element.29.z_high, bf16[2,16,64,256]{3,2,1,0:T(8,128)(2,1)S(1)} %get-tuple-element.30.z_low, bf16[64,384]{1,0:T(8,128)(2,1)S(1)} %get-tuple-element.31.at_ref, ...), custom_call_target="tpu_custom_call" | custom-call | tf_op jit(solution)/shard_map/bank/pallas_call | solution.py:411
  16.6 0.0 collective-permute-done.2.arrived_ref
  16.6 1.1 %collective-permute-start.6 = (f32[520,128]{1,0:T(8,128)S(1)}, f32[520,128]{1,0:T(8,128)S(1)}, u32[]{:S(2)}, u32[]{:S(2)}) collective-permute-start(f32[520,128]{1,0:T(8,128)S(1)} %get-tuple-element.41), channel_id=1, source_target_pairs={{0,28},{1,29},{2,30},{3,31},{4,0},{5,1},{6,2},{7,3},{8,4},{9,5},{1... | collective-permute-start | bytes 798728 | tf_op jit(solution)/shard_map/ppermute | solution.py:362
  17.7 1.8 %collective-permute-start.7 = (f32[136,128]{1,0:T(8,128)S(1)}, f32[136,128]{1,0:T(8,128)S(1)}, u32[]{:S(2)}, u32[]{:S(2)}) collective-permute-start(f32[136,128]{1,0:T(8,128)S(1)} %get-tuple-element.42), channel_id=1, source_target_pairs={{0,3},{1,0},{2,1},{3,2},{4,7},{5,4},{6,5},{7,6},{8,11},{9,8},{10,9... | collective-permute-start | bytes 208904 | tf_op jit(solution)/shard_map/ppermute | solution.py:362
  19.4 0.5 %collective-permute-start.8 = (f32[136,128]{1,0:T(8,128)S(1)}, f32[136,128]{1,0:T(8,128)S(1)}, u32[]{:S(2)}, u32[]{:S(2)}) collective-permute-start(f32[136,128]{1,0:T(8,128)S(1)} %get-tuple-element.43), channel_id=1, source_target_pairs={{0,31},{1,28},{2,29},{3,30},{4,3},{5,0},{6,1},{7,2},{8,7},{9,4},{1... | collective-permute-start | bytes 208904 | tf_op jit(solution)/shard_map/ppermute | solution.py:362
  19.9 0.2 begin.1
  20.1 1.0 %collective-permute-done.7.refs_6_ = f32[136,128]{1,0:T(8,128)S(1)} collective-permute-done((f32[136,128]{1,0:T(8,128)S(1)}, f32[136,128]{1,0:T(8,128)S(1)}, u32[]{:S(2)}, u32[]{:S(2)}) %collective-permute-start.7) | collective-permute-done | bytes 69664 | tf_op jit(solution)/shard_map/ppermute | solution.py:362
  21.2 2.9 %collective-permute-done.8.refs_7_ = f32[136,128]{1,0:T(8,128)S(1)} collective-permute-done((f32[136,128]{1,0:T(8,128)S(1)}, f32[136,128]{1,0:T(8,128)S(1)}, u32[]{:S(2)}, u32[]{:S(2)}) %collective-permute-start.8) | collective-permute-done | bytes 69664 | tf_op jit(solution)/shard_map/ppermute | solution.py:362
  24.1 0.0 collective-permute-done.6.refs_5_
  24.1 1.0 %last.1 = (f32[16,32,128]{2,1,0:T(8,128)}, f32[16,32,128]{2,1,0:T(8,128)}) custom-call(f32[16,32,128]{2,1,0:T(8,128)S(1)} %get-tuple-element.23.shifted_ref.refs_0_, f32[4,16,128]{2,1,0:T(8,128)S(1)} %get-tuple-element.25.refs_0_.basis_ref.refs_1_, f32[8,128]{1,0:T(8,128)S(1)} %get-tuple-element.36.after_ref.refs_2_, ...), custom_call_target="tpu_custom_call" | custom-call | tf_op jit(solution)/shard_map/last/pallas_call | solution.py:446
  (5 shorter events, 0.0 us)
Async XLA Ops:
  0.6 8.5 %copy-start.2 = (f32[2,256,256]{2,1,0:T(8,128)S(1)}, f32[2,256,256]{2,1,0:T(8,128)}, u32[]{:S(2)}) copy-start(f32[2,256,256]{2,1,0:T(8,128)} %constant.8.clone.cols_ref) | copy-start | bytes 1572868
  0.6 8.5 %copy-start.3 = (f32[128,64]{1,0:T(8,128)S(1)}, f32[128,64]{1,0:T(8,128)}, u32[]{:S(2)}) copy-start(f32[128,64]{1,0:T(8,128)} %constant.6.clone.rows_ref) | copy-start | bytes 98308
  0.7 8.5 %copy-start.4 = (f32[2,64,64]{2,1,0:T(8,128)S(1)}, f32[2,64,64]{2,1,0:T(8,128)}, u32[]{:S(2)}) copy-start(f32[2,64,64]{2,1,0:T(8,128)} %constant.7.clone.rows_t_ref) | copy-start | bytes 98308
  0.7 12.8 %collective-permute-start.3 = (f32[16,32,128]{2,1,0:T(8,128)}, f32[16,32,128]{2,1,0:T(8,128)S(1)}, u32[]{:S(2)}, u32[]{:S(2)}) collective-permute-start(f32[16,32,128]{2,1,0:T(8,128)} %start_hbm.1), channel_id=1, source_target_pairs={{0,4},{1,5},{2,6},{3,7},{4,8},{5,9},{6,10},{7,11},{8,12},{9,13},{1... | collective-permute-start | bytes 786440 | tf_op jit(solution)/shard_map/ppermute | solution.py:362
  4.6 4.2 %collective-permute-start = (f32[8,128]{1,0:T(8,128)S(1)}, f32[8,128]{1,0:T(8,128)S(1)}, u32[]{:S(2)}, u32[]{:S(2)}) collective-permute-start(f32[8,128]{1,0:T(8,128)S(1)} %get-tuple-element.24.value_ref), channel_id=1, source_target_pairs={{0,16},{4,20},{8,24},{12,28},{16,0},{20,4},{24,8},{28,12},{1,17},{... | collective-permute-start | bytes 12296 | tf_op jit(solution)/shard_map/ppermute | solution.py:320
  5.9 3.2 %copy-start = (f32[16,4]{0,1:T(4,128)S(1)}, f32[16,4]{0,1:T(4,128)}, u32[]{:S(2)}) copy-start(f32[16,4]{0,1:T(4,128)} %param.11) | copy-start | bytes 772
  5.9 6.7 %collective-permute-start.4 = (f32[16,8,128]{2,1,0:T(8,128)S(1)}, f32[16,8,128]{2,1,0:T(8,128)S(1)}, u32[]{:S(2)}, u32[]{:S(2)}) collective-permute-start(f32[16,8,128]{2,1,0:T(8,128)S(1)} %get-tuple-element.27), channel_id=1, source_target_pairs={{0,1},{1,2},{2,3},{3,0},{4,5},{5,6},{6,7},{7,4},{8,9},{9,10},{10,1... | collective-permute-start | bytes 196616 | tf_op jit(solution)/shard_map/ppermute | solution.py:362
  7.2 6.3 %collective-permute-start.5 = (f32[16,8,128]{2,1,0:T(8,128)S(1)}, f32[16,8,128]{2,1,0:T(8,128)S(1)}, u32[]{:S(2)}, u32[]{:S(2)}) collective-permute-start(f32[16,8,128]{2,1,0:T(8,128)S(1)} %get-tuple-element.27), channel_id=1, source_target_pairs={{0,5},{1,6},{2,7},{3,4},{4,9},{5,10},{6,11},{7,8},{8,13},{9,14},{1... | collective-permute-start | bytes 196616 | tf_op jit(solution)/shard_map/ppermute | solution.py:362
  8.8 0.7 %copy-start.1 = (s32[1,1,2,2]{3,2,1,0:T(2,128)S(1)}, s32[1,1,2,2]{3,2,1,0:T(2,128)}, u32[]{:S(2)}) copy-start(s32[1,1,2,2]{3,2,1,0:T(2,128)} %margin_ref.1) | copy-start | bytes 52
  8.9 2.5 %collective-permute-start.1 = (f32[8,128]{1,0:T(8,128)S(1)}, f32[8,128]{1,0:T(8,128)S(1)}, u32[]{:S(2)}, u32[]{:S(2)}) collective-permute-start(f32[8,128]{1,0:T(8,128)S(1)} %add.2.after_ref.value_ref), channel_id=1, source_target_pairs={{0,8},{4,12},{8,0},{12,4},{16,24},{20,28},{24,16},{28,20},{1,9},{5... | collective-permute-start | bytes 12296 | tf_op jit(solution)/shard_map/ppermute | solution.py:320
  11.4 5.2 %collective-permute-start.2 = (f32[8,128]{1,0:T(8,128)S(1)}, f32[8,128]{1,0:T(8,128)S(1)}, u32[]{:S(2)}, u32[]{:S(2)}) collective-permute-start(f32[8,128]{1,0:T(8,128)S(1)} %add.3.after_ref.value_ref), channel_id=1, source_target_pairs={{0,2},{1,3},{2,0},{3,1},{4,6},{5,7},{6,4},{7,5},{8,10},{9,11},{10,... | collective-permute-start | bytes 12296 | tf_op jit(solution)/shard_map/ppermute | solution.py:320
  16.6 7.5 %collective-permute-start.6 = (f32[520,128]{1,0:T(8,128)S(1)}, f32[520,128]{1,0:T(8,128)S(1)}, u32[]{:S(2)}, u32[]{:S(2)}) collective-permute-start(f32[520,128]{1,0:T(8,128)S(1)} %get-tuple-element.41), channel_id=1, source_target_pairs={{0,28},{1,29},{2,30},{3,31},{4,0},{5,1},{6,2},{7,3},{8,4},{9,5},{1... | collective-permute-start | bytes 798728 | tf_op jit(solution)/shard_map/ppermute | solution.py:362
  17.7 3.5 %collective-permute-start.7 = (f32[136,128]{1,0:T(8,128)S(1)}, f32[136,128]{1,0:T(8,128)S(1)}, u32[]{:S(2)}, u32[]{:S(2)}) collective-permute-start(f32[136,128]{1,0:T(8,128)S(1)} %get-tuple-element.42), channel_id=1, source_target_pairs={{0,3},{1,0},{2,1},{3,2},{4,7},{5,4},{6,5},{7,6},{8,11},{9,8},{10,9... | collective-permute-start | bytes 208904 | tf_op jit(solution)/shard_map/ppermute | solution.py:362
  19.4 4.6 %collective-permute-start.8 = (f32[136,128]{1,0:T(8,128)S(1)}, f32[136,128]{1,0:T(8,128)S(1)}, u32[]{:S(2)}, u32[]{:S(2)}) collective-permute-start(f32[136,128]{1,0:T(8,128)S(1)} %get-tuple-element.43), channel_id=1, source_target_pairs={{0,31},{1,28},{2,29},{3,30},{4,3},{5,0},{6,1},{7,2},{8,7},{9,4},{1... | collective-permute-start | bytes 208904 | tf_op jit(solution)/shard_map/ppermute | solution.py:362

commit v7 on v6

--- a/solution.py
+++ b/solution.py
@@ -190,10 +190,16 @@
     return lax.dot_general(a, b, (((1,), (1,)), ((), ())), preferred_element_type=jnp.float32)
 
 
-def rows_kernel(own_ref, above_ref, left_ref, corner_ref, a_ref, after_ref, z_high, z_low):
-    channels, rows, cols = own_ref.shape
+def bank_kernel(
+    own_ref, above_ref, corner_ref, left_ref, a_ref, at_ref, g_ref, after_ref,
+    own_out, above_out, left_out, corner_out, z_high, z_low, u_high, u_low,
+):
+    channels, rows, cols = own_out.shape
+    wide = cols + LANES
+    half = 2 * rows
+    size = channels // 4
     groups = rows // 8
-    half = 2 * rows
+
     for c in range(channels):
         upper = jnp.concatenate([above_ref[c], unpack_rows(corner_ref[c], 0, groups)], axis=1)
         lower = jnp.concatenate([own_ref[c], unpack_rows(left_ref[c], 0, groups)], axis=1)
@@ -203,14 +209,6 @@
         for level in range(LEVELS):
             z_high[level, c] = part_high[level * half : (level + 1) * half]
             z_low[level, c] = part_low[level * half : (level + 1) * half]
-
-def bank_kernel(
-    z_high, z_low, at_ref, g_ref, own_out, above_out, left_out, corner_out, u_high, u_low,
-):
-    channels, rows, cols = own_out.shape
-    wide = cols + LANES
-    half = 2 * rows
-    size = channels // 4
 
     low_rows = row_iota((half, 2 * cols)) < rows
     low_cols = lane_iota((half, 2 * cols)) < cols
@@ -396,27 +394,17 @@
     for round_ in rounds[1:-1]:
         energy = added(energy, partner(energy, round_), basis)
     arriving = partner(energy, rounds[-1])
-    bank_shape = jax.ShapeDtypeStruct((LEVELS, channels, half, wide), bf16)
-    z_high, z_low = pl.pallas_call(
-        rows_kernel,
-        out_shape=(bank_shape, bank_shape),
-        in_specs=[vmem] * 5 + [anywhere],
-        out_specs=(vmem,) * 2,
-        compiler_params=params,
-        name="rows",
-    )(own, above, left, corner, a, energy)
-
     above_shape = jax.ShapeDtypeStruct((channels * BORDER + 8, cols), f32)
     strip_shape = jax.ShapeDtypeStruct((channels * 8 + 8, LANES), f32)
     own_part, *parts = pl.pallas_call(
         bank_kernel,
         out_shape=(image_shape, above_shape, strip_shape, strip_shape),
-        in_specs=[vmem] * 4,
+        in_specs=[vmem] * 7 + [anywhere],
         out_specs=(vmem,) * 4,
-        scratch_shapes=[pltpu.VMEM(bank_shape.shape, bf16)] * 2,
+        scratch_shapes=[pltpu.VMEM((LEVELS, channels, half, wide), bf16)] * 4,
         compiler_params=params,
         name="bank",
-    )(z_high, z_low, a_t, g)
+    )(own, above, corner, left, a, a_t, g, energy)
     energy, *parts = pl.pallas_call(
         stamp_kernel,
         out_shape=(jax.ShapeDtypeStruct(energy.shape, f32), above_shape, strip_shape, strip_shape),

time: 25.3 us -> 25 us (0.988)
    pallas_call x1 -> x0, Pallas kernels: 0.53 us -> none  [per_device(): pl.pallas_call(rows_kernel, out_shape=(bank_shape, bank_shape), in_specs=...]
    pallas_call x1, Pallas kernels: 2.57 us -> 2.89 us  [per_device(): pl.pallas_call(bank_kernel, out_shape=(image_shape, above_shape, strip_sh...]
where the time goes in v7:
time: 25 us; the launch traced here: 24.9 us
  starting transfers between devices  11.7 us (47%)
  Pallas kernels  6.17 us (25%)
  waiting for transfers between devices  5.9 us (24%)
  between operations  0.7 us (3%)
  local copies, waits for them, and re-layouts  0.42 us (2%)
    ppermute x6, starting transfers between devices, moved(): return lax.ppermute(value, ('fy', 'fx'), shift(sizes, steps))  8.94 us
    ppermute x6, waiting for transfers between devices, moved(): return lax.ppermute(value, ('fy', 'fx'), shift(sizes, steps))  4.83 us
    pallas_call x1, Pallas kernels, per_device(): pl.pallas_call(bank_kernel, out_shape=(image_shape, above_shape, strip_sh...  2.89 us
    ppermute x3, starting transfers between devices, partner(): lax.ppermute(value, axis, [(i, i ^ step) for i in range(lax.axis_size(axi...  2.76 us
    pallas_call x1, Pallas kernels, per_device(): pl.pallas_call(first_kernel, out_shape=(jax.ShapeDtypeStruct((8, cols), f...  1.26 us
    ppermute x3, waiting for transfers between devices, partner(): lax.ppermute(value, axis, [(i, i ^ step) for i in range(lax.axis_size(axi...  1.07 us
    pallas_call x1, Pallas kernels, per_device(): pl.pallas_call(last, out_shape=(image_shape, image_shape), in_specs=[vmem...  1.03 us
    pallas_call x1, Pallas kernels, per_device(): pl.pallas_call(prepare_kernel, out_shape=(jax.ShapeDtypeStruct((rank, cha...  0.78 us
  transfers between devices with their start and end apart: 9, of which 4 were waited for; matrix products, arithmetic and copies ran while one was open for 0% of the time, Pallas kernels for 21%

profile of v7, /device:TPU:1, one launch (start us, length us, event | category | flops | bytes accessed | tf_op | source)
XLA Modules:
  0.0 24.9 jit_solution(9401094864179604240)
XLA Ops:
  0.6 0.0 copy-start.2
  0.6 0.0 copy-start.3
  0.7 0.0 copy-start.4
  0.7 2.7 %collective-permute-start.3 = (f32[16,32,128]{2,1,0:T(8,128)}, f32[16,32,128]{2,1,0:T(8,128)S(1)}, u32[]{:S(2)}, u32[]{:S(2)}) collective-permute-start(f32[16,32,128]{2,1,0:T(8,128)} %start_hbm.1), channel_id=1, source_target_pairs={{0,4},{1,5},{2,6},{3,7},{4,8},{5,9},{6,10},{7,11},{8,12},{9,13},{1... | collective-permute-start | bytes 786440 | tf_op jit(solution)/shard_map/ppermute | solution.py:360
  3.3 1.3 %first.1 = (f32[8,128]{1,0:T(8,128)S(1)}, f32[16,8,128]{2,1,0:T(8,128)S(1)}, f32[16,32,128]{2,1,0:T(8,128)S(1)}, f32[16,32,128]{2,1,0:T(8,128)S(1)}, f32[16,32,128]{2,1,0:T(8,128)S(1)}) custom-call(f32[16,32,128]{2,1,0:T(8,128)} %start_hbm.1, f32[16,32,128]{2,1,0:T(8,128)} %dirty_hbm.1, f32[16,32,128]{2,1,0:T(8,128)} %sampling_hbm.1), custom_call_target="tpu_custom_call" | custom-call | tf_op jit(solution)/shard_map/first/pallas_call | solution.py:363
  4.6 1.3 %collective-permute-start = (f32[8,128]{1,0:T(8,128)S(1)}, f32[8,128]{1,0:T(8,128)S(1)}, u32[]{:S(2)}, u32[]{:S(2)}) collective-permute-start(f32[8,128]{1,0:T(8,128)S(1)} %get-tuple-element.22.value_ref), channel_id=1, source_target_pairs={{0,16},{4,20},{8,24},{12,28},{16,0},{20,4},{24,8},{28,12},{1,17},{... | collective-permute-start | bytes 12296 | tf_op jit(solution)/shard_map/ppermute | solution.py:318
  5.9 0.0 copy-start
  5.9 1.3 %collective-permute-start.5 = (f32[16,8,128]{2,1,0:T(8,128)S(1)}, f32[16,8,128]{2,1,0:T(8,128)S(1)}, u32[]{:S(2)}, u32[]{:S(2)}) collective-permute-start(f32[16,8,128]{2,1,0:T(8,128)S(1)} %get-tuple-element.25), channel_id=1, source_target_pairs={{0,1},{1,2},{2,3},{3,0},{4,5},{5,6},{6,7},{7,4},{8,9},{9,10},{10,1... | collective-permute-start | bytes 196616 | tf_op jit(solution)/shard_map/ppermute | solution.py:360
  7.2 1.6 %collective-permute-start.4 = (f32[16,8,128]{2,1,0:T(8,128)S(1)}, f32[16,8,128]{2,1,0:T(8,128)S(1)}, u32[]{:S(2)}, u32[]{:S(2)}) collective-permute-start(f32[16,8,128]{2,1,0:T(8,128)S(1)} %get-tuple-element.25), channel_id=1, source_target_pairs={{0,5},{1,6},{2,7},{3,4},{4,9},{5,10},{6,11},{7,8},{8,13},{9,14},{1... | collective-permute-start | bytes 196616 | tf_op jit(solution)/shard_map/ppermute | solution.py:360
  8.8 0.0 collective-permute-done.arrived_ref
  8.8 0.3 %collective-permute-start.1 = (f32[8,128]{1,0:T(8,128)S(1)}, f32[8,128]{1,0:T(8,128)S(1)}, u32[]{:S(2)}, u32[]{:S(2)}) collective-permute-start(f32[8,128]{1,0:T(8,128)S(1)} %add.2.after_ref.value_ref), channel_id=1, source_target_pairs={{0,8},{4,12},{8,0},{12,4},{16,24},{20,28},{24,16},{28,20},{1,9},{5... | collective-permute-start | bytes 12296 | tf_op jit(solution)/shard_map/ppermute | solution.py:318
  9.1 0.0 copy-done.2
  9.1 0.0 copy-done.3
  9.1 0.0 copy-done.4
  9.1 0.0 copy-done
  9.1 0.4 %copy-done.1 = s32[1,1,2,2]{3,2,1,0:T(2,128)S(1)} copy-done((s32[1,1,2,2]{3,2,1,0:T(2,128)S(1)}, s32[1,1,2,2]{3,2,1,0:T(2,128)}, u32[]{:S(2)}) %copy-start.1) | copy-done | bytes 40
  9.5 0.8 %prepare.1 = (f32[4,16,128]{2,1,0:T(8,128)S(1)}, bf16[128,192]{1,0:T(8,128)(2,1)S(1)}, bf16[64,384]{1,0:T(8,128)(2,1)S(1)}, bf16[2,2,256,256]{3,2,1,0:T(8,128)(2,1)S(1)}) custom-call(s32[1,1,2,2]{3,2,1,0:T(2,128)S(1)} %copy-done.1, f32[4,16]{1,0:T(4,128)S(1)} %bitcast.1, f32[8,128]{1,0:T(8,128)S(1)} %add.2.after_ref.value_ref, f32[128,64]{1,0:T(8,128)S(1)} %copy-done.4, ...), custom_call_target="tpu_custom_call" | custom-call | flops 1000000000 | bytes 100000000 | tf_op jit(solution)/shard_map/prepare/pallas_call | solution.py:380
  10.3 1.1 %collective-permute-done.1.arrived_ref = f32[8,128]{1,0:T(8,128)S(1)} collective-permute-done((f32[8,128]{1,0:T(8,128)S(1)}, f32[8,128]{1,0:T(8,128)S(1)}, u32[]{:S(2)}, u32[]{:S(2)}) %collective-permute-start.1) | collective-permute-done | bytes 4128 | tf_op jit(solution)/shard_map/ppermute | solution.py:318
  11.4 1.2 %collective-permute-start.2 = (f32[8,128]{1,0:T(8,128)S(1)}, f32[8,128]{1,0:T(8,128)S(1)}, u32[]{:S(2)}, u32[]{:S(2)}) collective-permute-start(f32[8,128]{1,0:T(8,128)S(1)} %add.3.after_ref.value_ref), channel_id=1, source_target_pairs={{0,2},{1,3},{2,0},{3,1},{4,6},{5,7},{6,4},{7,5},{8,10},{9,11},{10,... | collective-permute-start | bytes 12296 | tf_op jit(solution)/shard_map/ppermute | solution.py:318
  12.6 0.0 collective-permute-done.5.left_ref
  12.6 0.9 %collective-permute-done.4.corner_ref = f32[16,8,128]{2,1,0:T(8,128)S(1)} collective-permute-done((f32[16,8,128]{2,1,0:T(8,128)S(1)}, f32[16,8,128]{2,1,0:T(8,128)S(1)}, u32[]{:S(2)}, u32[]{:S(2)}) %collective-permute-start.4) | collective-permute-done | bytes 65568 | tf_op jit(solution)/shard_map/ppermute | solution.py:360
  13.4 0.0 collective-permute-done.3.above_ref
  13.4 2.9 %bank.1 = (f32[16,32,128]{2,1,0:T(8,128)S(1)}, f32[520,128]{1,0:T(8,128)S(1)}, f32[136,128]{1,0:T(8,128)S(1)}, f32[136,128]{1,0:T(8,128)S(1)}) custom-call(f32[16,32,128]{2,1,0:T(8,128)S(1)} %get-tuple-element.24.own_ref, f32[16,32,128]{2,1,0:T(8,128)S(1)} %collective-permute-done.3.above_ref, f32[16,8,128]{2,1,0:T(8,128)S(1)} %collective-permute-done.4.corner_ref, ...), custom_call_target="tpu_custom_call" | custom-call | tf_op jit(solution)/shard_map/bank/pallas_call | solution.py:399
  16.3 0.0 collective-permute-done.2.arrived_ref
  16.4 1.1 %collective-permute-start.6 = (f32[520,128]{1,0:T(8,128)S(1)}, f32[520,128]{1,0:T(8,128)S(1)}, u32[]{:S(2)}, u32[]{:S(2)}) collective-permute-start(f32[520,128]{1,0:T(8,128)S(1)} %get-tuple-element.37), channel_id=1, source_target_pairs={{0,28},{1,29},{2,30},{3,31},{4,0},{5,1},{6,2},{7,3},{8,4},{9,5},{1... | collective-permute-start | bytes 798728 | tf_op jit(solution)/shard_map/ppermute | solution.py:360
  17.4 1.8 %collective-permute-start.7 = (f32[136,128]{1,0:T(8,128)S(1)}, f32[136,128]{1,0:T(8,128)S(1)}, u32[]{:S(2)}, u32[]{:S(2)}) collective-permute-start(f32[136,128]{1,0:T(8,128)S(1)} %get-tuple-element.38), channel_id=1, source_target_pairs={{0,3},{1,0},{2,1},{3,2},{4,7},{5,4},{6,5},{7,6},{8,11},{9,8},{10,9... | collective-permute-start | bytes 208904 | tf_op jit(solution)/shard_map/ppermute | solution.py:360
  19.2 0.5 %collective-permute-start.8 = (f32[136,128]{1,0:T(8,128)S(1)}, f32[136,128]{1,0:T(8,128)S(1)}, u32[]{:S(2)}, u32[]{:S(2)}) collective-permute-start(f32[136,128]{1,0:T(8,128)S(1)} %get-tuple-element.39), channel_id=1, source_target_pairs={{0,31},{1,28},{2,29},{3,30},{4,3},{5,0},{6,1},{7,2},{8,7},{9,4},{1... | collective-permute-start | bytes 208904 | tf_op jit(solution)/shard_map/ppermute | solution.py:360
  19.7 0.2 begin.1
  19.9 1.1 %collective-permute-done.7.refs_6_ = f32[136,128]{1,0:T(8,128)S(1)} collective-permute-done((f32[136,128]{1,0:T(8,128)S(1)}, f32[136,128]{1,0:T(8,128)S(1)}, u32[]{:S(2)}, u32[]{:S(2)}) %collective-permute-start.7) | collective-permute-done | bytes 69664 | tf_op jit(solution)/shard_map/ppermute | solution.py:360
  21.0 2.9 %collective-permute-done.8.refs_7_ = f32[136,128]{1,0:T(8,128)S(1)} collective-permute-done((f32[136,128]{1,0:T(8,128)S(1)}, f32[136,128]{1,0:T(8,128)S(1)}, u32[]{:S(2)}, u32[]{:S(2)}) %collective-permute-start.8) | collective-permute-done | bytes 69664 | tf_op jit(solution)/shard_map/ppermute | solution.py:360
  23.9 0.0 collective-permute-done.6.refs_5_
  23.9 1.0 %last.1 = (f32[16,32,128]{2,1,0:T(8,128)}, f32[16,32,128]{2,1,0:T(8,128)}) custom-call(f32[16,32,128]{2,1,0:T(8,128)S(1)} %get-tuple-element.21.shifted_ref.refs_0_, f32[4,16,128]{2,1,0:T(8,128)S(1)} %get-tuple-element.23.refs_0_.basis_ref.refs_1_, f32[8,128]{1,0:T(8,128)S(1)} %get-tuple-element.32.after_ref.refs_2_, ...), custom_call_target="tpu_custom_call" | custom-call | tf_op jit(solution)/shard_map/last/pallas_call | solution.py:434
  (4 shorter events, 0.0 us)
Async XLA Ops:
  0.6 8.5 %copy-start.2 = (f32[2,256,256]{2,1,0:T(8,128)S(1)}, f32[2,256,256]{2,1,0:T(8,128)}, u32[]{:S(2)}) copy-start(f32[2,256,256]{2,1,0:T(8,128)} %constant.8.clone.cols_ref) | copy-start | bytes 1572868
  0.6 8.5 %copy-start.3 = (f32[2,64,64]{2,1,0:T(8,128)S(1)}, f32[2,64,64]{2,1,0:T(8,128)}, u32[]{:S(2)}) copy-start(f32[2,64,64]{2,1,0:T(8,128)} %constant.7.clone.rows_t_ref) | copy-start | bytes 98308
  0.7 8.5 %copy-start.4 = (f32[128,64]{1,0:T(8,128)S(1)}, f32[128,64]{1,0:T(8,128)}, u32[]{:S(2)}) copy-start(f32[128,64]{1,0:T(8,128)} %constant.6.clone.rows_ref) | copy-start | bytes 98308
  0.7 12.8 %collective-permute-start.3 = (f32[16,32,128]{2,1,0:T(8,128)}, f32[16,32,128]{2,1,0:T(8,128)S(1)}, u32[]{:S(2)}, u32[]{:S(2)}) collective-permute-start(f32[16,32,128]{2,1,0:T(8,128)} %start_hbm.1), channel_id=1, source_target_pairs={{0,4},{1,5},{2,6},{3,7},{4,8},{5,9},{6,10},{7,11},{8,12},{9,13},{1... | collective-permute-start | bytes 786440 | tf_op jit(solution)/shard_map/ppermute | solution.py:360
  4.6 4.2 %collective-permute-start = (f32[8,128]{1,0:T(8,128)S(1)}, f32[8,128]{1,0:T(8,128)S(1)}, u32[]{:S(2)}, u32[]{:S(2)}) collective-permute-start(f32[8,128]{1,0:T(8,128)S(1)} %get-tuple-element.22.value_ref), channel_id=1, source_target_pairs={{0,16},{4,20},{8,24},{12,28},{16,0},{20,4},{24,8},{28,12},{1,17},{... | collective-permute-start | bytes 12296 | tf_op jit(solution)/shard_map/ppermute | solution.py:318
  5.9 3.2 %copy-start = (f32[16,4]{0,1:T(4,128)S(1)}, f32[16,4]{0,1:T(4,128)}, u32[]{:S(2)}) copy-start(f32[16,4]{0,1:T(4,128)} %param.11) | copy-start | bytes 772
  5.9 6.7 %collective-permute-start.5 = (f32[16,8,128]{2,1,0:T(8,128)S(1)}, f32[16,8,128]{2,1,0:T(8,128)S(1)}, u32[]{:S(2)}, u32[]{:S(2)}) collective-permute-start(f32[16,8,128]{2,1,0:T(8,128)S(1)} %get-tuple-element.25), channel_id=1, source_target_pairs={{0,1},{1,2},{2,3},{3,0},{4,5},{5,6},{6,7},{7,4},{8,9},{9,10},{10,1... | collective-permute-start | bytes 196616 | tf_op jit(solution)/shard_map/ppermute | solution.py:360
  7.2 6.3 %collective-permute-start.4 = (f32[16,8,128]{2,1,0:T(8,128)S(1)}, f32[16,8,128]{2,1,0:T(8,128)S(1)}, u32[]{:S(2)}, u32[]{:S(2)}) collective-permute-start(f32[16,8,128]{2,1,0:T(8,128)S(1)} %get-tuple-element.25), channel_id=1, source_target_pairs={{0,5},{1,6},{2,7},{3,4},{4,9},{5,10},{6,11},{7,8},{8,13},{9,14},{1... | collective-permute-start | bytes 196616 | tf_op jit(solution)/shard_map/ppermute | solution.py:360
  8.8 0.7 %copy-start.1 = (s32[1,1,2,2]{3,2,1,0:T(2,128)S(1)}, s32[1,1,2,2]{3,2,1,0:T(2,128)}, u32[]{:S(2)}) copy-start(s32[1,1,2,2]{3,2,1,0:T(2,128)} %margin_ref.1) | copy-start | bytes 52
  8.8 2.5 %collective-permute-start.1 = (f32[8,128]{1,0:T(8,128)S(1)}, f32[8,128]{1,0:T(8,128)S(1)}, u32[]{:S(2)}, u32[]{:S(2)}) collective-permute-start(f32[8,128]{1,0:T(8,128)S(1)} %add.2.after_ref.value_ref), channel_id=1, source_target_pairs={{0,8},{4,12},{8,0},{12,4},{16,24},{20,28},{24,16},{28,20},{1,9},{5... | collective-permute-start | bytes 12296 | tf_op jit(solution)/shard_map/ppermute | solution.py:318
  11.4 5.0 %collective-permute-start.2 = (f32[8,128]{1,0:T(8,128)S(1)}, f32[8,128]{1,0:T(8,128)S(1)}, u32[]{:S(2)}, u32[]{:S(2)}) collective-permute-start(f32[8,128]{1,0:T(8,128)S(1)} %add.3.after_ref.value_ref), channel_id=1, source_target_pairs={{0,2},{1,3},{2,0},{3,1},{4,6},{5,7},{6,4},{7,5},{8,10},{9,11},{10,... | collective-permute-start | bytes 12296 | tf_op jit(solution)/shard_map/ppermute | solution.py:318
  16.4 7.5 %collective-permute-start.6 = (f32[520,128]{1,0:T(8,128)S(1)}, f32[520,128]{1,0:T(8,128)S(1)}, u32[]{:S(2)}, u32[]{:S(2)}) collective-permute-start(f32[520,128]{1,0:T(8,128)S(1)} %get-tuple-element.37), channel_id=1, source_target_pairs={{0,28},{1,29},{2,30},{3,31},{4,0},{5,1},{6,2},{7,3},{8,4},{9,5},{1... | collective-permute-start | bytes 798728 | tf_op jit(solution)/shard_map/ppermute | solution.py:360
  17.4 3.5 %collective-permute-start.7 = (f32[136,128]{1,0:T(8,128)S(1)}, f32[136,128]{1,0:T(8,128)S(1)}, u32[]{:S(2)}, u32[]{:S(2)}) collective-permute-start(f32[136,128]{1,0:T(8,128)S(1)} %get-tuple-element.38), channel_id=1, source_target_pairs={{0,3},{1,0},{2,1},{3,2},{4,7},{5,4},{6,5},{7,6},{8,11},{9,8},{10,9... | collective-permute-start | bytes 208904 | tf_op jit(solution)/shard_map/ppermute | solution.py:360
  19.2 4.6 %collective-permute-start.8 = (f32[136,128]{1,0:T(8,128)S(1)}, f32[136,128]{1,0:T(8,128)S(1)}, u32[]{:S(2)}, u32[]{:S(2)}) collective-permute-start(f32[136,128]{1,0:T(8,128)S(1)} %get-tuple-element.39), channel_id=1, source_target_pairs={{0,31},{1,28},{2,29},{3,30},{4,3},{5,0},{6,1},{7,2},{8,7},{9,4},{1... | collective-permute-start | bytes 208904 | tf_op jit(solution)/shard_map/ppermute | solution.py:360

commit v8 on v7

--- a/solution.py
+++ b/solution.py
@@ -259,9 +259,19 @@
 
 def last_kernel(
     radius, shifted_ref, basis_ref, energy_ref, plain_ref, scaled_ref, below_ref, right_ref, corner_ref,
-    image_ref, dual_ref,
+    image_hbm, dual_hbm, image_ref, dual_ref, sems,
 ):
     channels, rows, cols = shifted_ref.shape
+    parts = sems.shape[1]
+    size = channels // parts
+    copies = []
+
+    def send(k, part):
+        at = pl.ds(part * size, size)
+        source, target = ((dual_ref, dual_hbm), (image_ref, image_hbm))[k]
+        copies.append(pltpu.make_async_copy(source.at[at], target.at[at], sems.at[k, part]))
+        copies[-1].start()
+
     rank = basis_ref.shape[0]
     groups = rows // 8
     energy = energy_ref[...]
@@ -274,6 +284,9 @@
     weights = [jnp.zeros((rows, cols), jnp.float32) for r in range(rank)]
     for c in range(channels):
         dual_ref[c] = factor * shifted_ref[c]
+        if (c + 1) % size == 0:
+            send(0, c // size)
+    for c in range(channels):
         strip = right_ref[8 * c : 8 * (c + 1)] + corner_ref[8 * c : 8 * (c + 1)]
         strip = unpack_rows(strip, cols - BORDER, groups)
         prior = below_ref[BORDER * c : BORDER * (c + 1)] + jnp.where(edge, strip, 0.0)
@@ -286,6 +299,10 @@
         for r in range(1, rank):
             total = total + basis_ref[r, c : c + 1, :] * weights[r]
         image_ref[c] = jnp.maximum(total, 0.0)
+        if (c + 1) % size == 0:
+            send(1, c // size)
+    for copy in copies:
+        copy.wait()
 
 
 def shift(axis_sizes, steps):
@@ -435,6 +452,12 @@
         last,
         out_shape=(image_shape, image_shape),
         in_specs=[vmem] * 8,
+        out_specs=(hbm, hbm),
+        scratch_shapes=[
+            pltpu.VMEM(image_shape.shape, f32),
+            pltpu.VMEM(image_shape.shape, f32),
+            pltpu.SemaphoreType.DMA((2, 2)),
+        ],
         compiler_params=params,
         name="last",
     )(shifted, basis, energy, plain, scaled, below, right, corner_back)

time: 25 us -> 25 us (level)
  no operation moved by 1% of the time
where the time goes in v8:
time: 25 us; the launch traced here: 24.8 us
  starting transfers between devices  11.7 us (47%)
  Pallas kernels  6.12 us (24%)
  waiting for transfers between devices  5.9 us (24%)
  between operations  0.7 us (3%)
  local copies, waits for them, and re-layouts  0.42 us (2%)
    ppermute x6, starting transfers between devices, moved(): return lax.ppermute(value, ('fy', 'fx'), shift(sizes, steps))  8.94 us
    ppermute x6, waiting for transfers between devices, moved(): return lax.ppermute(value, ('fy', 'fx'), shift(sizes, steps))  4.83 us
    pallas_call x1, Pallas kernels, per_device(): pl.pallas_call(bank_kernel, out_shape=(image_shape, above_shape, strip_sh...  2.89 us
    ppermute x3, starting transfers between devices, partner(): lax.ppermute(value, axis, [(i, i ^ step) for i in range(lax.axis_size(axi...  2.76 us
    pallas_call x1, Pallas kernels, per_device(): pl.pallas_call(first_kernel, out_shape=(jax.ShapeDtypeStruct((8, cols), f...  1.26 us
    ppermute x3, waiting for transfers between devices, partner(): lax.ppermute(value, axis, [(i, i ^ step) for i in range(lax.axis_size(axi...  1.07 us
    pallas_call x1, Pallas kernels, per_device(): pl.pallas_call(last, out_shape=(image_shape, image_shape), in_specs=[vmem...  0.97 us
    pallas_call x1, Pallas kernels, per_device(): pl.pallas_call(prepare_kernel, out_shape=(jax.ShapeDtypeStruct((rank, cha...  0.78 us
  transfers between devices with their start and end apart: 9, of which 4 were waited for; matrix products, arithmetic and copies ran while one was open for 0% of the time, Pallas kernels for 21%

profile of v8, /device:TPU:1, one launch (start us, length us, event | category | flops | bytes accessed | tf_op | source)
XLA Modules:
  0.0 24.8 jit_solution(15441271063453073063)
XLA Ops:
  0.6 0.0 copy-start.2
  0.6 0.0 copy-start.3
  0.7 0.0 copy-start.4
  0.7 2.7 %collective-permute-start.3 = (f32[16,32,128]{2,1,0:T(8,128)}, f32[16,32,128]{2,1,0:T(8,128)S(1)}, u32[]{:S(2)}, u32[]{:S(2)}) collective-permute-start(f32[16,32,128]{2,1,0:T(8,128)} %start_hbm.1), channel_id=1, source_target_pairs={{0,4},{1,5},{2,6},{3,7},{4,8},{5,9},{6,10},{7,11},{8,12},{9,13},{1... | collective-permute-start | bytes 786440 | tf_op jit(solution)/shard_map/ppermute | solution.py:377
  3.3 1.3 %first.1 = (f32[8,128]{1,0:T(8,128)S(1)}, f32[16,8,128]{2,1,0:T(8,128)S(1)}, f32[16,32,128]{2,1,0:T(8,128)S(1)}, f32[16,32,128]{2,1,0:T(8,128)S(1)}, f32[16,32,128]{2,1,0:T(8,128)S(1)}) custom-call(f32[16,32,128]{2,1,0:T(8,128)} %start_hbm.1, f32[16,32,128]{2,1,0:T(8,128)} %dirty_hbm.1, f32[16,32,128]{2,1,0:T(8,128)} %sampling_hbm.1), custom_call_target="tpu_custom_call" | custom-call | tf_op jit(solution)/shard_map/first/pallas_call | solution.py:380
  4.6 1.3 %collective-permute-start = (f32[8,128]{1,0:T(8,128)S(1)}, f32[8,128]{1,0:T(8,128)S(1)}, u32[]{:S(2)}, u32[]{:S(2)}) collective-permute-start(f32[8,128]{1,0:T(8,128)S(1)} %get-tuple-element.22.value_ref), channel_id=1, source_target_pairs={{0,16},{4,20},{8,24},{12,28},{16,0},{20,4},{24,8},{28,12},{1,17},{... | collective-permute-start | bytes 12296 | tf_op jit(solution)/shard_map/ppermute | solution.py:335
  5.9 0.0 copy-start
  5.9 1.3 %collective-permute-start.5 = (f32[16,8,128]{2,1,0:T(8,128)S(1)}, f32[16,8,128]{2,1,0:T(8,128)S(1)}, u32[]{:S(2)}, u32[]{:S(2)}) collective-permute-start(f32[16,8,128]{2,1,0:T(8,128)S(1)} %get-tuple-element.25), channel_id=1, source_target_pairs={{0,1},{1,2},{2,3},{3,0},{4,5},{5,6},{6,7},{7,4},{8,9},{9,10},{10,1... | collective-permute-start | bytes 196616 | tf_op jit(solution)/shard_map/ppermute | solution.py:377
  7.2 1.6 %collective-permute-start.4 = (f32[16,8,128]{2,1,0:T(8,128)S(1)}, f32[16,8,128]{2,1,0:T(8,128)S(1)}, u32[]{:S(2)}, u32[]{:S(2)}) collective-permute-start(f32[16,8,128]{2,1,0:T(8,128)S(1)} %get-tuple-element.25), channel_id=1, source_target_pairs={{0,5},{1,6},{2,7},{3,4},{4,9},{5,10},{6,11},{7,8},{8,13},{9,14},{1... | collective-permute-start | bytes 196616 | tf_op jit(solution)/shard_map/ppermute | solution.py:377
  8.8 0.0 collective-permute-done.arrived_ref
  8.8 0.3 %collective-permute-start.1 = (f32[8,128]{1,0:T(8,128)S(1)}, f32[8,128]{1,0:T(8,128)S(1)}, u32[]{:S(2)}, u32[]{:S(2)}) collective-permute-start(f32[8,128]{1,0:T(8,128)S(1)} %add.2.after_ref.value_ref), channel_id=1, source_target_pairs={{0,8},{4,12},{8,0},{12,4},{16,24},{20,28},{24,16},{28,20},{1,9},{5... | collective-permute-start | bytes 12296 | tf_op jit(solution)/shard_map/ppermute | solution.py:335
  9.1 0.0 copy-done.2
  9.1 0.0 copy-done.3
  9.1 0.0 copy-done.4
  9.1 0.0 copy-done
  9.1 0.4 %copy-done.1 = s32[1,1,2,2]{3,2,1,0:T(2,128)S(1)} copy-done((s32[1,1,2,2]{3,2,1,0:T(2,128)S(1)}, s32[1,1,2,2]{3,2,1,0:T(2,128)}, u32[]{:S(2)}) %copy-start.1) | copy-done | bytes 40
  9.5 0.8 %prepare.1 = (f32[4,16,128]{2,1,0:T(8,128)S(1)}, bf16[128,192]{1,0:T(8,128)(2,1)S(1)}, bf16[64,384]{1,0:T(8,128)(2,1)S(1)}, bf16[2,2,256,256]{3,2,1,0:T(8,128)(2,1)S(1)}) custom-call(s32[1,1,2,2]{3,2,1,0:T(2,128)S(1)} %copy-done.1, f32[4,16]{1,0:T(4,128)S(1)} %bitcast.1, f32[8,128]{1,0:T(8,128)S(1)} %add.2.after_ref.value_ref, f32[128,64]{1,0:T(8,128)S(1)} %copy-done.4, ...), custom_call_target="tpu_custom_call" | custom-call | flops 1000000000 | bytes 100000000 | tf_op jit(solution)/shard_map/prepare/pallas_call | solution.py:397
  10.3 1.1 %collective-permute-done.1.arrived_ref = f32[8,128]{1,0:T(8,128)S(1)} collective-permute-done((f32[8,128]{1,0:T(8,128)S(1)}, f32[8,128]{1,0:T(8,128)S(1)}, u32[]{:S(2)}, u32[]{:S(2)}) %collective-permute-start.1) | collective-permute-done | bytes 4128 | tf_op jit(solution)/shard_map/ppermute | solution.py:335
  11.4 1.2 %collective-permute-start.2 = (f32[8,128]{1,0:T(8,128)S(1)}, f32[8,128]{1,0:T(8,128)S(1)}, u32[]{:S(2)}, u32[]{:S(2)}) collective-permute-start(f32[8,128]{1,0:T(8,128)S(1)} %add.3.after_ref.value_ref), channel_id=1, source_target_pairs={{0,2},{1,3},{2,0},{3,1},{4,6},{5,7},{6,4},{7,5},{8,10},{9,11},{10,... | collective-permute-start | bytes 12296 | tf_op jit(solution)/shard_map/ppermute | solution.py:335
  12.6 0.0 collective-permute-done.5.left_ref
  12.6 0.9 %collective-permute-done.4.corner_ref = f32[16,8,128]{2,1,0:T(8,128)S(1)} collective-permute-done((f32[16,8,128]{2,1,0:T(8,128)S(1)}, f32[16,8,128]{2,1,0:T(8,128)S(1)}, u32[]{:S(2)}, u32[]{:S(2)}) %collective-permute-start.4) | collective-permute-done | bytes 65568 | tf_op jit(solution)/shard_map/ppermute | solution.py:377
  13.4 0.0 collective-permute-done.3.above_ref
  13.4 2.9 %bank.1 = (f32[16,32,128]{2,1,0:T(8,128)S(1)}, f32[520,128]{1,0:T(8,128)S(1)}, f32[136,128]{1,0:T(8,128)S(1)}, f32[136,128]{1,0:T(8,128)S(1)}) custom-call(f32[16,32,128]{2,1,0:T(8,128)S(1)} %get-tuple-element.24.own_ref, f32[16,32,128]{2,1,0:T(8,128)S(1)} %collective-permute-done.3.above_ref, f32[16,8,128]{2,1,0:T(8,128)S(1)} %collective-permute-done.4.corner_ref, ...), custom_call_target="tpu_custom_call" | custom-call | tf_op jit(solution)/shard_map/bank/pallas_call | solution.py:416
  16.3 0.0 collective-permute-done.2.arrived_ref
  16.4 1.1 %collective-permute-start.6 = (f32[520,128]{1,0:T(8,128)S(1)}, f32[520,128]{1,0:T(8,128)S(1)}, u32[]{:S(2)}, u32[]{:S(2)}) collective-permute-start(f32[520,128]{1,0:T(8,128)S(1)} %get-tuple-element.37), channel_id=1, source_target_pairs={{0,28},{1,29},{2,30},{3,31},{4,0},{5,1},{6,2},{7,3},{8,4},{9,5},{1... | collective-permute-start | bytes 798728 | tf_op jit(solution)/shard_map/ppermute | solution.py:377
  17.4 1.8 %collective-permute-start.7 = (f32[136,128]{1,0:T(8,128)S(1)}, f32[136,128]{1,0:T(8,128)S(1)}, u32[]{:S(2)}, u32[]{:S(2)}) collective-permute-start(f32[136,128]{1,0:T(8,128)S(1)} %get-tuple-element.38), channel_id=1, source_target_pairs={{0,3},{1,0},{2,1},{3,2},{4,7},{5,4},{6,5},{7,6},{8,11},{9,8},{10,9... | collective-permute-start | bytes 208904 | tf_op jit(solution)/shard_map/ppermute | solution.py:377
  19.2 0.5 %collective-permute-start.8 = (f32[136,128]{1,0:T(8,128)S(1)}, f32[136,128]{1,0:T(8,128)S(1)}, u32[]{:S(2)}, u32[]{:S(2)}) collective-permute-start(f32[136,128]{1,0:T(8,128)S(1)} %get-tuple-element.39), channel_id=1, source_target_pairs={{0,31},{1,28},{2,29},{3,30},{4,3},{5,0},{6,1},{7,2},{8,7},{9,4},{1... | collective-permute-start | bytes 208904 | tf_op jit(solution)/shard_map/ppermute | solution.py:377
  19.7 0.2 begin.1
  19.9 1.1 %collective-permute-done.7.refs_6_ = f32[136,128]{1,0:T(8,128)S(1)} collective-permute-done((f32[136,128]{1,0:T(8,128)S(1)}, f32[136,128]{1,0:T(8,128)S(1)}, u32[]{:S(2)}, u32[]{:S(2)}) %collective-permute-start.7) | collective-permute-done | bytes 69664 | tf_op jit(solution)/shard_map/ppermute | solution.py:377
  21.0 2.9 %collective-permute-done.8.refs_7_ = f32[136,128]{1,0:T(8,128)S(1)} collective-permute-done((f32[136,128]{1,0:T(8,128)S(1)}, f32[136,128]{1,0:T(8,128)S(1)}, u32[]{:S(2)}, u32[]{:S(2)}) %collective-permute-start.8) | collective-permute-done | bytes 69664 | tf_op jit(solution)/shard_map/ppermute | solution.py:377
  23.9 0.0 collective-permute-done.6.refs_5_
  23.9 1.0 %last.1 = (f32[16,32,128]{2,1,0:T(8,128)}, f32[16,32,128]{2,1,0:T(8,128)}) custom-call(f32[16,32,128]{2,1,0:T(8,128)S(1)} %get-tuple-element.21.shifted_ref.refs_0_, f32[4,16,128]{2,1,0:T(8,128)S(1)} %get-tuple-element.23.refs_0_.basis_ref.refs_1_, f32[8,128]{1,0:T(8,128)S(1)} %get-tuple-element.32.after_ref.refs_2_, ...), custom_call_target="tpu_custom_call" | custom-call | tf_op jit(solution)/shard_map/last/pallas_call | solution.py:451
  (4 shorter events, 0.0 us)
Async XLA Ops:
  0.6 8.5 %copy-start.2 = (f32[2,256,256]{2,1,0:T(8,128)S(1)}, f32[2,256,256]{2,1,0:T(8,128)}, u32[]{:S(2)}) copy-start(f32[2,256,256]{2,1,0:T(8,128)} %constant.8.clone.cols_ref) | copy-start | bytes 1572868
  0.6 8.5 %copy-start.3 = (f32[2,64,64]{2,1,0:T(8,128)S(1)}, f32[2,64,64]{2,1,0:T(8,128)}, u32[]{:S(2)}) copy-start(f32[2,64,64]{2,1,0:T(8,128)} %constant.7.clone.rows_t_ref) | copy-start | bytes 98308
  0.7 8.5 %copy-start.4 = (f32[128,64]{1,0:T(8,128)S(1)}, f32[128,64]{1,0:T(8,128)}, u32[]{:S(2)}) copy-start(f32[128,64]{1,0:T(8,128)} %constant.6.clone.rows_ref) | copy-start | bytes 98308
  0.7 12.8 %collective-permute-start.3 = (f32[16,32,128]{2,1,0:T(8,128)}, f32[16,32,128]{2,1,0:T(8,128)S(1)}, u32[]{:S(2)}, u32[]{:S(2)}) collective-permute-start(f32[16,32,128]{2,1,0:T(8,128)} %start_hbm.1), channel_id=1, source_target_pairs={{0,4},{1,5},{2,6},{3,7},{4,8},{5,9},{6,10},{7,11},{8,12},{9,13},{1... | collective-permute-start | bytes 786440 | tf_op jit(solution)/shard_map/ppermute | solution.py:377
  4.6 4.2 %collective-permute-start = (f32[8,128]{1,0:T(8,128)S(1)}, f32[8,128]{1,0:T(8,128)S(1)}, u32[]{:S(2)}, u32[]{:S(2)}) collective-permute-start(f32[8,128]{1,0:T(8,128)S(1)} %get-tuple-element.22.value_ref), channel_id=1, source_target_pairs={{0,16},{4,20},{8,24},{12,28},{16,0},{20,4},{24,8},{28,12},{1,17},{... | collective-permute-start | bytes 12296 | tf_op jit(solution)/shard_map/ppermute | solution.py:335
  5.9 3.2 %copy-start = (f32[16,4]{0,1:T(4,128)S(1)}, f32[16,4]{0,1:T(4,128)}, u32[]{:S(2)}) copy-start(f32[16,4]{0,1:T(4,128)} %param.11) | copy-start | bytes 772
  5.9 6.7 %collective-permute-start.5 = (f32[16,8,128]{2,1,0:T(8,128)S(1)}, f32[16,8,128]{2,1,0:T(8,128)S(1)}, u32[]{:S(2)}, u32[]{:S(2)}) collective-permute-start(f32[16,8,128]{2,1,0:T(8,128)S(1)} %get-tuple-element.25), channel_id=1, source_target_pairs={{0,1},{1,2},{2,3},{3,0},{4,5},{5,6},{6,7},{7,4},{8,9},{9,10},{10,1... | collective-permute-start | bytes 196616 | tf_op jit(solution)/shard_map/ppermute | solution.py:377
  7.2 6.3 %collective-permute-start.4 = (f32[16,8,128]{2,1,0:T(8,128)S(1)}, f32[16,8,128]{2,1,0:T(8,128)S(1)}, u32[]{:S(2)}, u32[]{:S(2)}) collective-permute-start(f32[16,8,128]{2,1,0:T(8,128)S(1)} %get-tuple-element.25), channel_id=1, source_target_pairs={{0,5},{1,6},{2,7},{3,4},{4,9},{5,10},{6,11},{7,8},{8,13},{9,14},{1... | collective-permute-start | bytes 196616 | tf_op jit(solution)/shard_map/ppermute | solution.py:377
  8.8 0.7 %copy-start.1 = (s32[1,1,2,2]{3,2,1,0:T(2,128)S(1)}, s32[1,1,2,2]{3,2,1,0:T(2,128)}, u32[]{:S(2)}) copy-start(s32[1,1,2,2]{3,2,1,0:T(2,128)} %margin_ref.1) | copy-start | bytes 52
  8.8 2.5 %collective-permute-start.1 = (f32[8,128]{1,0:T(8,128)S(1)}, f32[8,128]{1,0:T(8,128)S(1)}, u32[]{:S(2)}, u32[]{:S(2)}) collective-permute-start(f32[8,128]{1,0:T(8,128)S(1)} %add.2.after_ref.value_ref), channel_id=1, source_target_pairs={{0,8},{4,12},{8,0},{12,4},{16,24},{20,28},{24,16},{28,20},{1,9},{5... | collective-permute-start | bytes 12296 | tf_op jit(solution)/shard_map/ppermute | solution.py:335
  11.4 5.0 %collective-permute-start.2 = (f32[8,128]{1,0:T(8,128)S(1)}, f32[8,128]{1,0:T(8,128)S(1)}, u32[]{:S(2)}, u32[]{:S(2)}) collective-permute-start(f32[8,128]{1,0:T(8,128)S(1)} %add.3.after_ref.value_ref), channel_id=1, source_target_pairs={{0,2},{1,3},{2,0},{3,1},{4,6},{5,7},{6,4},{7,5},{8,10},{9,11},{10,... | collective-permute-start | bytes 12296 | tf_op jit(solution)/shard_map/ppermute | solution.py:335
  16.4 7.5 %collective-permute-start.6 = (f32[520,128]{1,0:T(8,128)S(1)}, f32[520,128]{1,0:T(8,128)S(1)}, u32[]{:S(2)}, u32[]{:S(2)}) collective-permute-start(f32[520,128]{1,0:T(8,128)S(1)} %get-tuple-element.37), channel_id=1, source_target_pairs={{0,28},{1,29},{2,30},{3,31},{4,0},{5,1},{6,2},{7,3},{8,4},{9,5},{1... | collective-permute-start | bytes 798728 | tf_op jit(solution)/shard_map/ppermute | solution.py:377
  17.4 3.5 %collective-permute-start.7 = (f32[136,128]{1,0:T(8,128)S(1)}, f32[136,128]{1,0:T(8,128)S(1)}, u32[]{:S(2)}, u32[]{:S(2)}) collective-permute-start(f32[136,128]{1,0:T(8,128)S(1)} %get-tuple-element.38), channel_id=1, source_target_pairs={{0,3},{1,0},{2,1},{3,2},{4,7},{5,4},{6,5},{7,6},{8,11},{9,8},{10,9... | collective-permute-start | bytes 208904 | tf_op jit(solution)/shard_map/ppermute | solution.py:377
  19.2 4.6 %collective-permute-start.8 = (f32[136,128]{1,0:T(8,128)S(1)}, f32[136,128]{1,0:T(8,128)S(1)}, u32[]{:S(2)}, u32[]{:S(2)}) collective-permute-start(f32[136,128]{1,0:T(8,128)S(1)} %get-tuple-element.39), channel_id=1, source_target_pairs={{0,31},{1,28},{2,29},{3,30},{4,3},{5,0},{6,1},{7,2},{8,7},{9,4},{1... | collective-permute-start | bytes 208904 | tf_op jit(solution)/shard_map/ppermute | solution.py:377

commit v9 on v8

--- a/solution.py
+++ b/solution.py
@@ -191,7 +191,7 @@
 
 
 def bank_kernel(
-    own_ref, above_ref, corner_ref, left_ref, a_ref, at_ref, g_ref, after_ref,
+    own_ref, corner_ref, left_ref, above_ref, a_ref, at_ref, g_ref, after_ref,
     own_out, above_out, left_out, corner_out, z_high, z_low, u_high, u_low,
 ):
     channels, rows, cols = own_out.shape
@@ -421,7 +421,7 @@
         scratch_shapes=[pltpu.VMEM((LEVELS, channels, half, wide), bf16)] * 4,
         compiler_params=params,
         name="bank",
-    )(own, above, corner, left, a, a_t, g, energy)
+    )(own, corner, left, above, a, a_t, g, energy)
     energy, *parts = pl.pallas_call(
         stamp_kernel,
         out_shape=(jax.ShapeDtypeStruct(energy.shape, f32), above_shape, strip_shape, strip_shape),

time: 25 us -> 25 us (level)
  no operation moved by 1% of the time
where the time goes in v9:
time: 25 us; the launch traced here: 24.8 us
  starting transfers between devices  11.7 us (47%)
  Pallas kernels  6.13 us (25%)
  waiting for transfers between devices  5.9 us (24%)
  between operations  0.7 us (3%)
  local copies, waits for them, and re-layouts  0.42 us (2%)
    ppermute x6, starting transfers between devices, moved(): return lax.ppermute(value, ('fy', 'fx'), shift(sizes, steps))  8.94 us
    ppermute x6, waiting for transfers between devices, moved(): return lax.ppermute(value, ('fy', 'fx'), shift(sizes, steps))  4.83 us
    pallas_call x1, Pallas kernels, per_device(): pl.pallas_call(bank_kernel, out_shape=(image_shape, above_shape, strip_sh...  2.9 us
    ppermute x3, starting transfers between devices, partner(): lax.ppermute(value, axis, [(i, i ^ step) for i in range(lax.axis_size(axi...  2.76 us
    pallas_call x1, Pallas kernels, per_device(): pl.pallas_call(first_kernel, out_shape=(jax.ShapeDtypeStruct((8, cols), f...  1.26 us
    ppermute x3, waiting for transfers between devices, partner(): lax.ppermute(value, axis, [(i, i ^ step) for i in range(lax.axis_size(axi...  1.07 us
    pallas_call x1, Pallas kernels, per_device(): pl.pallas_call(last, out_shape=(image_shape, image_shape), in_specs=[vmem...  0.97 us
    pallas_call x1, Pallas kernels, per_device(): pl.pallas_call(prepare_kernel, out_shape=(jax.ShapeDtypeStruct((rank, cha...  0.78 us
  transfers between devices with their start and end apart: 9, of which 4 were waited for; matrix products, arithmetic and copies ran while one was open for 0% of the time, Pallas kernels for 21%

profile of v9, /device:TPU:1, one launch (start us, length us, event | category | flops | bytes accessed | tf_op | source)
XLA Modules:
  0.0 24.8 jit_solution(12708355404154332281)
XLA Ops:
  0.6 0.0 copy-start.2
  0.6 0.0 copy-start.3
  0.7 0.0 copy-start.4
  0.7 2.7 %collective-permute-start.5 = (f32[16,32,128]{2,1,0:T(8,128)}, f32[16,32,128]{2,1,0:T(8,128)S(1)}, u32[]{:S(2)}, u32[]{:S(2)}) collective-permute-start(f32[16,32,128]{2,1,0:T(8,128)} %start_hbm.1), channel_id=1, source_target_pairs={{0,4},{1,5},{2,6},{3,7},{4,8},{5,9},{6,10},{7,11},{8,12},{9,13},{1... | collective-permute-start | bytes 786440 | tf_op jit(solution)/shard_map/ppermute | solution.py:377
  3.3 1.3 %first.1 = (f32[8,128]{1,0:T(8,128)S(1)}, f32[16,8,128]{2,1,0:T(8,128)S(1)}, f32[16,32,128]{2,1,0:T(8,128)S(1)}, f32[16,32,128]{2,1,0:T(8,128)S(1)}, f32[16,32,128]{2,1,0:T(8,128)S(1)}) custom-call(f32[16,32,128]{2,1,0:T(8,128)} %start_hbm.1, f32[16,32,128]{2,1,0:T(8,128)} %dirty_hbm.1, f32[16,32,128]{2,1,0:T(8,128)} %sampling_hbm.1), custom_call_target="tpu_custom_call" | custom-call | tf_op jit(solution)/shard_map/first/pallas_call | solution.py:380
  4.6 1.3 %collective-permute-start = (f32[8,128]{1,0:T(8,128)S(1)}, f32[8,128]{1,0:T(8,128)S(1)}, u32[]{:S(2)}, u32[]{:S(2)}) collective-permute-start(f32[8,128]{1,0:T(8,128)S(1)} %get-tuple-element.22.value_ref), channel_id=1, source_target_pairs={{0,16},{4,20},{8,24},{12,28},{16,0},{20,4},{24,8},{28,12},{1,17},{... | collective-permute-start | bytes 12296 | tf_op jit(solution)/shard_map/ppermute | solution.py:335
  5.9 0.0 copy-start
  5.9 1.3 %collective-permute-start.4 = (f32[16,8,128]{2,1,0:T(8,128)S(1)}, f32[16,8,128]{2,1,0:T(8,128)S(1)}, u32[]{:S(2)}, u32[]{:S(2)}) collective-permute-start(f32[16,8,128]{2,1,0:T(8,128)S(1)} %get-tuple-element.25), channel_id=1, source_target_pairs={{0,1},{1,2},{2,3},{3,0},{4,5},{5,6},{6,7},{7,4},{8,9},{9,10},{10,1... | collective-permute-start | bytes 196616 | tf_op jit(solution)/shard_map/ppermute | solution.py:377
  7.2 1.6 %collective-permute-start.3 = (f32[16,8,128]{2,1,0:T(8,128)S(1)}, f32[16,8,128]{2,1,0:T(8,128)S(1)}, u32[]{:S(2)}, u32[]{:S(2)}) collective-permute-start(f32[16,8,128]{2,1,0:T(8,128)S(1)} %get-tuple-element.25), channel_id=1, source_target_pairs={{0,5},{1,6},{2,7},{3,4},{4,9},{5,10},{6,11},{7,8},{8,13},{9,14},{1... | collective-permute-start | bytes 196616 | tf_op jit(solution)/shard_map/ppermute | solution.py:377
  8.8 0.0 collective-permute-done.arrived_ref
  8.8 0.3 %collective-permute-start.1 = (f32[8,128]{1,0:T(8,128)S(1)}, f32[8,128]{1,0:T(8,128)S(1)}, u32[]{:S(2)}, u32[]{:S(2)}) collective-permute-start(f32[8,128]{1,0:T(8,128)S(1)} %add.2.after_ref.value_ref), channel_id=1, source_target_pairs={{0,8},{4,12},{8,0},{12,4},{16,24},{20,28},{24,16},{28,20},{1,9},{5... | collective-permute-start | bytes 12296 | tf_op jit(solution)/shard_map/ppermute | solution.py:335
  9.1 0.0 copy-done.2
  9.1 0.0 copy-done.3
  9.1 0.0 copy-done.4
  9.1 0.0 copy-done
  9.1 0.4 %copy-done.1 = s32[1,1,2,2]{3,2,1,0:T(2,128)S(1)} copy-done((s32[1,1,2,2]{3,2,1,0:T(2,128)S(1)}, s32[1,1,2,2]{3,2,1,0:T(2,128)}, u32[]{:S(2)}) %copy-start.1) | copy-done | bytes 40
  9.5 0.8 %prepare.1 = (f32[4,16,128]{2,1,0:T(8,128)S(1)}, bf16[128,192]{1,0:T(8,128)(2,1)S(1)}, bf16[64,384]{1,0:T(8,128)(2,1)S(1)}, bf16[2,2,256,256]{3,2,1,0:T(8,128)(2,1)S(1)}) custom-call(s32[1,1,2,2]{3,2,1,0:T(2,128)S(1)} %copy-done.1, f32[4,16]{1,0:T(4,128)S(1)} %bitcast.1, f32[8,128]{1,0:T(8,128)S(1)} %add.2.after_ref.value_ref, f32[128,64]{1,0:T(8,128)S(1)} %copy-done.4, ...), custom_call_target="tpu_custom_call" | custom-call | flops 1000000000 | bytes 100000000 | tf_op jit(solution)/shard_map/prepare/pallas_call | solution.py:397
  10.3 1.1 %collective-permute-done.1.arrived_ref = f32[8,128]{1,0:T(8,128)S(1)} collective-permute-done((f32[8,128]{1,0:T(8,128)S(1)}, f32[8,128]{1,0:T(8,128)S(1)}, u32[]{:S(2)}, u32[]{:S(2)}) %collective-permute-start.1) | collective-permute-done | bytes 4128 | tf_op jit(solution)/shard_map/ppermute | solution.py:335
  11.4 1.2 %collective-permute-start.2 = (f32[8,128]{1,0:T(8,128)S(1)}, f32[8,128]{1,0:T(8,128)S(1)}, u32[]{:S(2)}, u32[]{:S(2)}) collective-permute-start(f32[8,128]{1,0:T(8,128)S(1)} %add.3.after_ref.value_ref), channel_id=1, source_target_pairs={{0,2},{1,3},{2,0},{3,1},{4,6},{5,7},{6,4},{7,5},{8,10},{9,11},{10,... | collective-permute-start | bytes 12296 | tf_op jit(solution)/shard_map/ppermute | solution.py:335
  12.6 0.0 collective-permute-done.4.left_ref
  12.6 0.9 %collective-permute-done.3.corner_ref = f32[16,8,128]{2,1,0:T(8,128)S(1)} collective-permute-done((f32[16,8,128]{2,1,0:T(8,128)S(1)}, f32[16,8,128]{2,1,0:T(8,128)S(1)}, u32[]{:S(2)}, u32[]{:S(2)}) %collective-permute-start.3) | collective-permute-done | bytes 65568 | tf_op jit(solution)/shard_map/ppermute | solution.py:377
  13.4 0.0 collective-permute-done.5.above_ref
  13.4 2.9 %bank.1 = (f32[16,32,128]{2,1,0:T(8,128)S(1)}, f32[520,128]{1,0:T(8,128)S(1)}, f32[136,128]{1,0:T(8,128)S(1)}, f32[136,128]{1,0:T(8,128)S(1)}) custom-call(f32[16,32,128]{2,1,0:T(8,128)S(1)} %get-tuple-element.24.own_ref, f32[16,8,128]{2,1,0:T(8,128)S(1)} %collective-permute-done.3.corner_ref, f32[16,8,128]{2,1,0:T(8,128)S(1)} %collective-permute-done.4.left_ref, ...), custom_call_target="tpu_custom_call" | custom-call | tf_op jit(solution)/shard_map/bank/pallas_call | solution.py:416
  16.3 0.0 collective-permute-done.2.arrived_ref
  16.4 1.1 %collective-permute-start.6 = (f32[520,128]{1,0:T(8,128)S(1)}, f32[520,128]{1,0:T(8,128)S(1)}, u32[]{:S(2)}, u32[]{:S(2)}) collective-permute-start(f32[520,128]{1,0:T(8,128)S(1)} %get-tuple-element.37), channel_id=1, source_target_pairs={{0,28},{1,29},{2,30},{3,31},{4,0},{5,1},{6,2},{7,3},{8,4},{9,5},{1... | collective-permute-start | bytes 798728 | tf_op jit(solution)/shard_map/ppermute | solution.py:377
  17.4 1.8 %collective-permute-start.7 = (f32[136,128]{1,0:T(8,128)S(1)}, f32[136,128]{1,0:T(8,128)S(1)}, u32[]{:S(2)}, u32[]{:S(2)}) collective-permute-start(f32[136,128]{1,0:T(8,128)S(1)} %get-tuple-element.38), channel_id=1, source_target_pairs={{0,3},{1,0},{2,1},{3,2},{4,7},{5,4},{6,5},{7,6},{8,11},{9,8},{10,9... | collective-permute-start | bytes 208904 | tf_op jit(solution)/shard_map/ppermute | solution.py:377
  19.2 0.5 %collective-permute-start.8 = (f32[136,128]{1,0:T(8,128)S(1)}, f32[136,128]{1,0:T(8,128)S(1)}, u32[]{:S(2)}, u32[]{:S(2)}) collective-permute-start(f32[136,128]{1,0:T(8,128)S(1)} %get-tuple-element.39), channel_id=1, source_target_pairs={{0,31},{1,28},{2,29},{3,30},{4,3},{5,0},{6,1},{7,2},{8,7},{9,4},{1... | collective-permute-start | bytes 208904 | tf_op jit(solution)/shard_map/ppermute | solution.py:377
  19.7 0.2 begin.1
  19.9 1.1 %collective-permute-done.7.refs_6_ = f32[136,128]{1,0:T(8,128)S(1)} collective-permute-done((f32[136,128]{1,0:T(8,128)S(1)}, f32[136,128]{1,0:T(8,128)S(1)}, u32[]{:S(2)}, u32[]{:S(2)}) %collective-permute-start.7) | collective-permute-done | bytes 69664 | tf_op jit(solution)/shard_map/ppermute | solution.py:377
  21.0 2.9 %collective-permute-done.8.refs_7_ = f32[136,128]{1,0:T(8,128)S(1)} collective-permute-done((f32[136,128]{1,0:T(8,128)S(1)}, f32[136,128]{1,0:T(8,128)S(1)}, u32[]{:S(2)}, u32[]{:S(2)}) %collective-permute-start.8) | collective-permute-done | bytes 69664 | tf_op jit(solution)/shard_map/ppermute | solution.py:377
  23.9 0.0 collective-permute-done.6.refs_5_
  23.9 1.0 %last.1 = (f32[16,32,128]{2,1,0:T(8,128)}, f32[16,32,128]{2,1,0:T(8,128)}) custom-call(f32[16,32,128]{2,1,0:T(8,128)S(1)} %get-tuple-element.21.shifted_ref.refs_0_, f32[4,16,128]{2,1,0:T(8,128)S(1)} %get-tuple-element.23.refs_0_.basis_ref.refs_1_, f32[8,128]{1,0:T(8,128)S(1)} %get-tuple-element.32.after_ref.refs_2_, ...), custom_call_target="tpu_custom_call" | custom-call | tf_op jit(solution)/shard_map/last/pallas_call | solution.py:451
  (4 shorter events, 0.0 us)
Async XLA Ops:
  0.6 8.5 %copy-start.2 = (f32[2,256,256]{2,1,0:T(8,128)S(1)}, f32[2,256,256]{2,1,0:T(8,128)}, u32[]{:S(2)}) copy-start(f32[2,256,256]{2,1,0:T(8,128)} %constant.8.clone.cols_ref) | copy-start | bytes 1572868
  0.6 8.5 %copy-start.3 = (f32[2,64,64]{2,1,0:T(8,128)S(1)}, f32[2,64,64]{2,1,0:T(8,128)}, u32[]{:S(2)}) copy-start(f32[2,64,64]{2,1,0:T(8,128)} %constant.7.clone.rows_t_ref) | copy-start | bytes 98308
  0.7 8.5 %copy-start.4 = (f32[128,64]{1,0:T(8,128)S(1)}, f32[128,64]{1,0:T(8,128)}, u32[]{:S(2)}) copy-start(f32[128,64]{1,0:T(8,128)} %constant.6.clone.rows_ref) | copy-start | bytes 98308
  0.7 12.8 %collective-permute-start.5 = (f32[16,32,128]{2,1,0:T(8,128)}, f32[16,32,128]{2,1,0:T(8,128)S(1)}, u32[]{:S(2)}, u32[]{:S(2)}) collective-permute-start(f32[16,32,128]{2,1,0:T(8,128)} %start_hbm.1), channel_id=1, source_target_pairs={{0,4},{1,5},{2,6},{3,7},{4,8},{5,9},{6,10},{7,11},{8,12},{9,13},{1... | collective-permute-start | bytes 786440 | tf_op jit(solution)/shard_map/ppermute | solution.py:377
  4.6 4.2 %collective-permute-start = (f32[8,128]{1,0:T(8,128)S(1)}, f32[8,128]{1,0:T(8,128)S(1)}, u32[]{:S(2)}, u32[]{:S(2)}) collective-permute-start(f32[8,128]{1,0:T(8,128)S(1)} %get-tuple-element.22.value_ref), channel_id=1, source_target_pairs={{0,16},{4,20},{8,24},{12,28},{16,0},{20,4},{24,8},{28,12},{1,17},{... | collective-permute-start | bytes 12296 | tf_op jit(solution)/shard_map/ppermute | solution.py:335
  5.9 3.2 %copy-start = (f32[16,4]{0,1:T(4,128)S(1)}, f32[16,4]{0,1:T(4,128)}, u32[]{:S(2)}) copy-start(f32[16,4]{0,1:T(4,128)} %param.11) | copy-start | bytes 772
  5.9 6.7 %collective-permute-start.4 = (f32[16,8,128]{2,1,0:T(8,128)S(1)}, f32[16,8,128]{2,1,0:T(8,128)S(1)}, u32[]{:S(2)}, u32[]{:S(2)}) collective-permute-start(f32[16,8,128]{2,1,0:T(8,128)S(1)} %get-tuple-element.25), channel_id=1, source_target_pairs={{0,1},{1,2},{2,3},{3,0},{4,5},{5,6},{6,7},{7,4},{8,9},{9,10},{10,1... | collective-permute-start | bytes 196616 | tf_op jit(solution)/shard_map/ppermute | solution.py:377
  7.2 6.3 %collective-permute-start.3 = (f32[16,8,128]{2,1,0:T(8,128)S(1)}, f32[16,8,128]{2,1,0:T(8,128)S(1)}, u32[]{:S(2)}, u32[]{:S(2)}) collective-permute-start(f32[16,8,128]{2,1,0:T(8,128)S(1)} %get-tuple-element.25), channel_id=1, source_target_pairs={{0,5},{1,6},{2,7},{3,4},{4,9},{5,10},{6,11},{7,8},{8,13},{9,14},{1... | collective-permute-start | bytes 196616 | tf_op jit(solution)/shard_map/ppermute | solution.py:377
  8.8 0.7 %copy-start.1 = (s32[1,1,2,2]{3,2,1,0:T(2,128)S(1)}, s32[1,1,2,2]{3,2,1,0:T(2,128)}, u32[]{:S(2)}) copy-start(s32[1,1,2,2]{3,2,1,0:T(2,128)} %margin_ref.1) | copy-start | bytes 52
  8.8 2.5 %collective-permute-start.1 = (f32[8,128]{1,0:T(8,128)S(1)}, f32[8,128]{1,0:T(8,128)S(1)}, u32[]{:S(2)}, u32[]{:S(2)}) collective-permute-start(f32[8,128]{1,0:T(8,128)S(1)} %add.2.after_ref.value_ref), channel_id=1, source_target_pairs={{0,8},{4,12},{8,0},{12,4},{16,24},{20,28},{24,16},{28,20},{1,9},{5... | collective-permute-start | bytes 12296 | tf_op jit(solution)/shard_map/ppermute | solution.py:335
  11.4 5.0 %collective-permute-start.2 = (f32[8,128]{1,0:T(8,128)S(1)}, f32[8,128]{1,0:T(8,128)S(1)}, u32[]{:S(2)}, u32[]{:S(2)}) collective-permute-start(f32[8,128]{1,0:T(8,128)S(1)} %add.3.after_ref.value_ref), channel_id=1, source_target_pairs={{0,2},{1,3},{2,0},{3,1},{4,6},{5,7},{6,4},{7,5},{8,10},{9,11},{10,... | collective-permute-start | bytes 12296 | tf_op jit(solution)/shard_map/ppermute | solution.py:335
  16.4 7.5 %collective-permute-start.6 = (f32[520,128]{1,0:T(8,128)S(1)}, f32[520,128]{1,0:T(8,128)S(1)}, u32[]{:S(2)}, u32[]{:S(2)}) collective-permute-start(f32[520,128]{1,0:T(8,128)S(1)} %get-tuple-element.37), channel_id=1, source_target_pairs={{0,28},{1,29},{2,30},{3,31},{4,0},{5,1},{6,2},{7,3},{8,4},{9,5},{1... | collective-permute-start | bytes 798728 | tf_op jit(solution)/shard_map/ppermute | solution.py:377
  17.4 3.5 %collective-permute-start.7 = (f32[136,128]{1,0:T(8,128)S(1)}, f32[136,128]{1,0:T(8,128)S(1)}, u32[]{:S(2)}, u32[]{:S(2)}) collective-permute-start(f32[136,128]{1,0:T(8,128)S(1)} %get-tuple-element.38), channel_id=1, source_target_pairs={{0,3},{1,0},{2,1},{3,2},{4,7},{5,4},{6,5},{7,6},{8,11},{9,8},{10,9... | collective-permute-start | bytes 208904 | tf_op jit(solution)/shard_map/ppermute | solution.py:377
  19.2 4.6 %collective-permute-start.8 = (f32[136,128]{1,0:T(8,128)S(1)}, f32[136,128]{1,0:T(8,128)S(1)}, u32[]{:S(2)}, u32[]{:S(2)}) collective-permute-start(f32[136,128]{1,0:T(8,128)S(1)} %get-tuple-element.39), channel_id=1, source_target_pairs={{0,31},{1,28},{2,29},{3,30},{4,3},{5,0},{6,1},{7,2},{8,7},{9,4},{1... | collective-permute-start | bytes 208904 | tf_op jit(solution)/shard_map/ppermute | solution.py:377
